TPU v7x, 32 devices: a whole 2x2x4 slice. The times are simulated.
32 devices in a mesh: batch: 8 (over z, y), rows: 4 (over x, core).
Axes of the slice: x: 2, y: 2, z: 4, core: 2. Of those that a mesh axis runs over, the one named last changes fastest.
Arguments:
- features: bfloat16 [72, 16, 14, 1024], P('batch', 'rows'), may hold values from -6 to 6
- w_reduce: bfloat16 [1024, 512], P('rows'), may hold values from -0.1875 to 0.1875
- w_spatial: bfloat16 [3, 3, 512, 512], P(None, None, 'rows'), may hold values from -0.09375 to 0.09375
- w_expand: bfloat16 [512, 2048], P('rows'), may hold values from -0.25 to 0.25
- w_shortcut: bfloat16 [1024, 2048], P('rows'), may hold values from -0.1875 to 0.1875
- w_squeeze: bfloat16 [2048, 512], P('rows'), may hold values from -0.125 to 0.125
- w_mixing: bfloat16 [3, 3, 512, 512], P(None, None, 'rows'), may hold values from -0.09375 to 0.09375
- w_widen: bfloat16 [512, 2048], P('rows'), may hold values from -0.25 to 0.25
- norm_reduce: float32 [2, 3, 512], replicated, as said below
- norm_spatial: float32 [2, 3, 512], replicated, as said below
- norm_expand: float32 [2, 3, 2048], replicated, as said below
- norm_shortcut: float32 [2, 3, 2048], replicated, as said below
- norm_squeeze: float32 [2, 3, 512], replicated, as said below
- norm_mixing: float32 [2, 3, 512], replicated, as said below
- norm_widen: float32 [2, 3, 2048], replicated, as said below
- cotangent: bfloat16 [72, 8, 7, 2048], P('batch', 'rows'), may hold values from -6 to 6
- resolution: int32 [72], replicated, may hold values from 0 to 2, as said below
- active: int32 [3], replicated, may hold values from 256 to 512, as said below
Outputs:
- mixed: bfloat16 [72, 8, 7, 2048], P('batch')
- grad_input: float32 [72, 16, 14, 1024], P('batch', 'rows')
- gw_reduce: float32 [1024, 512], P('batch')
- gw_spatial: float32 [3, 3, 512, 512], P(None, None, 'batch')
- gw_expand: float32 [512, 2048], P('batch')
- gw_shortcut: float32 [1024, 2048], P('batch')
- gw_squeeze: float32 [2048, 512], P('batch')
- gw_mixing: float32 [3, 3, 512, 512], P(None, None, 'batch')
- gw_widen: float32 [512, 2048], P('batch')
- gn_reduce: float32 [2, 3, 512], replicated
- gn_spatial: float32 [2, 3, 512], replicated
- gn_expand: float32 [2, 3, 2048], replicated
- gn_shortcut: float32 [2, 3, 2048], replicated
- gn_squeeze: float32 [2, 3, 512], replicated
- gn_mixing: float32 [2, 3, 512], replicated
- gn_widen: float32 [2, 3, 2048], replicated
Inputs may be any that keep to these rules, and one draw needn't show every extreme that they name: `resolution`: each of 0, 1, 2 (inputs of 160, 192, 224 pixels) names exactly 24 images. `active`: a multiple of 64; one group uses all 512. `norm_reduce`: row 0 gains between 0.5 and 1.5, row 1 biases between -0.8 and 0.8. `norm_spatial`: as norm_reduce. `norm_expand`: as norm_reduce. `norm_shortcut`: as norm_reduce. `norm_squeeze`: as norm_reduce. `norm_mixing`: as norm_reduce. `norm_widen`: as norm_reduce.
All inputs are finite; a program needn't handle non-finite values.
Results may differ from a plain program's by a relative error of at most 0.02.
Values may be sent and summed in bfloat16 or wider, within the bound.
A program may use at most 192 MiB of HBM per device.

v0:
```python
import jax
import jax.numpy as jnp
from jax import lax
from jax.sharding import PartitionSpec as P

eps = 1e-05
highest = lax.Precision.HIGHEST


def from_behind(x, axis, by):
    devices = lax.axis_size(axis)
    pairs = [(i, i + by) for i in range(devices) if 0 <= i + by < devices]
    return lax.ppermute(x, axis, pairs)


def padded_2(cells, sides, width):
    for axis, dim in sides:
        count = lax.axis_size(axis)
        ends = count - 1
        head = lax.slice_in_dim(cells, 0, width, axis=dim)
        tail = lax.slice_in_dim(cells, cells.shape[dim] - width, cells.shape[dim], axis=dim)
        cells = jnp.concatenate(
            [
                lax.ppermute(tail, axis, [(i, (i + 1) % count) for i in range(ends)]),
                cells,
                lax.ppermute(head, axis, [((i + 1) % count, i) for i in range(ends)]),
            ],
            axis=dim,
        )
    return cells


def silu_slope(values):
    logistic = jax.nn.sigmoid(values)
    return logistic * (1.0 + values * (1.0 - logistic))


def split_columns(joined, spans):
    pieces = []
    offset = 0
    for span_width in spans:
        pieces.append(joined[..., offset : offset + span_width])
        offset = offset + span_width
    return pieces


def global_sums(pieces):
    joined = jnp.concatenate(pieces, axis=-1)
    summed = lax.psum(joined, ("batch", "rows"))
    return split_columns(summed, [piece.shape[-1] for piece in pieces])


def global_grads(pieces):
    joined = jnp.concatenate(pieces, axis=-1)
    summed = lax.psum(joined, ("batch", "rows"))
    return split_columns(summed, [piece.shape[-1] for piece in pieces])


def group_sums(first, second, onehot):
    return jnp.stack(
        [jnp.dot(onehot.T, first, precision=highest), jnp.dot(onehot.T, second, precision=highest)]
    )


def forward_sums(pre, pixels, onehot):
    masked = pre * pixels[..., None]
    return group_sums(jnp.sum(masked, axis=(1, 2)), jnp.sum(masked * pre, axis=(1, 2)), onehot)


def backward_sums(grad_norm, normed, pixels, onehot):
    masked = grad_norm * pixels[..., None]
    return group_sums(jnp.sum(masked * normed, axis=(1, 2)), jnp.sum(masked, axis=(1, 2)), onehot)


def norm_setup(sums, params, counts, onehot):
    mean_grp = sums[0] / counts[:, None]
    var_grp = sums[1] / counts[:, None] - mean_grp * mean_grp
    inverse = lax.rsqrt(var_grp + eps)
    return (
        jnp.dot(onehot, mean_grp, precision=highest),
        jnp.dot(onehot, inverse, precision=highest),
        jnp.dot(onehot, params[0], precision=highest),
        jnp.dot(onehot, params[1], precision=highest),
    )


def expand_img(values):
    return values[:, None, None, :]


def norm_apply(pre, setup):
    normed = (pre - expand_img(setup[0])) * expand_img(setup[1])
    return (normed, normed * expand_img(setup[2]) + expand_img(setup[3]))


def norm_backward(grad_norm, normed, sums, setup, counts, pixels, onehot):
    scaled = sums / counts[None, :, None]
    gain_part = expand_img(jnp.dot(onehot, scaled[0], precision=highest))
    bias_part = expand_img(jnp.dot(onehot, scaled[1], precision=highest))
    factor = expand_img(setup[1] * setup[2])
    return (factor * (grad_norm - bias_part - normed * gain_part) * pixels[..., None]).astype(
        jnp.bfloat16
    )


def frame_part(sides, first_row, row_count, col_count):
    row_ids = first_row + jnp.arange(row_count, dtype=jnp.int32)
    col_ids = jnp.arange(col_count, dtype=jnp.int32)
    inside = (row_ids[None, :, None] < sides[:, None, None]) & (
        col_ids[None, None, :] < sides[:, None, None]
    )
    return inside.astype(jnp.float32)


def channel_mask(active_img, factor, channels):
    return (jnp.arange(channels, dtype=jnp.int32)[None, :] < active_img[:, None] * factor).astype(
        jnp.float32
    )


def stride_windows(padded, out_rows, out_cols):
    windows = [
        padded[
            :,
            row_step : row_step + 2 * out_rows - 1 : 2,
            col_step : col_step + 2 * out_cols - 1 : 2,
        ]
        for row_step in range(3)
        for col_step in range(3)
    ]
    return jnp.concatenate(windows, axis=-1)


def unit_windows(padded, out_rows, out_cols):
    windows = [
        padded[:, row_step : row_step + out_rows, col_step : col_step + out_cols]
        for row_step in range(3)
        for col_step in range(3)
    ]
    return jnp.concatenate(windows, axis=-1)


def apply_kernel(windows, kernel):
    flat = kernel.reshape(-1, kernel.shape[-1])
    return jnp.einsum("irck,kn->ircn", windows, flat, preferred_element_type=jnp.float32)


def kernel_grad(windows, grad_pre, kernel_shape):
    return jnp.einsum(
        "irck,ircn->kn", windows, grad_pre, preferred_element_type=jnp.float32
    ).reshape(kernel_shape)


def project(values, weight):
    return jnp.einsum("irck,kn->ircn", values, weight, preferred_element_type=jnp.float32)


def project_back(grads, weight):
    return jnp.einsum("ircn,kn->irck", grads, weight, preferred_element_type=jnp.float32)


def weight_grad(values, grads):
    return jnp.einsum("irck,ircn->kn", values, grads, preferred_element_type=jnp.float32)


def per_device(
    features,
    w_reduce,
    w_spatial,
    w_expand,
    w_shortcut,
    w_squeeze,
    w_mixing,
    w_widen,
    norm_reduce,
    norm_spatial,
    norm_expand,
    norm_shortcut,
    norm_squeeze,
    norm_mixing,
    norm_widen,
    cotangent,
    resolution,
    active,
):
    images, rows_dev, cols_in, channels_in = features.shape
    out_rows = rows_dev // 2
    out_cols = cols_in // 2
    k_reduce, k_spatial, k_expand, k_shortcut, k_squeeze, k_mixing, k_widen = (
        lax.all_gather(w_reduce, "rows", axis=0, tiled=True),
        lax.all_gather(w_spatial, "rows", axis=2, tiled=True),
        lax.all_gather(w_expand, "rows", axis=0, tiled=True),
        lax.all_gather(w_shortcut, "rows", axis=0, tiled=True),
        lax.all_gather(w_squeeze, "rows", axis=0, tiled=True),
        lax.all_gather(w_mixing, "rows", axis=2, tiled=True),
        lax.all_gather(w_widen, "rows", axis=0, tiled=True),
    )
    mid_width = k_reduce.shape[1]
    wide_width = k_expand.shape[1]
    groups = jnp.arange(3, dtype=jnp.int32)
    members = jnp.sum((resolution[:, None] == groups[None, :]).astype(jnp.float32), axis=0)
    sides_grp = 10.0 + 2.0 * groups.astype(jnp.float32)
    count_in = members * sides_grp * sides_grp
    count_out = members * (sides_grp * 0.5) * (sides_grp * 0.5)
    local_res = lax.dynamic_slice_in_dim(resolution, lax.axis_index("batch") * images, images)
    onehot_int = (local_res[:, None] == groups[None, :]).astype(jnp.int32)
    onehot = onehot_int.astype(jnp.float32)
    sides = 10 + 2 * local_res
    row_index = lax.axis_index("rows")
    pixel_in = frame_part(sides, row_index * rows_dev, rows_dev, cols_in)
    pixel_out = frame_part(sides // 2, row_index * out_rows, out_rows, out_cols)
    active_img = jnp.sum(onehot_int * active[None, :], axis=1)
    chan_in = channel_mask(active_img, channels_in // mid_width, channels_in)
    chan_mid = channel_mask(active_img, 1, mid_width)
    chan_wide = channel_mask(active_img, wide_width // mid_width, wide_width)
    mask_in = pixel_in[..., None] * chan_in[:, None, None, :]
    mask_mid_in = pixel_in[..., None] * chan_mid[:, None, None, :]
    mask_mid_out = pixel_out[..., None] * chan_mid[:, None, None, :]
    mask_wide_out = pixel_out[..., None] * chan_wide[:, None, None, :]
    masked_input = features * mask_in.astype(jnp.bfloat16)
    even_input = masked_input[:, ::2, ::2]
    pre_one = project(masked_input, k_reduce)
    sums_one = global_sums([forward_sums(pre_one, pixel_in, onehot)])[0]
    setup_one = norm_setup(sums_one, norm_reduce, count_in, onehot)
    normed_one, lifted_one = norm_apply(pre_one, setup_one)
    act_one = (jax.nn.silu(lifted_one) * mask_mid_in).astype(jnp.bfloat16)
    rim_rows = from_behind(act_one[:, rows_dev - 1 :], "rows", 1)
    padded_one = jnp.pad(
        jnp.concatenate([rim_rows, act_one], axis=1), ((0, 0), (0, 0), (1, 0), (0, 0))
    )
    windows_one = stride_windows(padded_one, out_rows, out_cols)
    pre_two = apply_kernel(windows_one, k_spatial)
    sums_two = global_sums([forward_sums(pre_two, pixel_out, onehot)])[0]
    setup_two = norm_setup(sums_two, norm_spatial, count_out, onehot)
    normed_two, lifted_two = norm_apply(pre_two, setup_two)
    act_two = (jax.nn.silu(lifted_two) * mask_mid_out).astype(jnp.bfloat16)
    pre_three = project(act_two, k_expand)
    pre_short = project(even_input, k_shortcut)
    sums_three, sums_short = global_sums(
        [forward_sums(pre_three, pixel_out, onehot), forward_sums(pre_short, pixel_out, onehot)]
    )
    setup_three = norm_setup(sums_three, norm_expand, count_out, onehot)
    setup_short = norm_setup(sums_short, norm_shortcut, count_out, onehot)
    normed_three, lifted_three = norm_apply(pre_three, setup_three)
    normed_short, lifted_short = norm_apply(pre_short, setup_short)
    block_pre = lifted_three + lifted_short
    block_one = (jax.nn.silu(block_pre) * mask_wide_out).astype(jnp.bfloat16)
    pre_four = project(block_one, k_squeeze)
    sums_four = global_sums([forward_sums(pre_four, pixel_out, onehot)])[0]
    setup_four = norm_setup(sums_four, norm_squeeze, count_out, onehot)
    normed_four, lifted_four = norm_apply(pre_four, setup_four)
    act_four = (jax.nn.silu(lifted_four) * mask_mid_out).astype(jnp.bfloat16)
    padded_four = jnp.pad(padded_2(act_four, (("rows", 1),), 1), ((0, 0), (0, 0), (1, 1), (0, 0)))
    windows_four = unit_windows(padded_four, out_rows, out_cols)
    pre_five = apply_kernel(windows_four, k_mixing)
    sums_five = global_sums([forward_sums(pre_five, pixel_out, onehot)])[0]
    setup_five = norm_setup(sums_five, norm_mixing, count_out, onehot)
    normed_five, lifted_five = norm_apply(pre_five, setup_five)
    act_five = (jax.nn.silu(lifted_five) * mask_mid_out).astype(jnp.bfloat16)
    pre_six = project(act_five, k_widen)
    sums_six = global_sums([forward_sums(pre_six, pixel_out, onehot)])[0]
    setup_six = norm_setup(sums_six, norm_widen, count_out, onehot)
    normed_six, lifted_six = norm_apply(pre_six, setup_six)
    final_pre = lifted_six + block_one.astype(jnp.float32)
    local_out = (jax.nn.silu(final_pre) * mask_wide_out).astype(jnp.bfloat16)
    mixed = lax.all_gather(local_out, "rows", axis=1, tiled=True)
    grad_final = cotangent.astype(jnp.float32) * mask_wide_out * silu_slope(final_pre)
    back_six = global_grads([backward_sums(grad_final, normed_six, pixel_out, onehot)])[0]
    grad_six = norm_backward(
        grad_final, normed_six, back_six, setup_six, count_out, pixel_out, onehot
    )
    gw_widen = weight_grad(act_five, grad_six)
    grad_lift_five = project_back(grad_six, k_widen) * mask_mid_out * silu_slope(lifted_five)
    back_five = global_grads([backward_sums(grad_lift_five, normed_five, pixel_out, onehot)])[0]
    grad_five = norm_backward(
        grad_lift_five, normed_five, back_five, setup_five, count_out, pixel_out, onehot
    )
    gw_mixing = kernel_grad(windows_four, grad_five, k_mixing.shape)
    halo_five = jnp.pad(padded_2(grad_five, (("rows", 1),), 1), ((0, 0), (0, 0), (1, 1), (0, 0)))
    flipped = jnp.transpose(k_mixing[::-1, ::-1], (0, 1, 3, 2))
    grad_act_four = apply_kernel(unit_windows(halo_five, out_rows, out_cols), flipped)
    grad_lift_four = grad_act_four * mask_mid_out * silu_slope(lifted_four)
    back_four = global_grads([backward_sums(grad_lift_four, normed_four, pixel_out, onehot)])[0]
    grad_four = norm_backward(
        grad_lift_four, normed_four, back_four, setup_four, count_out, pixel_out, onehot
    )
    gw_squeeze = weight_grad(block_one, grad_four)
    grad_block = grad_final + project_back(grad_four, k_squeeze)
    grad_block_pre = grad_block * mask_wide_out * silu_slope(block_pre)
    back_three, back_short = global_grads(
        [
            backward_sums(grad_block_pre, normed_three, pixel_out, onehot),
            backward_sums(grad_block_pre, normed_short, pixel_out, onehot),
        ]
    )
    grad_three = norm_backward(
        grad_block_pre, normed_three, back_three, setup_three, count_out, pixel_out, onehot
    )
    grad_short = norm_backward(
        grad_block_pre, normed_short, back_short, setup_short, count_out, pixel_out, onehot
    )
    gw_expand = weight_grad(act_two, grad_three)
    gw_shortcut = weight_grad(even_input, grad_short)
    grad_lift_two = project_back(grad_three, k_expand) * mask_mid_out * silu_slope(lifted_two)
    back_two = global_grads([backward_sums(grad_lift_two, normed_two, pixel_out, onehot)])[0]
    grad_two = norm_backward(
        grad_lift_two, normed_two, back_two, setup_two, count_out, pixel_out, onehot
    )
    gw_spatial = kernel_grad(windows_one, grad_two, k_spatial.shape)
    next_rows = from_behind(grad_two[:, 0:1], "rows", -1)
    extended = jnp.concatenate([grad_two, next_rows], axis=1)
    spread = jnp.einsum(
        "ircn,kn->irck",
        extended,
        k_spatial.reshape(-1, mid_width),
        preferred_element_type=jnp.float32,
    )
    placed = []
    for row_step in range(3):
        for col_step in range(3):
            window_index = 3 * row_step + col_step
            piece = spread[..., window_index * mid_width : (window_index + 1) * mid_width]
            placed.append(
                lax.pad(
                    piece,
                    jnp.float32(0.0),
                    (
                        (0, 0, 0),
                        (row_step, 2 - row_step, 1),
                        (col_step, 2 - col_step, 1),
                        (0, 0, 0),
                    ),
                )
            )
    gathered_back = functools_sum(placed)
    grad_act_one = gathered_back[:, 1 : 1 + rows_dev, 1 : 1 + cols_in]
    grad_lift_one = grad_act_one * mask_mid_in * silu_slope(lifted_one)
    back_one = global_grads([backward_sums(grad_lift_one, normed_one, pixel_in, onehot)])[0]
    grad_one = norm_backward(
        grad_lift_one, normed_one, back_one, setup_one, count_in, pixel_in, onehot
    )
    gw_reduce = weight_grad(masked_input, grad_one)
    short_back = lax.pad(
        project_back(grad_short, k_shortcut),
        jnp.float32(0.0),
        (
            (0, 0, 0),
            (0, rows_dev - 2 * out_rows + 1, 1),
            (0, cols_in - 2 * out_cols + 1, 1),
            (0, 0, 0),
        ),
    )
    grad_input = (project_back(grad_one, k_reduce) + short_back) * mask_in
    shared = (
        lax.psum_scatter(gw_reduce, "batch", scatter_dimension=0, tiled=True),
        lax.psum_scatter(gw_spatial, "batch", scatter_dimension=2, tiled=True),
        lax.psum_scatter(gw_expand, "batch", scatter_dimension=0, tiled=True),
        lax.psum_scatter(gw_shortcut, "batch", scatter_dimension=0, tiled=True),
        lax.psum_scatter(gw_squeeze, "batch", scatter_dimension=0, tiled=True),
        lax.psum_scatter(gw_mixing, "batch", scatter_dimension=2, tiled=True),
        lax.psum_scatter(gw_widen, "batch", scatter_dimension=0, tiled=True),
    )
    totals = (
        lax.psum(shared[0].astype(jnp.bfloat16), "rows").astype(jnp.float32),
        lax.psum(shared[1].astype(jnp.bfloat16), "rows").astype(jnp.float32),
        lax.psum(shared[2].astype(jnp.bfloat16), "rows").astype(jnp.float32),
        lax.psum(shared[3].astype(jnp.bfloat16), "rows").astype(jnp.float32),
        lax.psum(shared[4].astype(jnp.bfloat16), "rows").astype(jnp.float32),
        lax.psum(shared[5].astype(jnp.bfloat16), "rows").astype(jnp.float32),
        lax.psum(shared[6].astype(jnp.bfloat16), "rows").astype(jnp.float32),
    )
    return (
        mixed,
        grad_input,
        totals[0],
        totals[1],
        totals[2],
        totals[3],
        totals[4],
        totals[5],
        totals[6],
        back_one,
        back_two,
        back_three,
        back_short,
        back_four,
        back_five,
        back_six,
    )


def functools_sum(arrays):
    total = arrays[0]
    for extra in arrays[1:]:
        total = total + extra
    return total


def solution(mesh):
    return jax.shard_map(
        per_device,
        mesh=mesh,
        in_specs=(
            P("batch", "rows", None, None),
            P("rows", None),
            P(None, None, "rows", None),
            P("rows", None),
            P("rows", None),
            P("rows", None),
            P(None, None, "rows", None),
            P("rows", None),
            P(),
            P(),
            P(),
            P(),
            P(),
            P(),
            P(),
            P("batch", "rows", None, None),
            P(),
            P(),
        ),
        out_specs=(
            P("batch", None, None, None),
            P("batch", "rows", None, None),
            P("batch", None),
            P(None, None, "batch", None),
            P("batch", None),
            P("batch", None),
            P("batch", None),
            P(None, None, "batch", None),
            P("batch", None),
            P(),
            P(),
            P(),
            P(),
            P(),
            P(),
            P(),
        ),
        check_vma=False,
    )
```

profile of v0, /device:TPU:0, one launch (start us, length us, event | category | flops | bytes accessed | tf_op | source)
XLA Modules:
  0.0 1902.9 jit_solution(2650319542309106919)
XLA Ops:
  31.5 39.6 %psum.133 = f32[2,3,512]{2,1,0:T(4,128)S(1)} all-reduce(f32[2,3,512]{2,1,0:T(4,128)S(1)} %pad_maximum_fusion.6), channel_id=1, replica_groups=mesh['batch'=8,'rows'=4] {'batch','rows'}, use_global_device_ids=true, to_apply=%region_3.4 | all-reduce | flops 3072 | bytes 24576 | tf_op jit(solution)/shard_map/psum | solution.py:49
  109.9 41.2 %psum.134 = f32[2,3,512]{2,1,0:T(4,128)S(1)} all-reduce(f32[2,3,512]{2,1,0:T(4,128)S(1)} %pad_maximum_fusion.7), channel_id=1, replica_groups=mesh['batch'=8,'rows'=4] {'batch','rows'}, use_global_device_ids=true, to_apply=%region_7.8 | all-reduce | flops 3072 | bytes 24576 | tf_op jit(solution)/shard_map/psum | solution.py:49
  175.7 104.6 %all-reduce.18.cloned.1.call-done = f32[2,3,4096]{2,1,0:T(4,128)} async-done(((f32[2,3,4096]{2,1,0:T(4,128)}), f32[2,3,4096]{2,1,0:T(4,128)}) %all-reduce.18.cloned.1.call-update) | async-done | bytes 98320 | tf_op jit(solution)/shard_map/psum | solution.py:49
  289.0 14.4 all-gather.17.cloned.1.call-done
  306.3 39.8 %psum.136 = f32[2,3,512]{2,1,0:T(4,128)S(1)} all-reduce(f32[2,3,512]{2,1,0:T(4,128)S(1)} %pad_maximum_fusion.8), channel_id=1, replica_groups=mesh['batch'=8,'rows'=4] {'batch','rows'}, use_global_device_ids=true, to_apply=%region_15.16 | all-reduce | flops 3072 | bytes 24576 | tf_op jit(solution)/shard_map/psum | solution.py:49
  362.5 44.0 %psum.137 = f32[2,3,512]{2,1,0:T(4,128)S(1)} all-reduce(f32[2,3,512]{2,1,0:T(4,128)S(1)} %pad_maximum_fusion.9), channel_id=1, replica_groups=mesh['batch'=8,'rows'=4] {'batch','rows'}, use_global_device_ids=true, to_apply=%region_18.19 | all-reduce | flops 3072 | bytes 24576 | tf_op jit(solution)/shard_map/psum | solution.py:49
  411.9 39.9 %psum.138 = f32[2,3,2048]{2,1,0:T(4,128)S(1)} all-reduce(f32[2,3,2048]{2,1,0:T(4,128)S(1)} %pad_maximum_fusion.4), channel_id=1, replica_groups=mesh['batch'=8,'rows'=4] {'batch','rows'}, use_global_device_ids=true, to_apply=%region_21.22 | all-reduce | flops 12288 | bytes 98304 | tf_op jit(solution)/shard_map/psum | solution.py:49
  458.0 41.7 %psum.139 = f32[2,3,2048]{2,1,0:T(4,128)} all-reduce(f32[2,3,2048]{2,1,0:T(4,128)} %pad_maximum_fusion.5), channel_id=1, replica_groups=mesh['batch'=8,'rows'=4] {'batch','rows'}, use_global_device_ids=true, to_apply=%region_24.25 | all-reduce | flops 12288 | bytes 98304 | tf_op jit(solution)/shard_map/psum | solution.py:55
  505.8 39.2 %psum.140 = f32[2,3,512]{2,1,0:T(4,128)S(1)} all-reduce(f32[2,3,512]{2,1,0:T(4,128)S(1)} %pad_maximum_fusion.10), channel_id=1, replica_groups=mesh['batch'=8,'rows'=4] {'batch','rows'}, use_global_device_ids=true, to_apply=%region_27.28 | all-reduce | flops 3072 | bytes 24576 | tf_op jit(solution)/shard_map/psum | solution.py:55
  562.7 44.4 %psum.141 = f32[2,3,512]{2,1,0:T(4,128)S(1)} all-reduce(f32[2,3,512]{2,1,0:T(4,128)} %pad_maximum_fusion.11), channel_id=1, replica_groups=mesh['batch'=8,'rows'=4] {'batch','rows'}, use_global_device_ids=true, to_apply=%region_30.31 | all-reduce | flops 3072 | bytes 24576 | tf_op jit(solution)/shard_map/psum | solution.py:55
  616.4 122.2 %all-reduce.20.cloned.1.call-done = f32[2,3,4096]{2,1,0:T(4,128)} async-done(((f32[2,3,4096]{2,1,0:T(4,128)}), f32[2,3,4096]{2,1,0:T(4,128)}) %all-reduce.20.cloned.1.call-update) | async-done | bytes 98320 | tf_op jit(solution)/shard_map/psum | solution.py:55
  746.8 39.3 %psum.143 = f32[2,3,512]{2,1,0:T(4,128)S(1)} all-reduce(f32[2,3,512]{2,1,0:T(4,128)S(1)} %pad_maximum_fusion.12), channel_id=1, replica_groups=mesh['batch'=8,'rows'=4] {'batch','rows'}, use_global_device_ids=true, to_apply=%region_37.38 | all-reduce | flops 3072 | bytes 24576 | tf_op jit(solution)/shard_map/psum | solution.py:55
  806.5 14.0 pad.45
  820.5 14.0 pad.46
  834.6 14.0 pad.182
  926.5 41.1 %psum.144 = f32[2,3,512]{2,1,0:T(4,128)S(1)} all-reduce(f32[2,3,512]{2,1,0:T(4,128)S(1)} %pad_maximum_fusion.13), channel_id=1, replica_groups=mesh['batch'=8,'rows'=4] {'batch','rows'}, use_global_device_ids=true, to_apply=%region_40.41 | all-reduce | flops 3072 | bytes 24576 | tf_op jit(solution)/shard_map/psum | solution.py:55
  1004.9 34.8 %reduce-scatter.8.cloned.1.call-done = f32[128,512]{1,0:T(8,128)} async-done(((f32[1024,512]{1,0:T(8,128)}), f32[128,512]{1,0:T(8,128)}) %reduce-scatter.8.cloned.1.call-update) | async-done | bytes 262160 | tf_op jit(solution)/shard_map/reduce_scatter | solution.py:355
  1041.3 88.9 %reduce-scatter.20.cloned.1.call-done = f32[64,2048]{1,0:T(8,128)} async-done(((f32[512,2048]{1,0:T(8,128)}), f32[64,2048]{1,0:T(8,128)}) %reduce-scatter.20.cloned.1.call-update) | async-done | bytes 524304 | tf_op jit(solution)/shard_map/reduce_scatter | solution.py:361
  1132.0 89.8 %reduce-scatter.16.cloned.1.call-done = f32[256,512]{1,0:T(8,128)} async-done(((f32[2048,512]{1,0:T(8,128)}), f32[256,512]{1,0:T(8,128)}) %reduce-scatter.16.cloned.1.call-update) | async-done | bytes 524304 | tf_op jit(solution)/shard_map/reduce_scatter | solution.py:359
  1223.6 89.6 %reduce-scatter.12.cloned.1.call-done = f32[64,2048]{1,0:T(8,128)} async-done(((f32[512,2048]{1,0:T(8,128)}), f32[64,2048]{1,0:T(8,128)}) %reduce-scatter.12.cloned.1.call-update) | async-done | bytes 524304 | tf_op jit(solution)/shard_map/reduce_scatter | solution.py:357
  1314.9 150.9 %reduce-scatter.14.cloned.1.call-done = f32[128,2048]{1,0:T(8,128)} async-done(((f32[1024,2048]{1,0:T(8,128)}), f32[128,2048]{1,0:T(8,128)}) %reduce-scatter.14.cloned.1.call-update) | async-done | bytes 1048592 | tf_op jit(solution)/shard_map/reduce_scatter | solution.py:358
  1467.9 164.1 %reduce-scatter.18.cloned.1.call-done = f32[3,3,64,512]{3,2,1,0:T(8,128)} async-done(((f32[3,3,512,512]{3,2,1,0:T(8,128)}), f32[3,3,64,512]{3,2,1,0:T(8,128)}) %reduce-scatter.18.cloned.1.call-update) | async-done | bytes 1179664 | tf_op jit(solution)/shard_map/reduce_scatter | solution.py:360
  1634.1 164.1 %reduce-scatter.10.cloned.1.call-done = f32[3,3,64,512]{3,2,1,0:T(8,128)} async-done(((f32[3,3,512,512]{3,2,1,0:T(8,128)}), f32[3,3,64,512]{3,2,1,0:T(8,128)}) %reduce-scatter.10.cloned.1.call-update) | async-done | bytes 1179664 | tf_op jit(solution)/shard_map/reduce_scatter | solution.py:356
  1827.3 60.5 %all-reduce.22.cloned.1.call-done = (bf16[128,512]{1,0:T(8,128)(2,1)}, bf16[3,3,64,512]{3,2,1,0:T(8,128)(2,1)}, bf16[64,2048]{1,0:T(8,128)(2,1)}, bf16[128,2048]...) async-done(((bf16[128,512]{1,0:T(8,128)(2,1)}, bf16[3,3,64,512]{3,2,1,0:T(8,128)(2,1)}, ...) | async-done | bytes 2621456 | tf_op jit(solution)/shard_map/psum | solution.py:364
  (548 shorter events, 350.1 us)
Async XLA Ops:
  7.2 21.8 %all-gather.9.cloned.1.call-start = ((), (), s32[]{:S(2)}) async-start(), calls=%async_computation.7 | async-start | bytes 1310720 | tf_op jit(solution)/shard_map/all_gather | solution.py:190
  7.9 79.4 %all-gather.15.cloned.1.call-start = ((), (), s32[]{:S(2)}) async-start(), calls=%async_computation.10 | async-start | bytes 5242880 | tf_op jit(solution)/shard_map/all_gather | solution.py:193
  8.7 95.7 %all-gather.11.cloned.1.call-start = ((), (), s32[]{:S(2)}) async-start(), calls=%async_computation.8 | async-start | bytes 5898240 | tf_op jit(solution)/shard_map/all_gather | solution.py:191
  9.5 143.4 %all-gather.13.cloned.1.call-start = ((), (), s32[]{:S(2)}) async-start(), calls=%async_computation.9 | async-start | bytes 2621440 | tf_op jit(solution)/shard_map/all_gather | solution.py:192
  10.0 270.3 %all-reduce.18.cloned.1.call-start = ((), (), s32[]{:S(2)}) async-start(), calls=%async_computation.11 | async-start | bytes 262144 | tf_op jit(solution)/shard_map/psum | solution.py:49
  72.9 2.3 collective-permute-start
  157.8 145.6 %all-gather.17.cloned.1.call-start = ((), (), s32[]{:S(2)}) async-start(), calls=%async_computation.12 | async-start | bytes 2621440 | tf_op jit(solution)/shard_map/all_gather | solution.py:194
  158.4 191.9 %all-gather.19.cloned.1.call-start = ((), (), s32[]{:S(2)}) async-start(), calls=%async_computation.13 | async-start | bytes 5898240 | tf_op jit(solution)/shard_map/all_gather | solution.py:195
  160.8 246.8 %all-gather.21.cloned.1.call-start = ((), (), s32[]{:S(2)}) async-start(), calls=%async_computation.14 | async-start | bytes 2621440 | tf_op jit(solution)/shard_map/all_gather | solution.py:196
  161.6 577.0 %all-reduce.20.cloned.1.call-start = ((), (), s32[]{:S(2)}) async-start(), calls=%async_computation.16 | async-start | bytes 262144 | tf_op jit(solution)/shard_map/psum | solution.py:55
  347.4 9.6 collective-permute-start.1
  348.7 8.3 collective-permute-start.2
  547.4 7.5 collective-permute-start.3
  548.7 6.2 collective-permute-start.4
  616.3 423.3 %reduce-scatter.8.cloned.1.call-start = ((), (), s32[]{:S(2)}) async-start(), calls=%async_computation.17 | async-start | bytes 2359296 | tf_op jit(solution)/shard_map/reduce_scatter | solution.py:355
  786.9 3.2 collective-permute-start.5
  972.0 158.2 %reduce-scatter.20.cloned.1.call-start = ((), (), s32[]{:S(2)}) async-start(), calls=%async_computation.23 | async-start | bytes 4718592 | tf_op jit(solution)/shard_map/reduce_scatter | solution.py:361
  976.0 245.8 %reduce-scatter.16.cloned.1.call-start = ((), (), s32[]{:S(2)}) async-start(), calls=%async_computation.21 | async-start | bytes 4718592 | tf_op jit(solution)/shard_map/reduce_scatter | solution.py:359
  980.0 333.1 %reduce-scatter.12.cloned.1.call-start = ((), (), s32[]{:S(2)}) async-start(), calls=%async_computation.19 | async-start | bytes 4718592 | tf_op jit(solution)/shard_map/reduce_scatter | solution.py:357
  984.0 481.8 %reduce-scatter.14.cloned.1.call-start = ((), (), s32[]{:S(2)}) async-start(), calls=%async_computation.20 | async-start | bytes 9437184 | tf_op jit(solution)/shard_map/reduce_scatter | solution.py:358
  989.9 642.1 %reduce-scatter.18.cloned.1.call-start = ((), (), s32[]{:S(2)}) async-start(), calls=%async_computation.22 | async-start | bytes 10616832 | tf_op jit(solution)/shard_map/reduce_scatter | solution.py:360
  996.5 801.7 %reduce-scatter.10.cloned.1.call-start = ((), (), s32[]{:S(2)}) async-start(), calls=%async_computation.18 | async-start | bytes 10616832 | tf_op jit(solution)/shard_map/reduce_scatter | solution.py:356
  1004.2 818.6 %all-gather.23.cloned.1.call-start = ((), (), s32[]{:S(2)}) async-start(), calls=%async_computation.15 | async-start | bytes 2949120 | tf_op jit(solution)/shard_map/all_gather | solution.py:266
  1004.8 883.0 %all-reduce.22.cloned.1.call-start = ((), (), s32[]{:S(2)}) async-start(), calls=%async_computation.24 | async-start | bytes 5242880 | tf_op jit(solution)/shard_map/psum | solution.py:364
  (135 other events, 2381.9 us)
Sparse Core Ops, SparseCore 0:
  9.6 19.4 all-gather.8
  30.6 34.7 all-gather.14
  67.0 37.4 all-gather.10
  105.9 24.8 all-gather.12
  157.9 122.3 all-reduce.17
  281.7 21.6 all-gather.16
  305.5 38.5 all-gather.18
  345.6 23.4 all-gather.20
  616.5 122.1 all-reduce.19
  972.1 67.4 reduce-scatter.7
  1043.3 86.8 reduce-scatter.19
  1134.1 87.6 reduce-scatter.15
  1225.4 87.6 reduce-scatter.11
  1317.0 148.7 reduce-scatter.13
  1469.3 162.6 reduce-scatter.17
  1635.5 162.7 reduce-scatter.9
  1799.7 23.1 all-gather.22
  1826.7 61.0 all-reduce.21
where the time goes:
time: 1920 us; the launch traced here: 1900 us
  waiting for transfers between devices  1120 us (58%)
  blocking collectives  410 us (21%)
  local copies, waits for them, and re-layouts  184 us (10%)
  matrix products  109 us (6%)
  other arithmetic  54.8 us (3%)
    psum x5, blocking collectives, global_grads(): summed = lax.psum(joined, ('batch', 'rows'))  206 us
    psum x5, blocking collectives, global_sums(): summed = lax.psum(joined, ('batch', 'rows'))  205 us
    reduce_scatter x1, waiting for transfers between devices, per_device(): lax.psum_scatter(gw_spatial, 'batch', scatter_dimension=2, tiled=True)  164 us
    reduce_scatter x1, waiting for transfers between devices, per_device(): lax.psum_scatter(gw_mixing, 'batch', scatter_dimension=2, tiled=True)  164 us
    reduce_scatter x1, waiting for transfers between devices, per_device(): lax.psum_scatter(gw_shortcut, 'batch', scatter_dimension=0, tiled=True)  151 us
    psum x1, waiting for transfers between devices, global_grads(): summed = lax.psum(joined, ('batch', 'rows'))  122 us
    unnamed x305, local copies, waits for them, and re-layouts  114 us
    psum x1, waiting for transfers between devices, global_sums(): summed = lax.psum(joined, ('batch', 'rows'))  105 us
  transfers between devices with their start and end apart: 24, of which 16 were waited for; matrix products, arithmetic and copies ran while one was open for 8% of the time, Pallas kernels for 0%

commit v1 on v0

v1 whole, which is shorter than its diff:
```python
import functools
from types import SimpleNamespace

import jax
import jax.numpy as jnp
from jax import lax
from jax.experimental import pallas as pl
from jax.experimental.pallas import tpu as pltpu
from jax.sharding import PartitionSpec as P

eps = 1e-05
MESH = pl.DeviceIdType.MESH
BF = jnp.bfloat16
F32 = jnp.float32
LANES = 128


def dot(a, b):
    return jnp.dot(a, b, preferred_element_type=F32)


def dot_t(a, b):
    return lax.dot_general(a, b, (((1,), (1,)), ((), ())), preferred_element_type=F32)


def dot_w(a, b):
    return lax.dot_general(a, b, (((0,), (0,)), ((), ())), preferred_element_type=F32)


def aligned(index, size):
    return pl.ds(pl.multiple_of(index * size, size), size)


def loop(count, body):
    def step(i, carry):
        body(i)
        return carry

    lax.fori_loop(0, count, step, 0)


def silu_parts(u):
    s = jax.nn.sigmoid(u)
    return s, u * s


def slope(u):
    s = jax.nn.sigmoid(u)
    return s * (1.0 + u * (1.0 - s))


def block_kernel(names, cfg, *refs):
    R = SimpleNamespace(**dict(zip(names, refs)))
    S, RD, OD, NB = cfg.slots, cfg.in_rows, cfg.out_rows, cfg.batch
    MID, WIDE, CIN = cfg.mid, cfg.wide, cfg.cin
    M = OD * S
    b = lax.axis_index("batch")
    r = lax.axis_index("rows")
    core = lax.rem(r, 2)
    xb = lax.div(r, 2)
    core_peer = r + 1 - 2 * core
    x_row = lax.rem(r + 2, 4)
    diag = 3 - r
    half = lax.rem(b, 2)
    y_b = b + 1 - 2 * half

    def flip(i, j):
        out = jnp.int32(0)
        bit = 1
        while bit < 2 * NB:
            p, q = lax.rem(lax.div(i, bit), 2), lax.rem(lax.div(j, bit), 2)
            out = out + bit * (p + q - 2 * p * q)
            bit *= 2
        return out

    me = b * 2 + xb

    def remote(src, dst, send, recv, dev):
        return pltpu.make_async_remote_copy(
            src_ref=src, dst_ref=dst, send_sem=send, recv_sem=recv, device_id=dev, device_id_type=MESH
        )

    def team(id2):
        return (lax.div(id2, 2), 2 * lax.rem(id2, 2) + core)

    bar = pltpu.get_barrier_semaphore()
    for dev in ((b, core_peer), (b, diag)):
        pl.semaphore_signal(bar, inc=1, device_id=dev, device_id_type=MESH)

    def greet(j):
        pl.semaphore_signal(bar, inc=1, device_id=team(flip(me, j + 1)), device_id_type=MESH)

    loop(2 * NB - 1, greet)
    pl.semaphore_wait(bar, 2 * NB + 1)

    units = cfg.units
    wsend, wrecv, wloc = R.wsend, R.wrecv, R.wloc

    def wview(u, shard, part, source):
        name, conv, k0, kn = units[u]
        full = getattr(R, "f_" + name)
        if source:
            ref = getattr(R, name)
            if conv:
                if part is None:
                    return ref.at[pl.ds(k0, kn)]
                h = ref.shape[1] // 2
                return ref.at[pl.ds(k0, kn), aligned(part, h)]
            if part is None:
                return ref.at[pl.ds(k0, kn)]
            h = kn // 2
            return ref.at[pl.ds(pl.multiple_of(k0 + part * h, h), h)]
        if conv:
            if part is None:
                return full.at[pl.ds(k0, kn), shard]
            h = full.shape[2] // 2
            return full.at[pl.ds(k0, kn), shard, aligned(part, h)]
        if part is None:
            return full.at[shard, pl.ds(k0, kn)]
        h = kn // 2
        return full.at[shard, pl.ds(pl.multiple_of(k0 + part * h, h), h)]

    def w_copy(u, i):
        if i < 2:
            part = None if i == 0 else half
            dev = (b, core_peer) if i == 0 else (b, x_row)
            src, dst = wview(u, r, part, True), wview(u, r, part, False)
        else:
            src = dst = wview(u, x_row, 1 - half if i == 4 else half, False)
            dev = (y_b, r) if i == 3 else (b, core_peer)
        return remote(src, dst, wsend.at[u, i], wrecv.at[u, i], dev)

    def w_local(u):
        return pltpu.make_async_copy(wview(u, r, None, True), wview(u, r, None, False), wloc.at[u])

    def w_start(u):
        w_copy(u, 1).start()
        w_copy(u, 0).start()
        w_local(u).start()

    def w_second(u):
        w_copy(u, 1).wait_recv()
        w_copy(u, 3).start()
        w_copy(u, 2).start()

    def w_third(u):
        w_copy(u, 3).wait_recv()
        w_copy(u, 4).start()

    def w_ready(u):
        w_local(u).wait()
        for i in (0, 2, 4):
            w_copy(u, i).wait_recv()

    pumped = [0]

    def pump(steps):
        for _ in range(steps):
            n = pumped[0]
            if n >= len(units) + 2:
                return
            if n < len(units):
                w_start(n)
            if 0 <= n - 1 < len(units):
                w_second(n - 1)
            if 0 <= n - 2 < len(units):
                w_third(n - 2)
            pumped[0] = n + 1

    def need(name):
        last = max(u for u in range(len(units)) if units[u][0] == name)
        while pumped[0] < last + 3:
            pump(1)
        for u in range(len(units)):
            if units[u][0] == name:
                w_ready(u)

    def mid_start(k):
        p = k % 2
        swap = remote(R.loc.at[1 - core], R.rc.at[p], R.ms.at[0], R.mr.at[0, p], (b, core_peer))
        swap.start()
        swap.wait_recv()
        R.rq[p, me] = R.loc[core] + R.rc[p]

        def send(j):
            to = team(flip(me, j + 1))
            remote(R.rq.at[p, me], R.rq.at[p, me], R.ms.at[1], R.mr.at[1, p], to).start()

        loop(2 * NB - 1, send)
        swap.wait_send()

    def mid_finish(k, tot):
        p = k % 2
        rest = R.rq.at[p, pl.ds(0, 2 * NB - 1)]
        every = remote(rest, rest, R.ms.at[1], R.mr.at[1, p], (b, x_row))
        every.wait_recv()
        total = R.rq[p, 0]
        for j in range(1, 2 * NB):
            total = total + R.rq[p, j]
        tot[core] = total
        back = remote(tot.at[core], tot.at[core], R.ms.at[2], R.mr.at[2, p], (b, core_peer))
        back.start()
        every.wait_send()
        back.wait()

    def wide_start(k, loc):
        n = loc.shape[1]
        rw, wb = R.rw.at[k, :, pl.ds(0, n)], R.wb.at[k % 2, :, pl.ds(0, n)]
        rw[r] = loc[r]
        for to in (core_peer, x_row, diag):
            remote(loc.at[to], rw.at[r], R.ws.at[k, 0], R.wr.at[k, 0], (b, to)).start()
        three = remote(loc.at[pl.ds(0, 3)], rw.at[pl.ds(0, 3)], R.ws.at[k, 0], R.wr.at[k, 0], (b, core_peer))
        three.wait_recv()
        wb[b] = rw[0] + rw[1] + (rw[2] + rw[3])

        def send(j):
            to = lax.rem(b + j + 1, NB)
            remote(wb.at[b], wb.at[b], R.ws.at[k, 1], R.wr.at[k, 1], (to, r)).start()

        loop(NB - 1, send)
        three.wait_send()

    def wide_finish(k, tot):
        n = tot.shape[1]
        wb = R.wb.at[k % 2, :, pl.ds(0, n)]
        rest = wb.at[pl.ds(0, NB - 1)]
        every = remote(rest, rest, R.ws.at[k, 1], R.wr.at[k, 1], (b, x_row))
        every.wait_recv()
        total = wb[0]
        for j in range(1, NB):
            total = total + wb[j]
        tot[r] = total
        for to in (core_peer, x_row, diag):
            remote(tot.at[r], tot.at[r], R.ws.at[k, 2], R.wr.at[k, 2], (b, to)).start()
        three = remote(tot.at[pl.ds(0, 3)], tot.at[pl.ds(0, 3)], R.ws.at[k, 2], R.wr.at[k, 2], (b, core_peer))
        every.wait_send()
        three.wait()

    def mid_at(ref, j):
        return ref.at[lax.div(j, 2), :, aligned(lax.rem(j, 2), LANES)]

    def wide_at(ref, j):
        return ref.at[lax.div(j, 4), :, aligned(lax.rem(j, 4), LANES)]

    def group_rows(ref, row, values):
        for g in range(3):
            ref[row + g : row + g + 1, :] = jnp.sum(values * R.onehot[g], axis=0, keepdims=True)

    def blank(ref, row, rows):
        ref[row : row + rows, :] = jnp.zeros((rows, LANES), F32)

    def spread(rows3):
        return rows3[0] * R.onehot[0] + rows3[1] * R.onehot[1] + rows3[2] * R.onehot[2]

    def moments(sums, inv_n, row=0):
        means, invs = [], []
        for g in range(3):
            n = R.counts[inv_n + g : inv_n + g + 1, :]
            mean = sums[row + g : row + g + 1, :] * n
            var = sums[row + 3 + g : row + 4 + g, :] * n - mean * mean
            means.append(mean)
            invs.append(lax.rsqrt(var + eps))
        return means, invs

    IN, OUT = 0, 3

    def forward_terms(sums, params, cols, inv_n, row=0):
        means, invs = moments(sums, inv_n, row)
        scales = [invs[g] * params[g : g + 1, cols] for g in range(3)]
        shifts = [params[3 + g : 4 + g, cols] - means[g] * scales[g] for g in range(3)]
        return spread(scales), spread(shifts)

    def xhat_terms(sums, inv_n, row=0):
        means, invs = moments(sums, inv_n, row)
        return spread(invs), spread([-means[g] * invs[g] for g in range(3)])

    def backward_terms(sums, grads, params, cols, inv_n, row=0, g0=0, g1=3):
        means, invs = moments(sums, inv_n, row)
        fs, az, bz = [], [], []
        for g in range(3):
            n = R.counts[inv_n + g : inv_n + g + 1, :]
            f = invs[g] * params[g : g + 1, cols]
            gain = grads[g0 + g : g0 + g + 1, :] * n * invs[g]
            bias = grads[g1 + g : g1 + g + 1, :] * n
            fs.append(f)
            bz.append(f * gain)
            az.append(f * (bias - means[g] * gain))
        return spread(fs), spread(az), spread(bz)

    def keep(mask_ref, cols):
        return spread([mask_ref[g : g + 1, cols] for g in range(3)])

    def out_rows(k):
        return slice(k * S, (k + 1) * S)

    def forward_stats(z, loc_at, row=0):
        def body(j):
            cols = aligned(j, LANES)
            s = jnp.zeros((S, LANES), F32)
            q = jnp.zeros((S, LANES), F32)
            for o in range(OD):
                v = z[out_rows(o), cols]
                m = v * R.pix_out[out_rows(o), :]
                s = s + m
                q = q + m * v
            st = loc_at(j)
            group_rows(st, row, s)
            group_rows(st, row + 3, q)
            blank(st, row + 6, 2)

        loop(z.shape[-1] // LANES, body)

    def rolled(v, by):
        return pltpu.roll(v, by % S, 0)

    def unit_windows(halo, win, rows, flipped):
        def body(j):
            cols = aligned(j, LANES)
            for k in rows:
                v = halo[k, :, cols].astype(F32)
                moved = (rolled(v, 1).astype(BF), v.astype(BF), rolled(v, -1).astype(BF))
                for dr in range(3):
                    o = k - dr
                    if not 0 <= o < OD:
                        continue
                    for dc in range(3):
                        t = (2 - dr) * 3 + 2 - dc if flipped else dr * 3 + dc
                        win[out_rows(o), pl.ds(pl.multiple_of(t * MID + j * LANES, LANES), LANES)] = moved[dc]

        loop(MID // LANES, body)

    def edge_exchange(halo, k):
        up = remote(halo.at[1], halo.at[OD + 1], R.es.at[k, 0], R.er.at[k, 0], (b, jnp.maximum(r - 1, 0)))
        down = remote(halo.at[OD], halo.at[0], R.es.at[k, 1], R.er.at[k, 1], (b, jnp.minimum(r + 1, 3)))

        @pl.when(r > 0)
        def _():
            up.start()

        @pl.when(r < 3)
        def _():
            down.start()

        @pl.when(r == 0)
        def _():
            halo[0] = jnp.zeros(halo.shape[1:], BF)

        @pl.when(r == 3)
        def _():
            halo[OD + 1] = jnp.zeros(halo.shape[1:], BF)

        return up, down

    def edge_wait(pair):
        up, down = pair

        @pl.when(r < 3)
        def _():
            up.wait_recv()
            down.wait_send()

        @pl.when(r > 0)
        def _():
            down.wait_recv()
            up.wait_send()

    pump(3)
    need("w_reduce")

    def z1_rows(k):
        w = R.f_w_reduce[...].reshape(CIN, MID)
        R.z1[k] = dot(R.x0[k], w)

    loop(RD, z1_rows)

    def z1_stats(j):
        cols = aligned(j, LANES)
        s = jnp.zeros((S, LANES), F32)
        q = jnp.zeros((S, LANES), F32)
        for k in range(RD):
            for p in range(2):
                v = R.z1[k, out_rows(p), cols]
                m = v * R.pix_in[k, out_rows(p), :]
                s = s + m
                q = q + m * v
        st = mid_at(R.loc, j)
        group_rows(st, 0, s)
        group_rows(st, 3, q)
        blank(st, 6, 2)

    loop(MID // LANES, z1_stats)
    mid_start(0)
    pump(1)
    mid_finish(0, R.t1)

    last = RD - 1

    def h1_body(j):
        cols = aligned(j, LANES)
        sc, sh = forward_terms(mid_at(R.t1, j), R.norm_reduce, cols, IN)
        ch = keep(R.chan_mid, cols)
        for k in range(RD - 1, -1, -1):
            for p in range(2):
                u = R.z1[k, out_rows(p), cols] * sc + sh
                h = silu_parts(u)[1] * (ch * R.pix_in[k, out_rows(p), :])
                if k == last:
                    R.h1s[p, :, cols] = h.astype(BF)
                for dr in range(3):
                    o2 = k + 1 - dr
                    if o2 % 2 or not 0 <= o2 // 2 < OD:
                        continue
                    o = o2 // 2
                    taps = ((1, h),) if p == 0 else ((0, rolled(h, 1)), (2, h))
                    for dc, v in taps:
                        t = dr * 3 + dc
                        R.win1[out_rows(o), pl.ds(pl.multiple_of(t * MID + j * LANES, LANES), LANES)] = v.astype(BF)

    loop(MID // LANES, h1_body)
    down = remote(R.h1s, R.h1r, R.hs.at[0], R.hr.at[0], (b, jnp.minimum(r + 1, 3)))

    @pl.when(r < 3)
    def _():
        down.start()

    pump(1)

    @pl.when(r > 0)
    def _():
        down.wait_recv()

    @pl.when(r == 0)
    def _():
        R.h1r[...] = jnp.zeros(R.h1r.shape, BF)

    def h1_halo(j):
        cols = aligned(j, LANES)
        even = R.h1r[0, :, cols]
        odd = R.h1r[1, :, cols]
        for dc, v in ((0, rolled(odd.astype(F32), 1).astype(BF)), (1, even), (2, odd)):
            R.win1[out_rows(0), pl.ds(pl.multiple_of(dc * MID + j * LANES, LANES), LANES)] = v

    loop(MID // LANES, h1_halo)

    @pl.when(r < 3)
    def _():
        down.wait_send()

    need("w_spatial")

    def conv(win, weight, z):
        def body(j):
            cols = aligned(j, 256)
            z[:, cols] = dot(win[...], weight[:, :, :, cols].reshape(9 * MID, 256))

        loop(MID // 256, body)

    conv(R.win1, R.f_w_spatial, R.z2)
    forward_stats(R.z2, lambda j: mid_at(R.loc, j))
    mid_start(1)
    pump(1)
    mid_finish(1, R.t2)

    def activate(z, tot, params, dest):
        def body(j):
            cols = aligned(j, LANES)
            sc, sh = forward_terms(mid_at(tot, j), params, cols, OUT)
            ch = keep(R.chan_mid, cols)
            for o in range(OD):
                u = z[out_rows(o), cols] * sc + sh
                dest(o, cols, (silu_parts(u)[1] * (ch * R.pix_out[out_rows(o), :])).astype(BF))

        loop(MID // LANES, body)

    def to_h2(o, cols, v):
        R.h2[out_rows(o), cols] = v

    activate(R.z2, R.t2, R.norm_spatial, to_h2)
    need("w_expand")

    def expand_to(h, weight, z):
        def body(j):
            cols = aligned(j, 512)
            z[:, cols] = dot(h[...], weight[:, :, cols].reshape(-1, 512))

        loop(WIDE // 512, body)

    expand_to(R.h2, R.f_w_expand, R.z3)
    need("w_shortcut")

    def zs_body(j):
        cols = aligned(j, 512)
        w = R.f_w_shortcut[:, :, cols].reshape(CIN, 512)
        for o in range(OD):
            R.zs[out_rows(o), cols] = dot(R.x0[2 * o, 0:S, :], w)

    loop(WIDE // 512, zs_body)
    forward_stats(R.z3, lambda j: wide_at(R.locw2, j), 0)
    forward_stats(R.zs, lambda j: wide_at(R.locw2, j), 8)
    wide_start(0, R.locw2)
    pump(2)
    wide_finish(0, R.t3)

    def u1_terms(j):
        cols = aligned(j, LANES)
        tot = wide_at(R.t3, j)
        sc3, sh3 = forward_terms(tot, R.norm_expand, cols, OUT, 0)
        scs, shs = forward_terms(tot, R.norm_shortcut, cols, OUT, 8)
        shift = sh3 + shs

        def u1(o):
            return R.z3[out_rows(o), cols] * sc3 + R.zs[out_rows(o), cols] * scs + shift

        return u1

    def y1_body(j):
        cols = aligned(j, LANES)
        u1 = u1_terms(j)
        ch = keep(R.chan_wide, cols)
        for o in range(OD):
            y = silu_parts(u1(o))[1] * (ch * R.pix_out[out_rows(o), :])
            R.y1[out_rows(o), cols] = y.astype(BF)

    loop(WIDE // LANES, y1_body)
    need("w_squeeze")

    def squeeze_body(j):
        cols = aligned(j, 256)
        R.z4[:, cols] = dot(R.y1[...], R.f_w_squeeze[:, :, cols].reshape(WIDE, 256))

    loop(MID // 256, squeeze_body)
    forward_stats(R.z4, lambda j: mid_at(R.loc, j))
    mid_start(2)
    pump(2)
    mid_finish(2, R.t4)

    def to_h4(o, cols, v):
        R.h4[o + 1, :, cols] = v

    activate(R.z4, R.t4, R.norm_squeeze, to_h4)
    pair = edge_exchange(R.h4, 0)
    pump(1)
    unit_windows(R.h4, R.win4, range(1, OD + 1), False)
    edge_wait(pair)
    unit_windows(R.h4, R.win4, (0, OD + 1), False)
    need("w_mixing")
    conv(R.win4, R.f_w_mixing, R.z5)
    forward_stats(R.z5, lambda j: mid_at(R.loc, j))
    mid_start(3)
    pump(20)
    mid_finish(3, R.t5)

    def to_h5(o, cols, v):
        R.h5[out_rows(o), cols] = v

    activate(R.z5, R.t5, R.norm_mixing, to_h5)
    need("w_widen")
    expand_to(R.h5, R.f_w_widen, R.z6)
    forward_stats(R.z6, lambda j: wide_at(R.locw, j))
    wide_start(1, R.locw)
    wide_finish(1, R.t6)

    def u2_body(j):
        cols = aligned(j, LANES)
        tot = wide_at(R.t6, j)
        sc, sh = forward_terms(tot, R.norm_widen, cols, OUT)
        xa, xs = xhat_terms(tot, OUT)
        ch = keep(R.chan_wide, cols)
        g0 = jnp.zeros((S, LANES), F32)
        g1 = jnp.zeros((S, LANES), F32)
        for o in range(OD):
            z = R.z6[out_rows(o), cols]
            u = z * sc + sh + R.y1[out_rows(o), cols].astype(F32)
            mask = ch * R.pix_out[out_rows(o), :]
            s, su = silu_parts(u)
            R.mixed_local[o, :, cols] = (su * mask).astype(BF)
            d = R.cotangent[out_rows(o), cols].astype(F32) * mask * (s * (1.0 + u * (1.0 - s)))
            R.du2[out_rows(o), cols] = d
            g0 = g0 + d * (z * xa + xs)
            g1 = g1 + d
        st = wide_at(R.locw, j)
        group_rows(st, 0, g0)
        group_rows(st, 3, g1)
        blank(st, 6, 2)

    loop(WIDE // LANES, u2_body)
    wide_start(2, R.locw)
    mixed_copies = [
        remote(R.mixed_local, R.mixed.at[r], R.xs.at[i], R.xr.at[i], (b, to))
        for i, to in enumerate((core_peer, x_row))
    ]
    for c in mixed_copies:
        c.start()
    own = pltpu.make_async_copy(R.mixed_local, R.mixed.at[r], R.xl)
    own.start()
    wide_finish(2, R.g6)

    def widen_back(j):
        cols = aligned(j, LANES)
        f, a, bz = backward_terms(wide_at(R.t6, j), wide_at(R.g6, j), R.norm_widen, cols, OUT)
        for o in range(OD):
            d = f * R.du2[out_rows(o), cols] - a - R.z6[out_rows(o), cols] * bz
            R.dz6[out_rows(o), cols] = (d * R.pix_out[out_rows(o), :]).astype(BF)

    loop(WIDE // LANES, widen_back)

    grad_out = [None, None]
    turn = [0]

    def staged(n, off, fill):
        i = turn[0] % 2
        turn[0] += 1
        if grad_out[i] is not None:
            grad_out[i].wait()
        stage = R.stage.at[i]
        fill(stage)
        copy = pltpu.make_async_copy(
            stage.at[:, :, pl.ds(0, n)], R.grads.at[:, :, pl.ds(off, n)], R.gs.at[i]
        )
        copy.start()
        grad_out[i] = copy

    def fill_out(act, dz):
        def fill(stage):
            def body(j):
                res = dot_w(act(), dz[:, aligned(j, 512)])
                n = res.shape[0] // 8
                stage[:, j, 0:n, :] = res.reshape(8, n, 512).astype(BF)

            loop(WIDE // 512, body)

        return fill

    def fill_conv(win, dz):
        def fill(stage):
            def body(t):
                res = dot_w(win[:, aligned(t, MID)], dz())
                n = MID // 32
                stage[:, :, aligned(t, n), :] = res.reshape(8, 4, n, MID).astype(BF)

            loop(9, body)

        return fill

    def mid_back_sums(dh, z, tot, params):
        def body(j):
            cols = aligned(j, LANES)
            sums = mid_at(tot, j)
            sc, sh = forward_terms(sums, params, cols, OUT)
            xa, xs = xhat_terms(sums, OUT)
            ch = keep(R.chan_mid, cols)
            g0 = jnp.zeros((S, LANES), F32)
            g1 = jnp.zeros((S, LANES), F32)
            for o in range(OD):
                v = z[out_rows(o), cols]
                d = dh[out_rows(o), cols] * (ch * R.pix_out[out_rows(o), :]) * slope(v * sc + sh)
                dh[out_rows(o), cols] = d
                g0 = g0 + d * (v * xa + xs)
                g1 = g1 + d
            st = mid_at(R.loc, j)
            group_rows(st, 0, g0)
            group_rows(st, 3, g1)
            blank(st, 6, 2)

        loop(MID // LANES, body)

    def mid_back_apply(dh, z, tot, grads, params, dest):
        def body(j):
            cols = aligned(j, LANES)
            f, a, bz = backward_terms(mid_at(tot, j), mid_at(grads, j), params, cols, OUT)
            for o in range(OD):
                d = f * dh[out_rows(o), cols] - a - z[out_rows(o), cols] * bz
                dest(o, cols, (d * R.pix_out[out_rows(o), :]).astype(BF))

        loop(MID // LANES, body)

    def reduce_back(dz, weight, dh):
        def body(j):
            w = weight[aligned(j, 2)].reshape(MID // 2, WIDE)
            dh[:, aligned(j, MID // 2)] = dot_t(dz[...], w)

        loop(2, body)

    reduce_back(R.dz6, R.f_w_widen, R.dh)
    mid_back_sums(R.dh, R.z5, R.t5, R.norm_mixing)
    mid_start(4)
    staged(cfg.rows["w_widen"], cfg.offs["w_widen"], fill_out(lambda: R.h5[...], R.dz6))
    mid_finish(4, R.g5)

    def to_d5(o, cols, v):
        R.d5[o + 1, :, cols] = v

    mid_back_apply(R.dh, R.z5, R.t5, R.g5, R.norm_mixing, to_d5)
    pair = edge_exchange(R.d5, 1)
    unit_windows(R.d5, R.win5, range(1, OD + 1), True)
    edge_wait(pair)
    unit_windows(R.d5, R.win5, (0, OD + 1), True)

    def conv_back(j):
        acc = None
        for t in range(9):
            w = R.f_w_mixing[t, aligned(j, 2)].reshape(MID // 2, MID)
            v = dot_t(R.win5[:, t * MID : (t + 1) * MID], w)
            acc = v if acc is None else acc + v
        R.dh[:, aligned(j, MID // 2)] = acc

    loop(2, conv_back)
    mid_back_sums(R.dh, R.z4, R.t4, R.norm_squeeze)
    mid_start(5)
    staged(
        cfg.rows["w_mixing"],
        cfg.offs["w_mixing"],
        fill_conv(R.win4, lambda: R.d5[1 : OD + 1].reshape(M, MID)),
    )
    mid_finish(5, R.g4)

    def to_d4(o, cols, v):
        R.dz4[out_rows(o), cols] = v

    mid_back_apply(R.dh, R.z4, R.t4, R.g4, R.norm_squeeze, to_d4)

    def squeeze_back(j):
        w = R.f_w_squeeze[j]
        n = w.shape[0]
        R.du1[:, aligned(j, n)] = dot_t(R.dz4[...], w)

    loop(4, squeeze_back)

    def u1_back(j):
        cols = aligned(j, LANES)
        u1 = u1_terms(j)
        tot = wide_at(R.t3, j)
        xa3, xs3 = xhat_terms(tot, OUT, 0)
        xas, xss = xhat_terms(tot, OUT, 8)
        ch = keep(R.chan_wide, cols)
        g0 = jnp.zeros((S, LANES), F32)
        g1 = jnp.zeros((S, LANES), F32)
        g2 = jnp.zeros((S, LANES), F32)
        for o in range(OD):
            rows = out_rows(o)
            d = (R.du1[rows, cols] + R.du2[rows, cols]) * (ch * R.pix_out[rows, :]) * slope(u1(o))
            R.du1[rows, cols] = d
            g0 = g0 + d * (R.z3[rows, cols] * xa3 + xs3)
            g2 = g2 + d * (R.zs[rows, cols] * xas + xss)
            g1 = g1 + d
        st = wide_at(R.locw2, j)
        group_rows(st, 0, g0)
        group_rows(st, 3, g1)
        blank(st, 6, 2)
        group_rows(st, 8, g2)
        blank(st, 11, 5)

    loop(WIDE // LANES, u1_back)
    wide_start(3, R.locw2)

    def fill_squeeze(stage):
        def body(j):
            res = dot_w(R.y1[:, aligned(j, WIDE // 8)], R.dz4[...])
            n = res.shape[0] // 4
            stage[j, :, 0:n, :] = res.reshape(4, n, MID).astype(BF)

        loop(8, body)

    staged(cfg.rows["w_squeeze"], cfg.offs["w_squeeze"], fill_squeeze)
    wide_finish(3, R.g3)

    mixed_copies[1].wait_recv()
    onward = remote(R.mixed.at[x_row], R.mixed.at[x_row], R.xs.at[2], R.xr.at[2], (b, core_peer))
    onward.start()

    def u1_apply(j):
        cols = aligned(j, LANES)
        tot, grads = wide_at(R.t3, j), wide_at(R.g3, j)
        f3, a3, b3 = backward_terms(tot, grads, R.norm_expand, cols, OUT, 0, 0, 3)
        fs, as_, bs = backward_terms(tot, grads, R.norm_shortcut, cols, OUT, 8, 8, 3)
        for o in range(OD):
            rows = out_rows(o)
            d = R.du1[rows, cols]
            pix = R.pix_out[rows, :]
            R.dz3[rows, cols] = ((f3 * d - a3 - R.z3[rows, cols] * b3) * pix).astype(BF)
            R.dzs[rows, cols] = ((fs * d - as_ - R.zs[rows, cols] * bs) * pix).astype(BF)

    loop(WIDE // LANES, u1_apply)
    reduce_back(R.dz3, R.f_w_expand, R.dh)
    mid_back_sums(R.dh, R.z2, R.t2, R.norm_spatial)
    mid_start(6)
    staged(cfg.rows["w_expand"], cfg.offs["w_expand"], fill_out(lambda: R.h2[...], R.dz3))
    mid_finish(6, R.g2)

    def to_d2(o, cols, v):
        R.d2[o, :, cols] = v

    mid_back_apply(R.dh, R.z2, R.t2, R.g2, R.norm_spatial, to_d2)
    up = remote(R.d2.at[0], R.d2.at[OD], R.hs.at[1], R.hr.at[1], (b, jnp.maximum(r - 1, 0)))

    @pl.when(r > 0)
    def _():
        up.start()

    @pl.when(r == 3)
    def _():
        R.d2[OD] = jnp.zeros(R.d2.shape[1:], BF)

    def even_rows():
        return jnp.concatenate([R.x0[2 * o, 0:S, :] for o in range(OD)], axis=0)

    staged(cfg.rows["w_shortcut"], cfg.offs["w_shortcut"], fill_out(even_rows, R.dzs))

    @pl.when(r < 3)
    def _():
        up.wait_recv()

    @pl.when(r > 0)
    def _():
        up.wait_send()

    def d2_left(j):
        cols = aligned(j, LANES)
        for k in range(OD + 1):
            R.d2l[k, :, cols] = rolled(R.d2[k, :, cols].astype(F32), -1).astype(BF)

    loop(MID // LANES, d2_left)

    def spatial_back(j):
        here, left = R.d2[0:OD].reshape(M, MID), R.d2l[0:OD].reshape(M, MID)
        below, below_left = R.d2[1 : OD + 1].reshape(M, MID), R.d2l[1 : OD + 1].reshape(M, MID)

        def w(dr, dc):
            return R.f_w_spatial[dr * 3 + dc, aligned(j, 2)].reshape(MID // 2, MID)

        cols = aligned(j, MID // 2)
        parts = (
            ((here, 1, 1),),
            ((here, 1, 2), (left, 1, 0)),
            ((here, 2, 1), (below, 0, 1)),
            ((here, 2, 2), (left, 2, 0), (below, 0, 2), (below_left, 0, 0)),
        )
        for i, terms in enumerate(parts):
            rp, cp = divmod(i, 2)
            acc = None
            for v, dr, dc in terms:
                y = dot_t(v, w(dr, dc))
                acc = y if acc is None else acc + y
            for o in range(OD):
                R.dh1[2 * o + rp, out_rows(cp), cols] = acc[out_rows(o)]

    loop(2, spatial_back)

    def h1_back(j):
        cols = aligned(j, LANES)
        sums = mid_at(R.t1, j)
        sc, sh = forward_terms(sums, R.norm_reduce, cols, IN)
        xa, xs = xhat_terms(sums, IN)
        ch = keep(R.chan_mid, cols)
        g0 = jnp.zeros((S, LANES), F32)
        g1 = jnp.zeros((S, LANES), F32)
        for k in range(RD):
            for p in range(2):
                rows = out_rows(p)
                v = R.z1[k, rows, cols]
                d = R.dh1[k, rows, cols] * (ch * R.pix_in[k, rows, :]) * slope(v * sc + sh)
                R.dh1[k, rows, cols] = d
                g0 = g0 + d * (v * xa + xs)
                g1 = g1 + d
        st = mid_at(R.loc, j)
        group_rows(st, 0, g0)
        group_rows(st, 3, g1)
        blank(st, 6, 2)

    loop(MID // LANES, h1_back)
    mid_start(7)
    staged(
        cfg.rows["w_spatial"],
        cfg.offs["w_spatial"],
        fill_conv(R.win1, lambda: R.d2[0:OD].reshape(M, MID)),
    )

    def short_back(j):
        n = CIN // 4
        R.short[:, aligned(j, n)] = dot_t(R.dzs[...], R.f_w_shortcut[j])

    loop(4, short_back)
    mid_finish(7, R.g1)

    def h1_apply(j):
        cols = aligned(j, LANES)
        f, a, bz = backward_terms(mid_at(R.t1, j), mid_at(R.g1, j), R.norm_reduce, cols, IN)
        for k in range(RD):
            for p in range(2):
                rows = out_rows(p)
                d = f * R.dh1[k, rows, cols] - a - R.z1[k, rows, cols] * bz
                R.dz1[k, rows, cols] = (d * R.pix_in[k, rows, :]).astype(BF)

    loop(MID // LANES, h1_apply)

    def fill_reduce(stage):
        n = CIN // 32

        def body(j):
            act = R.x0[:, :, aligned(j, 256)].reshape(RD * 2 * S, 256)
            res = dot_w(act, R.dz1[...].reshape(RD * 2 * S, MID))
            c = 256 // (4 * n)
            stage[pl.ds(j * c, c), :, 0:n, :] = res.reshape(c, 4, n, MID).astype(BF)

        loop(CIN // 256, body)

    staged(cfg.rows["w_reduce"], cfg.offs["w_reduce"], fill_reduce)

    def input_grad(j):
        cols = aligned(j, CIN // 4)
        w = R.f_w_reduce[j]
        ch = jnp.concatenate(
            [keep(R.chan_in, pl.ds(pl.multiple_of(j * (CIN // 4) + i * LANES, LANES), LANES)) for i in range(CIN // 4 // LANES)],
            axis=1,
        )
        for k in range(RD):
            y = dot_t(R.dz1[k], w)
            for p in range(2):
                v = y[out_rows(p)]
                if p == 0 and k % 2 == 0:
                    v = v + R.short[out_rows(k // 2), cols]
                pix = R.pix_in[k, out_rows(p), :]
                R.gin[k, out_rows(p), cols] = v * ch * jnp.concatenate([pix] * (CIN // 4 // LANES), axis=1)

    loop(4, input_grad)

    for name, n in (("g1", 0), ("g2", 0), ("g4", 0), ("g5", 0)):
        out, src = getattr(R, "o" + name), getattr(R, name)
        out[...] = src[...]
    R.og3[...] = R.g3[...]
    R.og6[...] = R.g6[...]

    own.wait()
    mixed_copies[0].wait()
    mixed_copies[1].wait_send()
    onward.wait()
    for u in range(len(units)):
        for i in range(5):
            w_copy(u, i).wait_send()
    for copy in grad_out:
        if copy is not None:
            copy.wait()


def plan(features, w_reduce, w_expand, batch):
    images, rd, _, cin = features.shape
    mid, wide = w_reduce.shape[1], w_expand.shape[1]
    cfg = SimpleNamespace(
        slots=-(-images * 8 // 16) * 16, in_rows=rd, out_rows=rd // 2, batch=batch, mid=mid, wide=wide, cin=cin
    )
    q = (cin // 4, mid // 4, wide // 4)
    cfg.units = (
        [("w_reduce", False, 0, q[0])]
        + [("w_spatial", True, k, 3) for k in (0, 3, 6)]
        + [("w_expand", False, 0, q[1])]
        + [("w_shortcut", False, k * q[0] // 2, q[0] // 2) for k in (0, 1)]
        + [("w_squeeze", False, 0, q[2])]
        + [("w_mixing", True, k, 3) for k in (0, 3, 6)]
        + [("w_widen", False, 0, q[1])]
    )
    cfg.rows = {
        "w_reduce": cin // 32,
        "w_spatial": 9 * mid // 32,
        "w_expand": mid // 8,
        "w_shortcut": cin // 8,
        "w_squeeze": wide // 32,
        "w_mixing": 9 * mid // 32,
        "w_widen": mid // 8,
    }
    cfg.offs, total = {}, 0
    for name, n in cfg.rows.items():
        cfg.offs[name] = total
        total += n
    cfg.total = total
    return cfg


def run_blocks(cfg, vmem_args, hbm_args):
    S, RD, OD, NB = cfg.slots, cfg.in_rows, cfg.out_rows, cfg.batch
    MID, WIDE, CIN = cfg.mid, cfg.wide, cfg.cin
    M = OD * S
    U = len(cfg.units)
    vmem = pl.BlockSpec(memory_space=pltpu.VMEM)
    hbm = pl.BlockSpec(memory_space=pl.ANY)
    sds = jax.ShapeDtypeStruct
    outs = {
        "mixed": (sds((4, OD, S, WIDE), BF), hbm),
        "grads": (sds((8, 4, cfg.total, 512), BF), hbm),
        "gin": (sds((RD, 2 * S, CIN), F32), vmem),
        "og1": (sds((2, 8, MID // 2), F32), vmem),
        "og2": (sds((2, 8, MID // 2), F32), vmem),
        "og3": (sds((4, 16, WIDE // 4), F32), vmem),
        "og4": (sds((2, 8, MID // 2), F32), vmem),
        "og5": (sds((2, 8, MID // 2), F32), vmem),
        "og6": (sds((4, 8, WIDE // 4), F32), vmem),
    }
    V = pltpu.VMEM
    mid_tot = V((2, 8, MID // 2), F32)
    scratch = {
        "f_w_reduce": V((4, CIN // 4, MID), BF),
        "f_w_spatial": V((9, 4, MID // 4, MID), BF),
        "f_w_expand": V((4, MID // 4, WIDE), BF),
        "f_w_shortcut": V((4, CIN // 4, WIDE), BF),
        "f_w_squeeze": V((4, WIDE // 4, MID), BF),
        "f_w_mixing": V((9, 4, MID // 4, MID), BF),
        "f_w_widen": V((4, MID // 4, WIDE), BF),
        "z1": V((RD, 2 * S, MID), F32),
        "win1": V((M, 9 * MID), BF),
        "h1s": V((2, S, MID), BF),
        "h1r": V((2, S, MID), BF),
        "z2": V((M, MID), F32),
        "h2": V((M, MID), BF),
        "z3": V((M, WIDE), F32),
        "zs": V((M, WIDE), F32),
        "y1": V((M, WIDE), BF),
        "z4": V((M, MID), F32),
        "h4": V((OD + 2, S, MID), BF),
        "win4": V((M, 9 * MID), BF),
        "z5": V((M, MID), F32),
        "h5": V((M, MID), BF),
        "z6": V((M, WIDE), F32),
        "mixed_local": V((OD, S, WIDE), BF),
        "du2": V((M, WIDE), F32),
        "dz6": V((M, WIDE), BF),
        "dh": V((M, MID), F32),
        "d5": V((OD + 2, S, MID), BF),
        "win5": V((M, 9 * MID), BF),
        "dz4": V((M, MID), BF),
        "du1": V((M, WIDE), F32),
        "dz3": V((M, WIDE), BF),
        "dzs": V((M, WIDE), BF),
        "d2": V((OD + 1, S, MID), BF),
        "d2l": V((OD + 1, S, MID), BF),
        "dh1": V((RD, 2 * S, MID), F32),
        "dz1": V((RD, 2 * S, MID), BF),
        "short": V((M, CIN), F32),
        "stage": V((2, 8, 4, max(cfg.rows.values()), 512), BF),
        "loc": mid_tot,
        "locw": V((4, 8, WIDE // 4), F32),
        "locw2": V((4, 16, WIDE // 4), F32),
        "t1": mid_tot,
        "t2": mid_tot,
        "t3": V((4, 16, WIDE // 4), F32),
        "t4": mid_tot,
        "t5": mid_tot,
        "t6": V((4, 8, WIDE // 4), F32),
        "g1": mid_tot,
        "g2": mid_tot,
        "g3": V((4, 16, WIDE // 4), F32),
        "g4": mid_tot,
        "g5": mid_tot,
        "g6": V((4, 8, WIDE // 4), F32),
        "rc": V((2, 8, MID // 2), F32),
        "rq": V((2, 2 * NB, 8, MID // 2), F32),
        "rw": V((4, 4, 16, WIDE // 4), F32),
        "wb": V((2, NB, 16, WIDE // 4), F32),
        "wsend": pltpu.SemaphoreType.DMA((U, 5)),
        "wrecv": pltpu.SemaphoreType.DMA((U, 5)),
        "wloc": pltpu.SemaphoreType.DMA((U,)),
        "ms": pltpu.SemaphoreType.DMA((3,)),
        "mr": pltpu.SemaphoreType.DMA((3, 2)),
        "ws": pltpu.SemaphoreType.DMA((4, 3)),
        "wr": pltpu.SemaphoreType.DMA((4, 3)),
        "hs": pltpu.SemaphoreType.DMA((2,)),
        "hr": pltpu.SemaphoreType.DMA((2,)),
        "es": pltpu.SemaphoreType.DMA((2, 2)),
        "er": pltpu.SemaphoreType.DMA((2, 2)),
        "xs": pltpu.SemaphoreType.DMA((3,)),
        "xr": pltpu.SemaphoreType.DMA((3,)),
        "xl": pltpu.SemaphoreType.DMA,
        "gs": pltpu.SemaphoreType.DMA((2,)),
    }
    names = list(vmem_args) + list(hbm_args) + list(outs) + list(scratch)
    res = pl.pallas_call(
        functools.partial(block_kernel, names, cfg),
        out_shape=[o[0] for o in outs.values()],
        in_specs=[vmem] * len(vmem_args) + [hbm] * len(hbm_args),
        out_specs=[o[1] for o in outs.values()],
        scratch_shapes=list(scratch.values()),
        compiler_params=pltpu.CompilerParams(
            collective_id=0, has_side_effects=True, vmem_limit_bytes=63 * 2**20
        ),
    )(*vmem_args.values(), *hbm_args.values())
    return SimpleNamespace(**dict(zip(outs, res)))


def slot_layout(x, slots):
    images, rows, cols, channels = x.shape
    x = jnp.transpose(x, (1, 0, 2, 3)).reshape(rows, images * cols, channels)
    return jnp.pad(x, ((0, 0), (0, slots - images * cols), (0, 0)))


def lanes(x):
    return jnp.broadcast_to(x[..., None], x.shape + (LANES,))


def pad8(x):
    x = x.reshape(-1, x.shape[-1])
    return jnp.pad(x, ((0, 8 - x.shape[0]), (0, 0)))


def unfold_mid(g):
    return jnp.transpose(g, (1, 0, 2)).reshape(8, -1)


def per_device(
    features, w_reduce, w_spatial, w_expand, w_shortcut, w_squeeze, w_mixing, w_widen,
    norm_reduce, norm_spatial, norm_expand, norm_shortcut, norm_squeeze, norm_mixing, norm_widen,
    cotangent, resolution, active,
):
    images, rd, cols_in, cin = features.shape
    od = rd // 2
    nb = lax.axis_size("batch")
    cfg = plan(features, w_reduce, w_expand, nb)
    S, mid, wide = cfg.slots, cfg.mid, cfg.wide
    groups = jnp.arange(3, dtype=jnp.int32)
    members = jnp.sum((resolution[:, None] == groups[None, :]).astype(F32), axis=0)
    sides_grp = 10.0 + 2.0 * groups.astype(F32)
    count_in = members * sides_grp * sides_grp
    count_out = members * (sides_grp * 0.5) * (sides_grp * 0.5)
    counts = jnp.concatenate([1.0 / count_in, 1.0 / count_out, jnp.zeros((2,), F32)])
    local_res = lax.dynamic_slice_in_dim(resolution, lax.axis_index("batch") * images, images)
    row = lax.axis_index("rows")
    slot_res = jnp.pad(jnp.repeat(local_res, 8), (0, S - 8 * images), constant_values=-1)
    slot_col = jnp.pad(jnp.tile(jnp.arange(8, dtype=jnp.int32), images), (0, S - 8 * images))
    onehot = (slot_res[None, :] == groups[:, None]).astype(F32)
    side_out = jnp.where(slot_res >= 0, 5 + slot_res, 0)
    rows_out = row * od + jnp.arange(od, dtype=jnp.int32)
    rows_in = row * rd + jnp.arange(rd, dtype=jnp.int32)
    pix_out = ((rows_out[:, None] < side_out[None, :]) & (slot_col[None, :] < side_out[None, :])).astype(F32)
    parity = jnp.arange(2, dtype=jnp.int32)
    pix_in = (
        (rows_in[:, None, None] < 2 * side_out[None, None, :])
        & ((2 * slot_col[None, None, :] + parity[None, :, None]) < 2 * side_out[None, None, :])
    ).astype(F32)

    def chan(width):
        limit = active * (width // mid)
        return pad8((jnp.arange(width, dtype=jnp.int32)[None, :] < limit[:, None]).astype(F32))

    chan_in = chan(cin)
    x = jnp.pad(features, ((0, 0), (0, 0), (0, 16 - cols_in), (0, 0)))
    x = x.reshape(images, rd, 8, 2, cin)
    x = jnp.transpose(x, (1, 3, 0, 2, 4)).reshape(rd, 2, images * 8, cin)
    x = jnp.pad(x, ((0, 0), (0, 0), (0, S - images * 8), (0, 0)))
    slot_chan = jnp.where(slot_res[:, None] == 0, chan_in[0:1], jnp.where(slot_res[:, None] == 1, chan_in[1:2], chan_in[2:3]))
    x0 = jnp.where((pix_in[..., None] * slot_chan[None, None]) > 0, x, jnp.zeros((), BF)).reshape(rd, 2 * S, cin)
    ct = slot_layout(jnp.pad(cotangent, ((0, 0), (0, 0), (0, 8 - cotangent.shape[2]), (0, 0))), S)

    vmem_args = {
        "x0": x0,
        "cotangent": ct.reshape(od * S, wide),
        "pix_in": lanes(pix_in).reshape(rd, 2 * S, LANES),
        "pix_out": lanes(pix_out).reshape(od * S, LANES),
        "onehot": lanes(onehot),
        "counts": lanes(counts),
        "chan_mid": chan(mid),
        "chan_wide": chan(wide),
        "chan_in": chan_in,
        "norm_reduce": pad8(norm_reduce),
        "norm_spatial": pad8(norm_spatial),
        "norm_expand": pad8(norm_expand),
        "norm_shortcut": pad8(norm_shortcut),
        "norm_squeeze": pad8(norm_squeeze),
        "norm_mixing": pad8(norm_mixing),
        "norm_widen": pad8(norm_widen),
    }
    hbm_args = {
        "w_reduce": w_reduce,
        "w_spatial": w_spatial.reshape(9, -1, mid),
        "w_expand": w_expand,
        "w_shortcut": w_shortcut,
        "w_squeeze": w_squeeze,
        "w_mixing": w_mixing.reshape(9, -1, mid),
        "w_widen": w_widen,
    }
    res = run_blocks(cfg, vmem_args, hbm_args)
    out_cols = cotangent.shape[2]
    mixed = res.mixed.reshape(4 * od, S, wide)[:, : images * 8].reshape(4 * od, images, 8, wide)
    mixed = jnp.transpose(mixed, (1, 0, 2, 3))[:, :, :out_cols]
    gin = res.gin.reshape(rd, 2, S, cin)[:, :, : images * 8].reshape(rd, 2, images, 8, cin)
    gin = jnp.transpose(gin, (2, 0, 3, 1, 4)).reshape(images, rd, 16, cin)[:, :, :cols_in]

    def unpack(grads, name, b8):
        g = grads[:, :, cfg.offs[name] : cfg.offs[name] + cfg.rows[name]]
        n = cfg.rows[name]
        if name in ("w_spatial", "w_mixing"):
            k = n // 9
            return jnp.transpose(g.reshape(b8, 4, 9, k, 512), (2, 0, 1, 3, 4)).reshape(3, 3, b8 * 4 * k, 512)
        if name in ("w_expand", "w_shortcut", "w_widen"):
            return jnp.transpose(g, (0, 2, 1, 3)).reshape(b8 * n, 2048)
        return g.reshape(b8 * 4 * n, 512)

    order = ("w_reduce", "w_spatial", "w_expand", "w_shortcut", "w_squeeze", "w_mixing", "w_widen")
    totals = []
    for name in order:
        part = unpack(res.grads, name, 8)
        dim = 2 if part.ndim == 4 else 0
        part = lax.psum_scatter(part, "batch", scatter_dimension=dim, tiled=True)
        totals.append(lax.psum(part, "rows").astype(F32))

    def mid_norm(g):
        return unfold_mid(g)[:6].reshape(2, 3, mid)

    def wide_norm(g):
        return jnp.transpose(g, (1, 0, 2)).reshape(g.shape[1], wide)

    g3 = wide_norm(res.og3)
    return (
        mixed,
        gin,
        *totals,
        mid_norm(res.og1),
        mid_norm(res.og2),
        g3[:6].reshape(2, 3, wide),
        jnp.concatenate([g3[8:11], g3[3:6]]).reshape(2, 3, wide),
        mid_norm(res.og4),
        mid_norm(res.og5),
        wide_norm(res.og6)[:6].reshape(2, 3, wide),
    )


def solution(mesh):
    w2, w4 = P("rows", None), P(None, None, "rows", None)
    o2, o4 = P("batch", None), P(None, None, "batch", None)
    return jax.shard_map(
        per_device,
        mesh=mesh,
        in_specs=(P("batch", "rows", None, None), w2, w4, w2, w2, w2, w4, w2)
        + (P(),) * 7
        + (P("batch", "rows", None, None), P(), P()),
        out_specs=(P("batch", None, None, None), P("batch", "rows", None, None), o2, o4, o2, o2, o2, o4, o2)
        + (P(),) * 7,
        check_vma=False,
    )
```

time: 1920 us -> 895 us (0.47)
  waiting for transfers between devices: 1120 us -> 582 us
  blocking collectives: 410 us -> 0 us
  Pallas kernels: 0 us -> 216 us
  local copies, waits for them, and re-layouts: 184 us -> 67.2 us
  matrix products: 109 us -> 0 us
  other arithmetic: 54.8 us -> 14 us
    psum x10 -> x0, blocking collectives: 410 us -> none  [the longest x5 206 us: global_grads(): summed = lax.psum(joined, ('batch', 'rows'))]
    reduce_scatter x7 -> x6, waiting for transfers between devices: 782 us -> 473 us  [per_device(): part = lax.psum_scatter(part, 'batch', scatter_dimension=dim, tiled=True)]
    psum x3 -> x1, waiting for transfers between devices: 287 us -> 52.2 us  [per_device(): totals.append(lax.psum(part, 'rows').astype(F32))]
    pallas_call x0 -> x1, Pallas kernels: none -> 216 us  [run_blocks(): pl.pallas_call(functools.partial(block_kernel, names, cfg), out_shape=[o[...]
    dot_general x90 -> x0, matrix products: 109 us -> none  [the longest x5 15.9 us: weight_grad(): jnp.einsum('irck,ircn->kn', values, grads, preferred_element_type=jnp.flo...]
    unnamed x305 -> x60, local copies, waits for them, and re-layouts: 114 us -> 19.4 us
    unnamed x18 -> x9, waiting for transfers between devices: 4.51 us -> 57.2 us
    all_gather x8 -> x0, waiting for transfers between devices: 41.9 us -> none  [the longest x1 14.4 us: per_device(): lax.all_gather(w_squeeze, 'rows', axis=0, tiled=True)]
  transfers between devices with their start and end apart: 24 -> 8, of which waited for: 16 -> 8; matrix products, arithmetic and copies ran while one was open for 8% -> 5% of each run, Pallas kernels for 0% -> 0%
where the time goes in v1:
time: 895 us
  waiting for transfers between devices  582 us (65%)
  Pallas kernels  216 us (24%)
  local copies, waits for them, and re-layouts  67.2 us (8%)
  between operations  14.6 us (2%)
  other arithmetic  14 us (2%)
    reduce_scatter x6, waiting for transfers between devices, per_device(): part = lax.psum_scatter(part, 'batch', scatter_dimension=dim, tiled=True)  473 us
    pallas_call x1, Pallas kernels, run_blocks(): pl.pallas_call(functools.partial(block_kernel, names, cfg), out_shape=[o[...  216 us
    unnamed x9, waiting for transfers between devices  57.2 us
    psum x1, waiting for transfers between devices, per_device(): totals.append(lax.psum(part, 'rows').astype(F32))  52.2 us
    unnamed x60, local copies, waits for them, and re-layouts  19.4 us
  transfers between devices with their start and end apart: 8, of which 8 were waited for; matrix products, arithmetic and copies ran while one was open for 5% of the time, Pallas kernels for 0%

profile of v1, /device:TPU:0, one launch (start us, length us, event | category | flops | bytes accessed | tf_op | source)
XLA Modules:
  0.0 894.9 jit_solution(7541121474489896462)
XLA Ops:
  10.4 1.7 pad.64
  26.5 216.3 %shard_map.297 = (bf16[4,2,80,2048]{3,2,1,0:T(8,128)(2,1)}, bf16[8,4,640,512]{3,2,1,0:T(8,128)(2,1)}, f32[4,160,1024]{2,1,0:T(8,128)}, f32[2,8,256]{2,1,0:T(8,12...) custom-call(bf16[4,160,1024]{2,1,0:T(8,128)(2,1)} %bitcast.80, ...), custom_call_target="tpu_custom_call" | custom-call | tf_op jit(solution)/shard_map/pallas_call | solution.py:1073
  242.9 2.5 slice_bitcast_fusion
  245.4 3.2 copy.139
  248.6 3.4 copy.142
  252.1 2.3 slice.97
  254.5 4.9 slice_bitcast_fusion.2
  261.0 1.9 copy.141
  265.5 1.9 copy.143
  267.5 6.7 fusion.5
  274.2 2.7 copy.118
  277.0 5.4 copy.121
  282.5 56.6 %reduce-scatter.22.cloned.1.call-done = bf16[128,2048]{1,0:T(8,128)(2,1)} async-done(((bf16[1024,2048]{1,0:T(8,128)(2,1)}), bf16[128,2048]{1,0:T(8,128)(2,1)}) %reduce-scatter.22.cloned.1.call-update) | async-done | bytes 524304
  339.1 2.0 copy.138
  341.1 65.4 %reduce-scatter.10.cloned.1.call-done = bf16[128,512]{1,0:T(8,128)(2,1)} async-done(((bf16[1024,512]{1,0:T(8,128)(2,1)}), bf16[128,512]{1,0:T(8,128)(2,1)}) %reduce-scatter.10.cloned.1.call-update) | async-done | bytes 131088 | tf_op jit(solution)/shard_map/reduce_scatter | solution.py:1198
  406.5 70.1 %reduce-scatter.14.cloned.1.call-done = bf16[64,2048]{1,0:T(8,128)(2,1)} async-done(((bf16[512,2048]{1,0:T(8,128)(2,1)}), bf16[64,2048]{1,0:T(8,128)(2,1)}) %reduce-scatter.14.cloned.1.call-update) | async-done | bytes 262160 | tf_op jit(solution)/shard_map/reduce_scatter | solution.py:1198
  476.7 70.0 %reduce-scatter.16.cloned.1.call-done = bf16[256,512]{1,0:T(8,128)(2,1)} async-done(((bf16[2048,512]{1,0:T(8,128)(2,1)}), bf16[256,512]{1,0:T(8,128)(2,1)}) %reduce-scatter.16.cloned.1.call-update) | async-done | bytes 262160 | tf_op jit(solution)/shard_map/reduce_scatter | solution.py:1198
  546.7 70.0 %reduce-scatter.20.cloned.1.call-done = bf16[64,2048]{1,0:T(8,128)(2,1)} async-done(((bf16[512,2048]{1,0:T(8,128)(2,1)}), bf16[64,2048]{1,0:T(8,128)(2,1)}) %reduce-scatter.20.cloned.1.call-update) | async-done | bytes 262160 | tf_op jit(solution)/shard_map/reduce_scatter | solution.py:1198
  616.8 98.2 %reduce-scatter.12.cloned.1.call-done = bf16[3,3,64,512]{3,2,1,0:T(8,128)(2,1)} async-done(((bf16[3,3,512,512]{3,2,1,0:T(8,128)(2,1)}), bf16[3,3,64,512]{3,2,1,0:T(8,128)(2,1)}) %reduce-scatter.12.cloned.1.call-update) | async-done | bytes 589840 | tf_op jit(solution)/shard_map/reduce_scatter | solution.py:1198
  714.9 99.1 %reduce-scatter.18.cloned.1.call-done = bf16[3,3,64,512]{3,2,1,0:T(8,128)(2,1)} async-done(((bf16[3,3,512,512]{3,2,1,0:T(8,128)(2,1)}), bf16[3,3,64,512]{3,2,1,0:T(8,128)(2,1)}) %reduce-scatter.18.cloned.1.call-update) | async-done | bytes 589840 | tf_op jit(solution)/shard_map/reduce_scatter | solution.py:1198
  826.1 52.2 %all-reduce.19.cloned.1.call-done = (bf16[128,2048]{0,1:T(8,128)(2,1)}, bf16[128,512]{1,0:T(8,128)(2,1)}, bf16[3,3,64,512]{3,2,1,0:T(8,128)(2,1)}, bf16[64,2048]...) async-done(((bf16[128,2048]{0,1:T(8,128)(2,1)}, bf16[128,512]{1,0:T(8,128)(2,1)}, ...) | async-done | bytes 2621456 | tf_op jit(solution)/shard_map/psum | solution.py:1199
  878.2 1.7 convert_element_type.92
  879.9 2.3 convert_element_type.93
  882.2 1.8 convert_element_type.94
  (159 shorter events, 37.8 us)
Async XLA Ops:
  7.2 6.0 copy-start.4
  7.2 331.9 %reduce-scatter.22.cloned.1.call-start = ((), (), s32[]{:S(2)}) async-start(), calls=%async_computation.13 | async-start | bytes 4718592
  12.8 4.4 copy-start.16
  12.8 5.0 copy-start.17
  12.8 5.6 copy-start.9
  12.8 6.3 copy-start.10
  12.9 7.0 copy-start.18
  13.2 7.3 copy-start.19
  13.2 8.0 copy-start.11
  252.1 154.5 %reduce-scatter.10.cloned.1.call-start = ((), (), s32[]{:S(2)}) async-start(), calls=%async_computation.7 | async-start | bytes 1179648 | tf_op jit(solution)/shard_map/reduce_scatter | solution.py:1198
  254.5 222.2 %reduce-scatter.14.cloned.1.call-start = ((), (), s32[]{:S(2)}) async-start(), calls=%async_computation.9 | async-start | bytes 2359296 | tf_op jit(solution)/shard_map/reduce_scatter | solution.py:1198
  263.0 283.7 %reduce-scatter.16.cloned.1.call-start = ((), (), s32[]{:S(2)}) async-start(), calls=%async_computation.10 | async-start | bytes 2359296 | tf_op jit(solution)/shard_map/reduce_scatter | solution.py:1198
  263.6 353.2 %reduce-scatter.20.cloned.1.call-start = ((), (), s32[]{:S(2)}) async-start(), calls=%async_computation.12 | async-start | bytes 2359296 | tf_op jit(solution)/shard_map/reduce_scatter | solution.py:1198
  267.4 447.5 %reduce-scatter.12.cloned.1.call-start = ((), (), s32[]{:S(2)}) async-start(), calls=%async_computation.8 | async-start | bytes 5308416 | tf_op jit(solution)/shard_map/reduce_scatter | solution.py:1198
  276.9 537.1 %reduce-scatter.18.cloned.1.call-start = ((), (), s32[]{:S(2)}) async-start(), calls=%async_computation.11 | async-start | bytes 5308416 | tf_op jit(solution)/shard_map/reduce_scatter | solution.py:1198
  282.4 531.6 %copy-start.1 = (bf16[4,2,80,2048]{3,2,1,0:T(8,128)(2,1)S(1)}, bf16[4,2,80,2048]{3,2,1,0:T(8,128)(2,1)}, u32[]{:S(2)}) copy-start(bf16[4,2,80,2048]{3,2,1,0:T(8,128)(2,1)} %get-tuple-element.25) | copy-start | bytes 7864324
  282.4 595.8 %all-reduce.19.cloned.1.call-start = ((), (), s32[]{:S(2)}) async-start(), calls=%async_computation.14 | async-start | bytes 5242880 | tf_op jit(solution)/shard_map/psum | solution.py:1199
  819.7 4.3 copy-start.13
  819.8 4.9 copy-start.12
  819.8 5.6 copy-start.8
  878.2 5.8 copy-start.3
  878.2 7.0 copy-start.6
  879.9 6.2 copy-start.2
  882.2 5.0 copy-start.5
  (4 other events, 9.0 us)
Sparse Core Ops, SparseCore 0:
  252.2 86.8 reduce-scatter.21
  343.4 63.0 reduce-scatter.9
  410.1 66.5 reduce-scatter.13
  480.1 66.5 reduce-scatter.15
  550.1 66.6 reduce-scatter.19
  620.3 94.6 reduce-scatter.11
  718.6 95.3 reduce-scatter.17
  817.4 60.7 all-reduce.18

commit v2 on v1

v2 whole, which is shorter than its diff:
```python
import functools
from types import SimpleNamespace

import jax
import jax.numpy as jnp
from jax import lax
from jax.experimental import pallas as pl
from jax.experimental.pallas import tpu as pltpu
from jax.sharding import PartitionSpec as P

eps = 1e-05
MESH = pl.DeviceIdType.MESH
BF = jnp.bfloat16
F32 = jnp.float32
LANES = 128
REDUCE, SPATIAL, EXPAND, SHORTCUT, SQUEEZE, MIXING, WIDEN = range(7)
DX, DY, DN, DF = range(4)


def dot(a, b):
    return jnp.dot(a, b, preferred_element_type=F32)


def dot_t(a, b):
    return lax.dot_general(a, b, (((1,), (1,)), ((), ())), preferred_element_type=F32)


def dot_w(a, b):
    return lax.dot_general(a, b, (((0,), (0,)), ((), ())), preferred_element_type=F32)


def aligned(index, size):
    return pl.ds(pl.multiple_of(index * size, size), size)


def loop(count, body):
    def step(i, carry):
        body(i)
        return carry

    lax.fori_loop(0, count, step, 0)


def silu_parts(u):
    s = jax.nn.sigmoid(u)
    return s, u * s


def slope(u):
    s = jax.nn.sigmoid(u)
    return s * (1.0 + u * (1.0 - s))


def block_kernel(names, cfg, *refs):
    R = SimpleNamespace(**dict(zip(names, refs)))
    S, RD, OD, NB = cfg.slots, cfg.in_rows, cfg.out_rows, cfg.batch
    MID, WIDE, CIN = cfg.mid, cfg.wide, cfg.cin
    M = OD * S
    b = lax.axis_index("batch")
    r = lax.axis_index("rows")
    core = lax.rem(r, 2)
    xb = lax.div(r, 2)
    core_peer = r + 1 - 2 * core
    x_row = lax.rem(r + 2, 4)
    diag = 3 - r
    half = lax.rem(b, 2)
    y_b = b + 1 - 2 * half

    def flip(i, j):
        out = jnp.int32(0)
        bit = 1
        while bit < 2 * NB:
            p, q = lax.rem(lax.div(i, bit), 2), lax.rem(lax.div(j, bit), 2)
            out = out + bit * (p + q - 2 * p * q)
            bit *= 2
        return out

    me = b * 2 + xb

    def remote(src, dst, send, recv, dev):
        return pltpu.make_async_remote_copy(
            src_ref=src, dst_ref=dst, send_sem=send, recv_sem=recv, device_id=dev, device_id_type=MESH
        )

    def team(id2):
        return (lax.div(id2, 2), 2 * lax.rem(id2, 2) + core)

    units = cfg.units
    wsend, wrecv, wloc = R.wsend, R.wrecv, R.wloc

    def wview(u, shard, part):
        w, k0, kn = units[u]
        start, size = k0, kn
        if part is not None:
            size = kn // 2
            start = k0 + part * size
        full = getattr(R, "f" + str(w))
        return full.at[pl.ds(pl.multiple_of(shard * (full.shape[0] // 4) + start, 16), size)]

    def w_copy(u, i):
        if i < 2:
            view = wview(u, r, None if i == 0 else half)
            dev = (b, core_peer) if i == 0 else (b, x_row)
        else:
            view = wview(u, x_row, 1 - half if i == 4 else half)
            dev = (y_b, r) if i == 3 else (b, core_peer)
        return remote(view, view, wsend.at[u, i], wrecv.at[u, i], dev)

    def w_local(w):
        src, full = getattr(R, "w" + str(w)), getattr(R, "f" + str(w))
        n, quarter = src.shape[0], full.shape[0] // 4
        return [
            pltpu.make_async_copy(
                src.at[:, pl.ds(512 * i, 512)],
                full.at[pl.ds(pl.multiple_of(r * quarter + i * n, 16), n)],
                wloc.at[w, i],
            )
            for i in range(src.shape[1] // 512)
        ]

    loaded = [w_local(w) for w in range(7)]
    for w in range(7):
        for c in loaded[w]:
            c.start()
        if w == 0:
            x0_load = pltpu.make_async_copy(R.features, R.x0, R.ld.at[0])
            x0_load.start()
    ct_load = pltpu.make_async_copy(R.cotangent, R.ct, R.ld.at[1])
    ct_load.start()
    at_home = set()

    images = cfg.images
    column = lax.broadcasted_iota(jnp.int32, (8, LANES), 0).astype(F32)
    if 8 * images < S:
        tail = slice(8 * images, S)
        none = jnp.zeros((S - 8 * images, LANES), F32)
        R.active_slot[tail, :] = none
        for g in range(3):
            R.onehot[g, tail, :] = none
        for o in range(OD):
            R.pix_out[o * S + 8 * images : (o + 1) * S, :] = none
        for k in range(RD):
            for p in range(2):
                R.pix_in[k, p * S + 8 * images : (p + 1) * S, :] = none

    for i in range(images):
        group = R.resolution[b * images + i]
        side = (5 + group).astype(F32)
        here = slice(8 * i, 8 * i + 8)
        limit = jnp.zeros((8, LANES), F32)
        for g in range(3):
            is_g = jnp.where(group == g, 1.0, 0.0)
            R.onehot[g, here, :] = jnp.full((8, LANES), is_g, F32)
            limit = limit + is_g * R.active[g].astype(F32)
        R.active_slot[here, :] = limit
        for o in range(OD):
            inside = jnp.where((r * OD + o).astype(F32) < side, side, 0.0)
            R.pix_out[o * S + 8 * i : o * S + 8 * i + 8, :] = jnp.where(column < inside, 1.0, 0.0)
        for k in range(RD):
            inside = jnp.where((r * RD + k).astype(F32) < 2.0 * side, 2.0 * side, 0.0)
            for p in range(2):
                R.pix_in[k, p * S + 8 * i : p * S + 8 * i + 8, :] = jnp.where(2.0 * column + p < inside, 1.0, 0.0)

    bar = pltpu.get_barrier_semaphore()
    for dev in ((b, core_peer), (b, diag)):
        pl.semaphore_signal(bar, inc=1, device_id=dev, device_id_type=MESH)

    def greet(j):
        pl.semaphore_signal(bar, inc=1, device_id=team(flip(me, j + 1)), device_id_type=MESH)

    loop(2 * NB - 1, greet)
    pl.semaphore_wait(bar, 2 * NB + 1)

    def w_start(u):
        w = units[u][0]
        if w not in at_home:
            at_home.add(w)
            for c in loaded[w]:
                c.wait()
        w_copy(u, 1).start()
        w_copy(u, 0).start()

    def w_second(u):
        w_copy(u, 1).wait_recv()
        w_copy(u, 3).start()
        w_copy(u, 2).start()

    def w_third(u):
        w_copy(u, 3).wait_recv()
        w_copy(u, 4).start()

    def w_ready(u):
        for i in (0, 2, 4):
            w_copy(u, i).wait_recv()

    pumped = [0]

    def pump(steps):
        for _ in range(steps):
            n = pumped[0]
            if n >= len(units) + 2:
                return
            if n < len(units):
                w_start(n)
            if 0 <= n - 1 < len(units):
                w_second(n - 1)
            if 0 <= n - 2 < len(units):
                w_third(n - 2)
            pumped[0] = n + 1

    def need(name):
        last = max(u for u in range(len(units)) if units[u][0] == name)
        while pumped[0] < last + 3:
            pump(1)
        for u in range(len(units)):
            if units[u][0] == name:
                w_ready(u)

    def mid_start(k):
        p = k % 2
        swap = remote(R.loc.at[1 - core], R.rc.at[p], R.ms.at[0], R.mr.at[0, p], (b, core_peer))
        swap.start()
        swap.wait_recv()
        R.rq[p, me] = R.loc[core] + R.rc[p]

        def send(j):
            to = team(flip(me, j + 1))
            remote(R.rq.at[p, me], R.rq.at[p, me], R.ms.at[1], R.mr.at[1, p], to).start()

        loop(2 * NB - 1, send)
        swap.wait_send()

    def mid_finish(k, tot):
        p = k % 2
        rest = R.rq.at[p, pl.ds(0, 2 * NB - 1)]
        every = remote(rest, rest, R.ms.at[1], R.mr.at[1, p], (b, x_row))
        every.wait_recv()
        total = R.rq[p, 0]
        for j in range(1, 2 * NB):
            total = total + R.rq[p, j]
        tot[core] = total
        back = remote(tot.at[core], tot.at[core], R.ms.at[2], R.mr.at[2, p], (b, core_peer))
        back.start()
        every.wait_send()
        back.wait()

    def wide_start(k, loc):
        n = loc.shape[1]
        rw, wb = R.rw.at[k % 2, :, pl.ds(0, n)], R.wb.at[k % 2, :, pl.ds(0, n)]
        rw[r] = loc[r]
        for to in (core_peer, x_row, diag):
            remote(loc.at[to], rw.at[r], R.ws.at[k, 0], R.wr.at[k, 0], (b, to)).start()
        three = remote(loc.at[pl.ds(0, 3)], rw.at[pl.ds(0, 3)], R.ws.at[k, 0], R.wr.at[k, 0], (b, core_peer))
        three.wait_recv()
        wb[b] = rw[0] + rw[1] + (rw[2] + rw[3])

        def send(j):
            to = lax.rem(b + j + 1, NB)
            remote(wb.at[b], wb.at[b], R.ws.at[k, 1], R.wr.at[k, 1], (to, r)).start()

        loop(NB - 1, send)
        three.wait_send()

    def wide_finish(k, tot):
        n = tot.shape[1]
        wb = R.wb.at[k % 2, :, pl.ds(0, n)]
        rest = wb.at[pl.ds(0, NB - 1)]
        every = remote(rest, rest, R.ws.at[k, 1], R.wr.at[k, 1], (b, x_row))
        every.wait_recv()
        total = wb[0]
        for j in range(1, NB):
            total = total + wb[j]
        tot[r] = total
        for to in (core_peer, x_row, diag):
            remote(tot.at[r], tot.at[r], R.ws.at[k, 2], R.wr.at[k, 2], (b, to)).start()
        three = remote(tot.at[pl.ds(0, 3)], tot.at[pl.ds(0, 3)], R.ws.at[k, 2], R.wr.at[k, 2], (b, core_peer))
        every.wait_send()
        three.wait()

    def mid_at(ref, j):
        return ref.at[lax.div(j, 2), :, aligned(lax.rem(j, 2), LANES)]

    def wide_at(ref, j):
        return ref.at[lax.div(j, 4), :, aligned(lax.rem(j, 4), LANES)]

    def group_rows(ref, row, values):
        for g in range(3):
            ref[row + g : row + g + 1, :] = jnp.sum(values * R.onehot[g], axis=0, keepdims=True)

    def blank(ref, row, rows):
        ref[row : row + rows, :] = jnp.zeros((rows, LANES), F32)

    def spread(rows3):
        return rows3[0] * R.onehot[0] + rows3[1] * R.onehot[1] + rows3[2] * R.onehot[2]

    def moments(sums, inv_n, row=0):
        means, invs = [], []
        for g in range(3):
            n = 1.0 / inv_n[g]
            mean = sums[row + g : row + g + 1, :] * n
            var = sums[row + 3 + g : row + 4 + g, :] * n - mean * mean
            means.append(mean)
            invs.append(lax.rsqrt(var + eps))
        return means, invs

    OUT = [cfg.members * (5.0 + g) * (5.0 + g) for g in range(3)]
    IN = [cfg.members * (10.0 + 2.0 * g) * (10.0 + 2.0 * g) for g in range(3)]

    def forward_terms(sums, params, cols, inv_n, row=0):
        means, invs = moments(sums, inv_n, row)
        scales = [invs[g] * params[0, g : g + 1, cols] for g in range(3)]
        shifts = [params[1, g : g + 1, cols] - means[g] * scales[g] for g in range(3)]
        return spread(scales), spread(shifts)

    def xhat_terms(sums, inv_n, row=0):
        means, invs = moments(sums, inv_n, row)
        return spread(invs), spread([-means[g] * invs[g] for g in range(3)])

    def backward_terms(sums, grads, params, cols, inv_n, row=0, g0=0, g1=3):
        means, invs = moments(sums, inv_n, row)
        fs, az, bz = [], [], []
        for g in range(3):
            n = 1.0 / inv_n[g]
            f = invs[g] * params[0, g : g + 1, cols]
            gain = grads[g0 + g : g0 + g + 1, :] * n * invs[g]
            bias = grads[g1 + g : g1 + g + 1, :] * n
            fs.append(f)
            bz.append(f * gain)
            az.append(f * (bias - means[g] * gain))
        return spread(fs), spread(az), spread(bz)

    def keep(j, ratio):
        lane = lax.broadcasted_iota(jnp.int32, (S, LANES), 1).astype(F32) + j * float(LANES)
        return jnp.where(lane < R.active_slot[...] * ratio, 1.0, 0.0)

    def out_rows(k):
        return slice(k * S, (k + 1) * S)

    def groups16(o):
        return slice(o * (S // 16), (o + 1) * (S // 16))

    def forward_stats(z, loc_at, row=0):
        def body(j):
            cols = aligned(j, LANES)
            s = jnp.zeros((S, LANES), F32)
            q = jnp.zeros((S, LANES), F32)
            for o in range(OD):
                v = z[out_rows(o), cols]
                m = v * R.pix_out[out_rows(o), :]
                s = s + m
                q = q + m * v
            st = loc_at(j)
            group_rows(st, row, s)
            group_rows(st, row + 3, q)
            blank(st, row + 6, 2)

        loop(z.shape[-1] // LANES, body)

    def rolled(v, by):
        return pltpu.roll(v, by % S, 0)

    def by_shard(t, j):
        return pl.ds(pl.multiple_of(j * (9 * LANES) + t * LANES, LANES), LANES)

    def by_tap(t, j):
        return pl.ds(pl.multiple_of(t * MID + j * LANES, LANES), LANES)

    def unit_windows(halo, win, rows, flipped):
        place = by_tap if flipped else by_shard

        def body(j):
            cols = aligned(j, LANES)
            for k in rows:
                v = halo[k, :, cols].astype(F32)
                moved = (rolled(v, 1).astype(BF), v.astype(BF), rolled(v, -1).astype(BF))
                for dr in range(3):
                    o = k - dr
                    if not 0 <= o < OD:
                        continue
                    for dc in range(3):
                        t = (2 - dr) * 3 + 2 - dc if flipped else dr * 3 + dc
                        win[out_rows(o), place(t, j)] = moved[dc]

        loop(MID // LANES, body)

    def edge_exchange(halo, k):
        up = remote(halo.at[1], halo.at[OD + 1], R.es.at[k, 0], R.er.at[k, 0], (b, jnp.maximum(r - 1, 0)))
        down = remote(halo.at[OD], halo.at[0], R.es.at[k, 1], R.er.at[k, 1], (b, jnp.minimum(r + 1, 3)))

        @pl.when(r > 0)
        def _():
            up.start()

        @pl.when(r < 3)
        def _():
            down.start()

        @pl.when(r == 0)
        def _():
            halo[0] = jnp.zeros(halo.shape[1:], BF)

        @pl.when(r == 3)
        def _():
            halo[OD + 1] = jnp.zeros(halo.shape[1:], BF)

        return up, down

    def edge_wait(pair):
        up, down = pair

        @pl.when(r < 3)
        def _():
            up.wait_recv()
            down.wait_send()

        @pl.when(r > 0)
        def _():
            down.wait_recv()
            up.wait_send()

    pump(3)
    x0_load.wait()
    need(REDUCE)

    def z1_rows(k):
        def mask(j):
            cols = aligned(j, LANES)
            ch = keep(j, float(CIN // MID))
            for p in range(2):
                m = (ch * R.pix_in[k, out_rows(p), :]).astype(BF)
                R.x0[k, out_rows(p), cols] = R.x0[k, out_rows(p), cols] * m

        loop(CIN // LANES, mask)
        R.z1[k] = dot(R.x0[k], R.f0[...])

    loop(RD, z1_rows)

    def z1_stats(j):
        cols = aligned(j, LANES)
        s = jnp.zeros((S, LANES), F32)
        q = jnp.zeros((S, LANES), F32)
        for k in range(RD):
            for p in range(2):
                v = R.z1[k, out_rows(p), cols]
                m = v * R.pix_in[k, out_rows(p), :]
                s = s + m
                q = q + m * v
        st = mid_at(R.loc, j)
        group_rows(st, 0, s)
        group_rows(st, 3, q)
        blank(st, 6, 2)

    loop(MID // LANES, z1_stats)
    mid_start(0)
    pump(1)
    mid_finish(0, R.t1)

    last = RD - 1

    def h1_body(j):
        cols = aligned(j, LANES)
        sc, sh = forward_terms(mid_at(R.t1, j), R.norm_reduce, cols, IN)
        ch = keep(j, 1.0)
        for k in range(RD - 1, -1, -1):
            for p in range(2):
                u = R.z1[k, out_rows(p), cols] * sc + sh
                h = silu_parts(u)[1] * (ch * R.pix_in[k, out_rows(p), :])
                if k == last:
                    R.h1s[p, :, cols] = h.astype(BF)
                for dr in range(3):
                    o2 = k + 1 - dr
                    if o2 % 2 or not 0 <= o2 // 2 < OD:
                        continue
                    o = o2 // 2
                    taps = ((1, h),) if p == 0 else ((0, rolled(h, 1)), (2, h))
                    for dc, v in taps:
                        t = dr * 3 + dc
                        R.win1[out_rows(o), by_shard(t, j)] = v.astype(BF)

    loop(MID // LANES, h1_body)
    down = remote(R.h1s, R.h1r, R.hs.at[0], R.hr.at[0], (b, jnp.minimum(r + 1, 3)))

    @pl.when(r < 3)
    def _():
        down.start()

    pump(1)

    @pl.when(r > 0)
    def _():
        down.wait_recv()

    @pl.when(r == 0)
    def _():
        R.h1r[...] = jnp.zeros(R.h1r.shape, BF)

    def h1_halo(j):
        cols = aligned(j, LANES)
        even = R.h1r[0, :, cols]
        odd = R.h1r[1, :, cols]
        for dc, v in ((0, rolled(odd.astype(F32), 1).astype(BF)), (1, even), (2, odd)):
            R.win1[out_rows(0), by_shard(dc, j)] = v

    loop(MID // LANES, h1_halo)

    @pl.when(r < 3)
    def _():
        down.wait_send()

    need(SPATIAL)

    def conv(win, weight, z):
        def body(j):
            cols = aligned(j, 256)
            z[:, cols] = dot(win[...], weight[:, cols])

        loop(MID // 256, body)

    conv(R.win1, R.f1, R.z2)
    forward_stats(R.z2, lambda j: mid_at(R.loc, j))
    mid_start(1)
    pump(1)
    mid_finish(1, R.t2)

    def activate(z, tot, params, dest):
        def body(j):
            cols = aligned(j, LANES)
            sc, sh = forward_terms(mid_at(tot, j), params, cols, OUT)
            ch = keep(j, 1.0)
            for o in range(OD):
                u = z[out_rows(o), cols] * sc + sh
                dest(o, cols, (silu_parts(u)[1] * (ch * R.pix_out[out_rows(o), :])).astype(BF))

        loop(MID // LANES, body)

    def to_h2(o, cols, v):
        R.h2[out_rows(o), cols] = v

    activate(R.z2, R.t2, R.norm_spatial, to_h2)
    need(EXPAND)

    def piece(weight, shard, j):
        n = weight.shape[0] // 16
        return weight[pl.ds(pl.multiple_of((shard * 4 + j) * n, n), n), :]

    def block(weight, j):
        return jnp.concatenate([piece(weight, q, j) for q in range(4)], axis=0)

    def expand_to(h, weight, z):
        def body(j):
            z[:, aligned(j, 512)] = dot(h[...], block(weight, j))

        loop(WIDE // 512, body)

    expand_to(R.h2, R.f2, R.z3)
    need(SHORTCUT)

    def zs_body(j):
        cols = aligned(j, 512)
        w = block(R.f3, j)
        for o in range(OD):
            R.zs[out_rows(o), cols] = dot(R.x0[2 * o, 0:S, :], w)

    loop(WIDE // 512, zs_body)
    forward_stats(R.z3, lambda j: wide_at(R.locw2, j), 0)
    forward_stats(R.zs, lambda j: wide_at(R.locw2, j), 8)
    wide_start(0, R.locw2)
    pump(2)
    wide_finish(0, R.t3)

    def u1_terms(j):
        cols = aligned(j, LANES)
        tot = wide_at(R.t3, j)
        sc3, sh3 = forward_terms(tot, R.norm_expand, cols, OUT, 0)
        scs, shs = forward_terms(tot, R.norm_shortcut, cols, OUT, 8)
        shift = sh3 + shs

        def u1(o):
            return R.z3[out_rows(o), cols] * sc3 + R.zs[out_rows(o), cols] * scs + shift

        return u1

    def y1_body(j):
        cols = aligned(j, LANES)
        u1 = u1_terms(j)
        ch = keep(j, float(WIDE // MID))
        for o in range(OD):
            y = silu_parts(u1(o))[1] * (ch * R.pix_out[out_rows(o), :])
            R.y1[out_rows(o), cols] = y.astype(BF)

    loop(WIDE // LANES, y1_body)
    need(SQUEEZE)

    def squeeze_body(j):
        cols = aligned(j, 256)
        R.z4[:, cols] = dot(R.y1[...], R.f4[:, cols])

    loop(MID // 256, squeeze_body)
    forward_stats(R.z4, lambda j: mid_at(R.loc, j))
    mid_start(2)
    pump(2)
    mid_finish(2, R.t4)

    def to_h4(o, cols, v):
        R.h4[o + 1, :, cols] = v

    activate(R.z4, R.t4, R.norm_squeeze, to_h4)
    pair = edge_exchange(R.h4, 0)
    pump(1)
    unit_windows(R.h4, R.win4, range(1, OD + 1), False)
    edge_wait(pair)
    unit_windows(R.h4, R.win4, (0, OD + 1), False)
    need(MIXING)
    conv(R.win4, R.f5, R.z5)
    forward_stats(R.z5, lambda j: mid_at(R.loc, j))
    mid_start(3)
    pump(20)
    mid_finish(3, R.t5)

    def to_h5(o, cols, v):
        R.h5[out_rows(o), cols] = v

    activate(R.z5, R.t5, R.norm_mixing, to_h5)
    need(WIDEN)
    expand_to(R.h5, R.f6, R.z6)
    forward_stats(R.z6, lambda j: wide_at(R.locw, j))
    wide_start(1, R.locw)
    wide_finish(1, R.t6)
    for u in range(len(units)):
        for i in range(5):
            w_copy(u, i).wait_send()

    def u2_body(j):
        cols = aligned(j, LANES)
        tot = wide_at(R.t6, j)
        sc, sh = forward_terms(tot, R.norm_widen, cols, OUT)
        xa, xs = xhat_terms(tot, OUT)
        ch = keep(j, float(WIDE // MID))
        g0 = jnp.zeros((S, LANES), F32)
        g1 = jnp.zeros((S, LANES), F32)
        for o in range(OD):
            z = R.z6[out_rows(o), cols]
            u = z * sc + sh + R.y1[out_rows(o), cols].astype(F32)
            mask = ch * R.pix_out[out_rows(o), :]
            s, su = silu_parts(u)
            R.mixed_local[o, :, :, cols] = (su * mask).reshape(S // 8, 8, LANES).astype(BF)
            d = R.ct[out_rows(o), cols].astype(F32) * mask * (s * (1.0 + u * (1.0 - s)))
            R.du2[groups16(o), :, cols] = d.reshape(S // 16, 16, LANES)
            g0 = g0 + d * (z * xa + xs)
            g1 = g1 + d
        st = wide_at(R.locw, j)
        group_rows(st, 0, g0)
        group_rows(st, 3, g1)
        blank(st, 6, 2)

    ct_load.wait()
    loop(WIDE // LANES, u2_body)
    wide_start(2, R.locw)
    def mixed_copy(i, o):
        row = (x_row if i == 2 else r) * OD + o
        dst = R.mixed.at[:, row]
        src = dst if i == 2 else R.mixed_local.at[o, pl.ds(0, images)]
        if i == 3:
            return pltpu.make_async_copy(src, dst, R.xl.at[o])
        return remote(src, dst, R.xs.at[i, o], R.xr.at[i, o], (b, x_row if i == 1 else core_peer))

    for o in range(OD):
        for i in (1, 0, 3):
            mixed_copy(i, o).start()
    wide_finish(2, R.g6)

    def widen_back(j):
        cols = aligned(j, LANES)
        f, a, bz = backward_terms(wide_at(R.t6, j), wide_at(R.g6, j), R.norm_widen, cols, OUT)
        for o in range(OD):
            d = f * R.du2[groups16(o), :, cols].reshape(S, LANES) - a - R.z6[out_rows(o), cols] * bz
            R.dz6[out_rows(o), cols] = (d * R.pix_out[out_rows(o), :]).astype(BF)

    loop(WIDE // LANES, widen_back)

    mine = {DY: lax.rem(b, 2), DN: lax.rem(lax.div(b, 2), 2), DF: lax.div(b, 4), DX: xb}
    turn = [1]
    begun = {}

    def partner(d):
        other = 1 - 2 * mine[d]
        if d == DX:
            return (b, x_row)
        return (b + other * {DY: 1, DN: 2, DF: 4}[d], r)

    def put(stage, w, core_of, bits, start, value):
        for n0, np_, order in cfg.parts[w]:
            lo, hi = max(start, n0), min(start + value.shape[0], n0 + np_)
            if lo >= hi:
                continue
            idx = 0
            for d in order:
                idx = 2 * idx + bits[d]
            row = 32 * n0 + (core_of * 16 + idx) * np_ + lo - n0
            stage[pl.ds(row if isinstance(row, int) else pl.multiple_of(row, 16), hi - lo), :] = value[
                lo - start : hi - start
            ].astype(BF)

    def batch_bits(y, zn, zf, x):
        return {DY: y, DN: zn, DF: zf, DX: x}

    def staged(w, fill):
        i = turn[0] % 2
        turn[0] += 1
        stage = (R.stage0, R.stage1)[i]
        n = cfg.rows[w]
        assert 32 * n <= stage.shape[0], w
        if cfg.reduce:
            fill(stage)
            begun[w] = (stage, 0)
            for p in range(len(cfg.parts[w])):
                rs_core(w, p).start()
            return
        if i in begun:
            begun[i].wait()
        fill(stage)
        off = 32 * cfg.offs[w]
        begun[i] = pltpu.make_async_copy(
            stage.at[pl.ds(0, 32 * n)], R.grads.at[pl.ds(off, 32 * n)], R.gs.at[i]
        )
        begun[i].start()

    def land_of(w):
        return getattr(R, ("l" if w in cfg.own_landing else "f") + str(w))

    def rs_core(w, p):
        n0, np_, order = cfg.parts[w][p]
        stage = begun[w][0]
        src = stage.at[pl.ds(pl.multiple_of(32 * n0 + (1 - core) * 16 * np_, 16), 16 * np_)]
        dst = land_of(w).at[pl.ds(32 * n0, 16 * np_)]
        return remote(src, dst, R.rs.at[w, p, 0], R.rr.at[w, p, 0], (b, core_peer))

    def rs_kept(w, p, step):
        n0, np_, order = cfg.parts[w][p]
        at, size = 0, 16 * np_
        for d in order[:step]:
            size = size // 2
            at = at + mine[d] * size
        return at, size

    def rs_link(w, p, step):
        n0, np_, order = cfg.parts[w][p]
        at, size = rs_kept(w, p, step - 1)
        size = size // 2
        d = order[step - 1]
        src = land_of(w).at[pl.ds(pl.multiple_of(32 * n0 + at + (1 - mine[d]) * size, 16), size)]
        dst = land_of(w).at[pl.ds(32 * n0 + 32 * np_ - 2 * size, size)]
        i = w
        return remote(src, dst, R.rs.at[i, p, step], R.rr.at[i, p, step], partner(d))

    def final(w):
        return getattr(R, "e" + str(w))

    def rs_add(w, p, step):
        n0, np_, order = cfg.parts[w][p]
        land = land_of(w)
        at, size = rs_kept(w, p, step)
        if step == 0:
            other, start = begun[w][0], 32 * n0 + core * 16 * np_
        else:
            other, start = land, 32 * n0 + 32 * np_ - 2 * size
        last_step = step == 4

        def body(i):
            rows = pl.ds(pl.multiple_of(32 * n0 + at + i * np_, 16), np_)
            v = land[rows, :] + other[pl.ds(pl.multiple_of(start + i * np_, 16), np_), :]
            if not last_step:
                land[rows, :] = v
            elif w in (SPATIAL, MIXING):
                k = cfg.rows[w] // 9
                final(w)[n0 // k : (n0 + np_) // k] = v.reshape(np_ // k, k, 512)
            else:
                final(w)[n0 : n0 + np_, :] = v

        if size == np_:
            body(0)
        else:
            loop(size // np_, body)

    def home(w, row):
        out, n = getattr(R, "o" + str(w)), cfg.rows[w]
        if w in (SPATIAL, MIXING):
            return out.at[:, aligned(row, n // 9)]
        if w in (EXPAND, SHORTCUT, WIDEN):
            return out.at[:, aligned(row, 512)]
        return out.at[aligned(row, n)]

    def fin_copy(w, i):
        dst = home(w, x_row if i == 2 else r)
        src = dst if i == 2 else final(w)
        if i == 3:
            return pltpu.make_async_copy(src, dst, R.fl.at[w])
        return remote(src, dst, R.fs.at[w, i], R.fr.at[w, i], (b, x_row if i == 1 else core_peer))

    def rs_step(*kernels):
        if not cfg.reduce:
            return
        for w in kernels:
            stage, step = begun[w]
            if step == 5:
                fin_copy(w, 1).wait_recv()
                fin_copy(w, 2).start()
            else:
                for p in range(len(cfg.parts[w])):
                    c = rs_core(w, p) if step == 0 else rs_link(w, p, step)
                    c.wait_recv()
                    rs_add(w, p, step)
                    if step < 4:
                        rs_link(w, p, step + 1).start()
                    c.wait_send()
                if step == 4:
                    for i in (1, 0, 3):
                        fin_copy(w, i).start()
            begun[w] = (stage, step + 1)

    def rs_end():
        if not cfg.reduce:
            for copy in begun.values():
                copy.wait()
            return
        left = True
        while left:
            left = [w for w in cfg.rows if begun[w][1] < 6]
            if left:
                low = min(begun[w][1] for w in left)
                rs_step(*[w for w in left if begun[w][1] == low])
        for w in cfg.rows:
            fin_copy(w, 0).wait()
            fin_copy(w, 1).wait_send()
            fin_copy(w, 2).wait()
            fin_copy(w, 3).wait()

    def fill_out(w, act, dz):
        def fill(stage):
            def body(j):
                res = dot_w(act(), dz[:, aligned(j, 512)])
                n = res.shape[0] // 8
                for i in range(8):
                    bits = batch_bits(i % 2, i // 2 % 2, i // 4, lax.div(j, 2))
                    put(stage, w, lax.rem(j, 2), bits, 0, res[i * n : (i + 1) * n])

            loop(WIDE // 512, body)

        return fill

    def fill_conv(w, win, dz):
        def fill(stage):
            n = MID // 32

            def body(q):
                for t0 in range(0, 9, 3):
                    cols = pl.ds(pl.multiple_of(q * (9 * LANES) + t0 * LANES, LANES), 3 * LANES)
                    res = dot_w(win[:, cols], dz())
                    for t in range(3):
                        for i in range(8):
                            bits = batch_bits(i // 4, lax.rem(q, 2), lax.div(q, 2), i // 2 % 2)
                            at = t * LANES + i * n
                            put(stage, w, i % 2, bits, (t0 + t) * n, res[at : at + n])

            loop(4, body)

        return fill

    def mid_back_sums(dh, z, tot, params):
        def body(j):
            cols = aligned(j, LANES)
            sums = mid_at(tot, j)
            sc, sh = forward_terms(sums, params, cols, OUT)
            xa, xs = xhat_terms(sums, OUT)
            ch = keep(j, 1.0)
            g0 = jnp.zeros((S, LANES), F32)
            g1 = jnp.zeros((S, LANES), F32)
            for o in range(OD):
                v = z[out_rows(o), cols]
                d = dh[out_rows(o), cols] * (ch * R.pix_out[out_rows(o), :]) * slope(v * sc + sh)
                dh[out_rows(o), cols] = d
                g0 = g0 + d * (v * xa + xs)
                g1 = g1 + d
            st = mid_at(R.loc, j)
            group_rows(st, 0, g0)
            group_rows(st, 3, g1)
            blank(st, 6, 2)

        loop(MID // LANES, body)

    def mid_back_apply(dh, z, tot, grads, params, dest):
        def body(j):
            cols = aligned(j, LANES)
            f, a, bz = backward_terms(mid_at(tot, j), mid_at(grads, j), params, cols, OUT)
            for o in range(OD):
                d = f * dh[out_rows(o), cols] - a - z[out_rows(o), cols] * bz
                dest(o, cols, (d * R.pix_out[out_rows(o), :]).astype(BF))

        loop(MID // LANES, body)

    def reduce_back(dz, weight, dh):
        def body(i):
            acc = None
            for j in range(4):
                w = jnp.concatenate([piece(weight, 2 * i + q, j) for q in range(2)], axis=0)
                v = dot_t(dz[:, j * 512 : (j + 1) * 512], w)
                acc = v if acc is None else acc + v
            dh[:, aligned(i, MID // 2)] = acc

        loop(2, body)

    def tap_rows(weight, i, t):
        n = MID // 4
        return jnp.concatenate(
            [weight[pl.ds(pl.multiple_of(((2 * i + q) * 9 + t) * n, n), n), :] for q in range(2)], axis=0
        )

    reduce_back(R.dz6, R.f6, R.dh)
    mid_back_sums(R.dh, R.z5, R.t5, R.norm_mixing)
    mid_start(4)
    staged(WIDEN, fill_out(WIDEN, lambda: R.h5[...], R.dz6))
    mid_finish(4, R.g5)

    def to_d5(o, cols, v):
        R.d5[o + 1, :, cols] = v

    mid_back_apply(R.dh, R.z5, R.t5, R.g5, R.norm_mixing, to_d5)
    pair = edge_exchange(R.d5, 1)
    rs_step(WIDEN)
    unit_windows(R.d5, R.win5, range(1, OD + 1), True)
    edge_wait(pair)
    unit_windows(R.d5, R.win5, (0, OD + 1), True)

    def conv_back(j):
        acc = None
        for t in range(9):
            v = dot_t(R.win5[:, t * MID : (t + 1) * MID], tap_rows(R.f5, j, t))
            acc = v if acc is None else acc + v
        R.dh[:, aligned(j, MID // 2)] = acc

    loop(2, conv_back)
    mid_back_sums(R.dh, R.z4, R.t4, R.norm_squeeze)
    mid_start(5)
    rs_step(WIDEN)
    staged(MIXING, fill_conv(MIXING, R.win4, lambda: R.d5[1 : OD + 1].reshape(M, MID)))
    mid_finish(5, R.g4)

    def to_d4(o, cols, v):
        R.dz4[out_rows(o), cols] = v

    mid_back_apply(R.dh, R.z4, R.t4, R.g4, R.norm_squeeze, to_d4)

    def squeeze_back(j):
        n = WIDE // 4
        R.du1[:, :, aligned(j, n)] = dot_t(R.dz4[...], R.f4[aligned(j, n), :]).reshape(M // 16, 16, n)

    loop(4, squeeze_back)

    def u1_back(j):
        cols = aligned(j, LANES)
        u1 = u1_terms(j)
        tot = wide_at(R.t3, j)
        xa3, xs3 = xhat_terms(tot, OUT, 0)
        xas, xss = xhat_terms(tot, OUT, 8)
        ch = keep(j, float(WIDE // MID))
        g0 = jnp.zeros((S, LANES), F32)
        g1 = jnp.zeros((S, LANES), F32)
        g2 = jnp.zeros((S, LANES), F32)
        for o in range(OD):
            rows = out_rows(o)
            d = (R.du1[groups16(o), :, cols] + R.du2[groups16(o), :, cols]).reshape(S, LANES) * (ch * R.pix_out[rows, :]) * slope(u1(o))
            R.du1[groups16(o), :, cols] = d.reshape(S // 16, 16, LANES)
            g0 = g0 + d * (R.z3[rows, cols] * xa3 + xs3)
            g2 = g2 + d * (R.zs[rows, cols] * xas + xss)
            g1 = g1 + d
        st = wide_at(R.locw2, j)
        group_rows(st, 0, g0)
        group_rows(st, 3, g1)
        blank(st, 6, 2)
        group_rows(st, 8, g2)
        blank(st, 11, 5)

    loop(WIDE // LANES, u1_back)
    wide_start(3, R.locw2)

    def fill_squeeze(stage):
        def body(j):
            res = dot_w(R.y1[:, aligned(j, WIDE // 8)], R.dz4[...])
            n = res.shape[0] // 4
            bits = (lax.rem(j, 2), lax.rem(lax.div(j, 2), 2), lax.div(j, 4))
            for i in range(4):
                put(stage, SQUEEZE, i % 2, batch_bits(*bits, i // 2), 0, res[i * n : (i + 1) * n])

        loop(8, body)

    rs_step(MIXING, WIDEN)
    staged(SQUEEZE, fill_squeeze)
    wide_finish(3, R.g3)

    for o in range(OD):
        mixed_copy(1, o).wait_recv()
        mixed_copy(2, o).start()

    def u1_apply(j):
        cols = aligned(j, LANES)
        tot, grads = wide_at(R.t3, j), wide_at(R.g3, j)
        f3, a3, b3 = backward_terms(tot, grads, R.norm_expand, cols, OUT, 0, 0, 3)
        fs, as_, bs = backward_terms(tot, grads, R.norm_shortcut, cols, OUT, 8, 8, 3)
        for o in range(OD):
            rows = out_rows(o)
            d = R.du1[groups16(o), :, cols].reshape(S, LANES)
            pix = R.pix_out[rows, :]
            R.dz6[rows, cols] = ((f3 * d - a3 - R.z3[rows, cols] * b3) * pix).astype(BF)
            R.dzs[rows, cols] = ((fs * d - as_ - R.zs[rows, cols] * bs) * pix).astype(BF)

    loop(WIDE // LANES, u1_apply)
    reduce_back(R.dz6, R.f2, R.dh)
    mid_back_sums(R.dh, R.z2, R.t2, R.norm_spatial)
    mid_start(6)
    rs_step(SQUEEZE, MIXING, WIDEN)
    staged(EXPAND, fill_out(EXPAND, lambda: R.h2[...], R.dz6))

    def even_rows():
        return jnp.concatenate([R.x0[2 * o, 0:S, :] for o in range(OD)], axis=0)

    staged(SHORTCUT, fill_out(SHORTCUT, even_rows, R.dzs))
    mid_finish(6, R.g2)

    def to_d2(o, cols, v):
        R.d2[o, :, cols] = v

    mid_back_apply(R.dh, R.z2, R.t2, R.g2, R.norm_spatial, to_d2)
    up = remote(R.d2.at[0], R.d2.at[OD], R.hs.at[1], R.hr.at[1], (b, jnp.maximum(r - 1, 0)))

    @pl.when(r > 0)
    def _():
        up.start()

    @pl.when(r == 3)
    def _():
        R.d2[OD] = jnp.zeros(R.d2.shape[1:], BF)

    rs_step(EXPAND, SHORTCUT, WIDEN)
    staged(SPATIAL, fill_conv(SPATIAL, R.win1, lambda: R.d2[0:OD].reshape(M, MID)))

    @pl.when(r < 3)
    def _():
        up.wait_recv()

    @pl.when(r > 0)
    def _():
        up.wait_send()

    def dh1_at(k, j, width):
        return pl.ds(pl.multiple_of(k * MID + j * width, LANES), width)

    def d2_left(j):
        cols = aligned(j, LANES)
        for k in range(OD + 1):
            R.d2l[k, :, cols] = rolled(R.d2[k, :, cols].astype(F32), -1).astype(BF)

    loop(MID // LANES, d2_left)

    def spatial_back(j):
        here, left = R.d2[0:OD].reshape(M, MID), R.d2l[0:OD].reshape(M, MID)
        below, below_left = R.d2[1 : OD + 1].reshape(M, MID), R.d2l[1 : OD + 1].reshape(M, MID)

        def w(dr, dc):
            return tap_rows(R.f1, j, dr * 3 + dc)

        cols = aligned(j, MID // 2)
        parts = (
            ((here, 1, 1),),
            ((here, 1, 2), (left, 1, 0)),
            ((here, 2, 1), (below, 0, 1)),
            ((here, 2, 2), (left, 2, 0), (below, 0, 2), (below_left, 0, 0)),
        )
        for i, terms in enumerate(parts):
            rp, cp = divmod(i, 2)
            acc = None
            for v, dr, dc in terms:
                y = dot_t(v, w(dr, dc))
                acc = y if acc is None else acc + y
            for o in range(OD):
                R.zs[out_rows(cp), dh1_at(2 * o + rp, j, MID // 2)] = acc[out_rows(o)]

    loop(2, spatial_back)

    def h1_back(j):
        cols = aligned(j, LANES)
        sums = mid_at(R.t1, j)
        sc, sh = forward_terms(sums, R.norm_reduce, cols, IN)
        xa, xs = xhat_terms(sums, IN)
        ch = keep(j, 1.0)
        g0 = jnp.zeros((S, LANES), F32)
        g1 = jnp.zeros((S, LANES), F32)
        for k in range(RD):
            for p in range(2):
                rows = out_rows(p)
                v = R.z1[k, rows, cols]
                d = R.zs[rows, dh1_at(k, j, LANES)] * (ch * R.pix_in[k, rows, :]) * slope(v * sc + sh)
                R.zs[rows, dh1_at(k, j, LANES)] = d
                g0 = g0 + d * (v * xa + xs)
                g1 = g1 + d
        st = mid_at(R.loc, j)
        group_rows(st, 0, g0)
        group_rows(st, 3, g1)
        blank(st, 6, 2)

    loop(MID // LANES, h1_back)
    mid_start(7)
    rs_step(SPATIAL, SQUEEZE, MIXING, EXPAND, SHORTCUT)

    def short_back(j):
        acc = None
        for i in range(4):
            v = dot_t(R.dzs[:, i * 512 : (i + 1) * 512], piece(R.f3, j, i))
            acc = v if acc is None else acc + v
        R.z6[:, aligned(j, CIN // 4)] = acc

    loop(4, short_back)
    mid_finish(7, R.g1)

    def h1_apply(j):
        cols = aligned(j, LANES)
        f, a, bz = backward_terms(mid_at(R.t1, j), mid_at(R.g1, j), R.norm_reduce, cols, IN)
        for k in range(RD):
            for p in range(2):
                rows = out_rows(p)
                d = f * R.zs[rows, dh1_at(k, j, LANES)] - a - R.z1[k, rows, cols] * bz
                R.y1[rows, dh1_at(k, j, LANES)] = (d * R.pix_in[k, rows, :]).astype(BF)

    loop(MID // LANES, h1_apply)

    def dz1(k):
        return R.y1[:, k * MID : (k + 1) * MID]

    def fill_reduce(stage):
        n = CIN // 32

        def body(j):
            act = R.x0[:, :, aligned(j, 256)].reshape(RD * 2 * S, 256)
            res = dot_w(act, jnp.concatenate([dz1(k) for k in range(RD)], axis=0))
            for i in range(8):
                bits = batch_bits(i // 4, lax.rem(j, 2), lax.div(j, 2), i // 2 % 2)
                put(stage, REDUCE, i % 2, bits, 0, res[i * n : (i + 1) * n])

        loop(4, body)

    rs_step(SPATIAL, SQUEEZE, MIXING, EXPAND, SHORTCUT)
    staged(REDUCE, fill_reduce)
    rs_step(SPATIAL, SQUEEZE, MIXING, EXPAND, SHORTCUT)

    def input_grad(j):
        cols = aligned(j, CIN // 4)
        w = R.f0[aligned(j, CIN // 4), :]
        ch = jnp.concatenate(
            [keep(j * (CIN // 4 // LANES) + i, float(CIN // MID)) for i in range(CIN // 4 // LANES)],
            axis=1,
        )
        for k in range(RD):
            y = dot_t(dz1(k), w)
            for c in range(0, CIN // 4, LANES):
                base = c // LANES * 2 * S
                for p in range(2):
                    v = y[out_rows(p), c : c + LANES]
                    if p == 0 and k % 2 == 0:
                        v = v + R.z6[out_rows(k // 2), pl.ds(pl.multiple_of(j * (CIN // 4) + c, LANES), LANES)]
                    v = v * (ch[:, c : c + LANES] * R.pix_in[k, out_rows(p), :])
                    R.weave[pl.ds(base + p, S, stride=2), :] = v
                at = pl.ds(pl.multiple_of(k % 2 * CIN + j * (CIN // 4) + c, LANES), LANES)
                woven = R.weave[base : base + 2 * S, :]
                (R.du2, R.du1)[k // 2][:, :, at] = woven.reshape(M // 16, 16, LANES)

    loop(4, input_grad)
    gin_copies = [
        pltpu.make_async_copy(
            (R.du2, R.du1)[k // 2].at[pl.ds(0, images), :, pl.ds(k % 2 * CIN, CIN)], R.gin.at[:, k], R.gn.at[k]
        )
        for k in range(RD)
    ]
    for c in gin_copies:
        c.start()
    rs_end()

    for out, src in ((R.gn1, R.g1), (R.gn2, R.g2), (R.gn4, R.g4), (R.gn5, R.g5)):
        for h in range(2):
            for i in range(2):
                out[i, :, h * (MID // 2) : (h + 1) * (MID // 2)] = src[h, 3 * i : 3 * i + 3, :]
    for out, src, rows in ((R.gn3, R.g3, (0, 3)), (R.gns, R.g3, (8, 3)), (R.gn6, R.g6, (0, 3))):
        for h in range(4):
            for i in range(2):
                out[i, :, h * (WIDE // 4) : (h + 1) * (WIDE // 4)] = src[h, rows[i] : rows[i] + 3, :]

    for o in range(OD):
        mixed_copy(0, o).wait()
        mixed_copy(1, o).wait_send()
        mixed_copy(2, o).wait()
        mixed_copy(3, o).wait()
    for c in gin_copies:
        c.wait()


def plan(features, w_reduce, w_expand, batch):
    images, rd, _, cin = features.shape
    mid, wide = w_reduce.shape[1], w_expand.shape[1]
    cfg = SimpleNamespace(
        images=images,
        members=images * batch // 3,
        slots=-(-images * 8 // 16) * 16, in_rows=rd, out_rows=rd // 2, batch=batch, mid=mid, wide=wide, cin=cin
    )
    flat = {
        REDUCE: cin,
        SPATIAL: 9 * mid,
        EXPAND: mid * wide // 512,
        SHORTCUT: cin * wide // 512,
        SQUEEZE: wide,
        MIXING: 9 * mid,
        WIDEN: mid * wide // 512,
    }
    pieces = {SPATIAL: 3, MIXING: 3, SHORTCUT: 2}
    cfg.units = []
    for name, n in flat.items():
        k = pieces.get(name, 1)
        cfg.units += [(name, i * n // 4 // k, n // 4 // k) for i in range(k)]
    cfg.flat = flat
    cfg.rows = {name: n // 32 for name, n in flat.items()}
    cfg.reduce = batch == 8
    orders = ((DX, DY, DN, DF), (DY, DX, DN, DF), (DN, DF, DX, DY))
    thirds = {WIDEN: 1, SQUEEZE: 0, EXPAND: 2}
    cfg.parts = {}
    for name, n in cfg.rows.items():
        if not cfg.reduce:
            cfg.parts[name] = [(0, n, (DF, DN, DY, DX))]
            continue
        tiles = [n // 16 // 3] * 3
        for i in range(n // 16 - sum(tiles)):
            tiles[(thirds.get(name, 0) + i) % 3] += 1
        cfg.parts[name], n0 = [], 0
        for tile, order in zip(tiles, orders):
            if tile:
                cfg.parts[name].append((n0, 16 * tile, order))
                n0 += 16 * tile
    cfg.own_landing = (REDUCE, SPATIAL, SHORTCUT)
    cfg.offs, total = {}, 0
    for name, n in cfg.rows.items():
        cfg.offs[name] = total
        total += n
    cfg.total = total
    return cfg


def run_blocks(cfg, smem_args, vmem_args, hbm_args):
    S, RD, OD, NB = cfg.slots, cfg.in_rows, cfg.out_rows, cfg.batch
    MID, WIDE, CIN = cfg.mid, cfg.wide, cfg.cin
    M = OD * S
    U = len(cfg.units)
    vmem = pl.BlockSpec(memory_space=pltpu.VMEM)
    hbm = pl.BlockSpec(memory_space=pl.ANY)
    sds = jax.ShapeDtypeStruct
    outs = dict(
        mixed=(sds((cfg.images, 4 * OD, 8, WIDE), BF), hbm),
        gin=(sds((cfg.images, RD, 16, CIN), F32), hbm),
        gn1=(sds((2, 3, MID), F32), vmem),
        gn2=(sds((2, 3, MID), F32), vmem),
        gn3=(sds((2, 3, WIDE), F32), vmem),
        gns=(sds((2, 3, WIDE), F32), vmem),
        gn4=(sds((2, 3, MID), F32), vmem),
        gn5=(sds((2, 3, MID), F32), vmem),
        gn6=(sds((2, 3, WIDE), F32), vmem),
    )
    final = {}
    if cfg.reduce:
        for w, n in cfg.rows.items():
            final[w] = (9, n // 9, 512) if w in (SPATIAL, MIXING) else (n, 512)
            shape = (n, 2048) if w in (EXPAND, SHORTCUT, WIDEN) else final[w][:-2] + (4 * final[w][-2], 512)
            outs["o" + str(w)] = (sds(shape, BF), hbm)
    else:
        outs.update(grads=(sds((32 * cfg.total, 512), BF), hbm))
    V = pltpu.VMEM
    mid_tot = V((2, 8, MID // 2), F32)
    scratch = dict(
        z1=V((RD, 2 * S, MID), F32),
        win1=V((M, 9 * MID), BF),
        h1s=V((2, S, MID), BF),
        h1r=V((2, S, MID), BF),
        z2=V((M, MID), F32),
        h2=V((M, MID), BF),
        z3=V((M, WIDE), F32),
        zs=V((M, WIDE), F32),
        y1=V((M, WIDE), BF),
        z4=V((M, MID), F32),
        h4=V((OD + 2, S, MID), BF),
        win4=V((M, 9 * MID), BF),
        z5=V((M, MID), F32),
        h5=V((M, MID), BF),
        z6=V((M, WIDE), F32),
        mixed_local=V((OD, S // 8, 8, WIDE), BF),
        du2=V((M // 16, 16, WIDE), F32),
        dz6=V((M, WIDE), BF),
        dh=V((M, MID), F32),
        d5=V((OD + 2, S, MID), BF),
        win5=V((M, 9 * MID), BF),
        dz4=V((M, MID), BF),
        du1=V((M // 16, 16, WIDE), F32),
        dzs=V((M, WIDE), BF),
        d2=V((OD + 1, S, MID), BF),
        d2l=V((OD + 1, S, MID), BF),
        stage0=V((32 * cfg.rows[MIXING], 512), BF),
        stage1=V((32 * cfg.rows[SHORTCUT], 512), BF),
        loc=mid_tot,
        locw=V((4, 8, WIDE // 4), F32),
        locw2=V((4, 16, WIDE // 4), F32),
        t1=mid_tot,
        t2=mid_tot,
        t3=V((4, 16, WIDE // 4), F32),
        t4=mid_tot,
        t5=mid_tot,
        t6=V((4, 8, WIDE // 4), F32),
        g1=mid_tot,
        g2=mid_tot,
        g3=V((4, 16, WIDE // 4), F32),
        g4=mid_tot,
        g5=mid_tot,
        g6=V((4, 8, WIDE // 4), F32),
        rc=V((2, 8, MID // 2), F32),
        rq=V((2, 2 * NB, 8, MID // 2), F32),
        rw=V((2, 4, 16, WIDE // 4), F32),
        wb=V((2, NB, 16, WIDE // 4), F32),
        wsend=pltpu.SemaphoreType.DMA((U, 5)),
        wrecv=pltpu.SemaphoreType.DMA((U, 5)),
        wloc=pltpu.SemaphoreType.DMA((7, 4)),
        ms=pltpu.SemaphoreType.DMA((3,)),
        mr=pltpu.SemaphoreType.DMA((3, 2)),
        ws=pltpu.SemaphoreType.DMA((4, 3)),
        wr=pltpu.SemaphoreType.DMA((4, 3)),
        hs=pltpu.SemaphoreType.DMA((2,)),
        hr=pltpu.SemaphoreType.DMA((2,)),
        es=pltpu.SemaphoreType.DMA((2, 2)),
        er=pltpu.SemaphoreType.DMA((2, 2)),
        xs=pltpu.SemaphoreType.DMA((3, OD)),
        xr=pltpu.SemaphoreType.DMA((3, OD)),
        xl=pltpu.SemaphoreType.DMA((OD,)),
        gs=pltpu.SemaphoreType.DMA((2,)),
        gn=pltpu.SemaphoreType.DMA((RD,)),
        rs=pltpu.SemaphoreType.DMA((7, 3, 5)),
        rr=pltpu.SemaphoreType.DMA((7, 3, 5)),
        fs=pltpu.SemaphoreType.DMA((7, 3)),
        fr=pltpu.SemaphoreType.DMA((7, 3)),
        fl=pltpu.SemaphoreType.DMA((7,)),
        x0=V((RD, 2 * S, CIN), BF),
        weave=V((4 * S, LANES), F32),
        ct=V((M, WIDE), BF),
        onehot=V((3, S, LANES), F32),
        active_slot=V((S, LANES), F32),
        pix_in=V((RD, 2 * S, LANES), F32),
        pix_out=V((M, LANES), F32),
        ld=pltpu.SemaphoreType.DMA((2,)),
    )
    scratch.update({"f" + str(name): V((n, 512), BF) for name, n in cfg.flat.items()})
    scratch.update({"l" + str(name): V((cfg.flat[name], 512), BF) for name in cfg.own_landing if cfg.reduce})
    scratch.update({"e" + str(w): V(shape, BF) for w, shape in final.items()})
    names = list(smem_args) + list(vmem_args) + list(hbm_args) + list(outs) + list(scratch)
    smem = pl.BlockSpec(memory_space=pltpu.SMEM)
    res = pl.pallas_call(
        functools.partial(block_kernel, names, cfg),
        out_shape=[o[0] for o in outs.values()],
        in_specs=[smem] * len(smem_args) + [vmem] * len(vmem_args) + [hbm] * len(hbm_args),
        out_specs=[o[1] for o in outs.values()],
        scratch_shapes=list(scratch.values()),
        compiler_params=pltpu.CompilerParams(
            collective_id=0, has_side_effects=True, vmem_limit_bytes=63 * 2**20
        ),
    )(*smem_args.values(), *vmem_args.values(), *hbm_args.values())
    return SimpleNamespace(**dict(zip(outs, res)))


def slot_layout(x, slots):
    images, rows, cols, channels = x.shape
    x = jnp.transpose(x, (1, 0, 2, 3)).reshape(rows, images * cols, channels)
    return jnp.pad(x, ((0, 0), (0, slots - images * cols), (0, 0)))


def per_device(
    features, w_reduce, w_spatial, w_expand, w_shortcut, w_squeeze, w_mixing, w_widen,
    norm_reduce, norm_spatial, norm_expand, norm_shortcut, norm_squeeze, norm_mixing, norm_widen,
    cotangent, resolution, active,
):
    images, rd, cols_in, cin = features.shape
    od = rd // 2
    nb = lax.axis_size("batch")
    cfg = plan(features, w_reduce, w_expand, nb)
    S, mid, wide = cfg.slots, cfg.mid, cfg.wide
    x = jnp.pad(features, ((0, 0), (0, 0), (0, 16 - cols_in), (0, 0)))
    x = x.reshape(images, rd, 8, 2, cin)
    x = jnp.transpose(x, (1, 3, 0, 2, 4)).reshape(rd, 2, images * 8, cin)
    x = jnp.pad(x, ((0, 0), (0, 0), (0, S - images * 8), (0, 0))).reshape(rd, 2 * S, cin)
    out_cols = cotangent.shape[2]
    ct = slot_layout(jnp.pad(cotangent, ((0, 0), (0, 0), (0, 8 - out_cols), (0, 0))), S)
    res = run_blocks(
        cfg,
        dict(resolution=resolution, active=active),
        dict(
            norm_reduce=norm_reduce,
            norm_spatial=norm_spatial,
            norm_expand=norm_expand,
            norm_shortcut=norm_shortcut,
            norm_squeeze=norm_squeeze,
            norm_mixing=norm_mixing,
            norm_widen=norm_widen,
        ),
        dict(
            features=x,
            cotangent=ct.reshape(od * S, wide),
            w0=w_reduce,
            w1=w_spatial.reshape(-1, mid),
            w2=w_expand,
            w3=w_shortcut,
            w4=w_squeeze,
            w5=w_mixing.reshape(-1, mid),
            w6=w_widen,
        ),
    )
    mixed = res.mixed[:, :, :out_cols]
    gin = res.gin[:, :, :cols_in]

    def unpack(g, name):
        b8, _, n, _ = g.shape
        if name in (SPATIAL, MIXING):
            k = n // 9
            return jnp.transpose(g.reshape(b8, 4, 9, k, 512), (2, 0, 1, 3, 4)).reshape(3, 3, b8 * 4 * k, 512)
        if name in (EXPAND, SHORTCUT, WIDEN):
            return jnp.transpose(g, (0, 2, 1, 3)).reshape(b8 * n, 2048)
        return g.reshape(b8 * 4 * n, 512)

    totals = []
    for name, n in cfg.rows.items():
        if cfg.reduce:
            g = getattr(res, "o" + str(name)).astype(F32)
            totals.append(g.reshape((3, 3) + g.shape[1:]) if g.ndim == 3 else g)
            continue
        at = cfg.offs[name]
        part = res.grads[32 * at : 32 * (at + n)].reshape(2, 8, 2, n, 512)
        part = unpack(jnp.transpose(part, (1, 2, 0, 3, 4)).reshape(8, 4, n, 512), name)
        dim = 2 if part.ndim == 4 else 0
        part = lax.psum_scatter(part, "batch", scatter_dimension=dim, tiled=True)
        totals.append(lax.psum(part, "rows").astype(F32))

    return (mixed, gin, *totals, res.gn1, res.gn2, res.gn3, res.gns, res.gn4, res.gn5, res.gn6)


def solution(mesh):
    w2, w4 = P("rows", None), P(None, None, "rows", None)
    o2, o4 = P("batch", None), P(None, None, "batch", None)
    return jax.shard_map(
        per_device,
        mesh=mesh,
        in_specs=(P("batch", "rows", None, None), w2, w4, w2, w2, w2, w4, w2)
        + (P(),) * 7
        + (P("batch", "rows", None, None), P(), P()),
        out_specs=(P("batch", None, None, None), P("batch", "rows", None, None), o2, o4, o2, o2, o2, o4, o2)
        + (P(),) * 7,
        check_vma=False,
    )
```

time: 895 us -> 317 us (0.35)
  waiting for transfers between devices: 582 us -> 0 us
  Pallas kernels: 216 us -> 288 us
  local copies, waits for them, and re-layouts: 67.2 us -> 21.3 us
  between operations: 14.6 us -> 0.82 us
    reduce_scatter x6 -> x0, waiting for transfers between devices: 473 us -> none  [per_device(): part = lax.psum_scatter(part, 'batch', scatter_dimension=dim, tiled=True)]
    pallas_call x1, Pallas kernels: 216 us -> 288 us  [run_blocks(): pl.pallas_call(functools.partial(block_kernel, names, cfg), out_shape=[o[...]
    unnamed x9 -> x0, waiting for transfers between devices: 57.2 us -> none
    psum x1 -> x0, waiting for transfers between devices: 52.2 us -> none  [per_device(): totals.append(lax.psum(part, 'rows').astype(F32))]
    transpose x6 -> x0, local copies, waits for them, and re-layouts: 18.7 us -> none  [the longest x4 10.6 us: unpack(): return jnp.transpose(g, (0, 2, 1, 3)).reshape(b8 * n, 2048)]
    slice x15 -> x0, local copies, waits for them, and re-layouts: 13.5 us -> none  [the longest x2 9.04 us: unpack(): g = grads[:, :, cfg.offs[name]:cfg.offs[name] + cfg.rows[name]]]
    unnamed x60 -> x62, local copies, waits for them, and re-layouts: 19.4 us -> 16.2 us
  transfers between devices with their start and end apart: 8 -> 0, of which waited for: 8 -> 0; matrix products, arithmetic and copies ran while one was open for 5% -> 0% of each run, Pallas kernels for 0% -> 0%
where the time goes in v2:
time: 317 us; the launch traced here: 316 us
  Pallas kernels  288 us (91%)
  local copies, waits for them, and re-layouts  21.3 us (7%)
  other arithmetic  6.64 us (2%)
    pallas_call x1, Pallas kernels, run_blocks(): pl.pallas_call(functools.partial(block_kernel, names, cfg), out_shape=[o[...  288 us
    unnamed x62, local copies, waits for them, and re-layouts  16.2 us

profile of v2, /device:TPU:0, one launch (start us, length us, event | category | flops | bytes accessed | tf_op | source)
XLA Modules:
  0.0 316.4 jit_solution(1707718141833702927)
XLA Ops:
  0.6 1.7 pad.16
  2.4 0.7 copy.53
  3.0 1.2 pad.17
  5.0 0.9 pad.19
  5.9 0.7 copy.38.refs_4_
  6.6 0.7 copy.39.refs_5_
  7.2 0.7 copy.42.refs_8_
  7.9 0.6 copy.36.refs_2_
  8.5 0.6 copy.37.refs_3_
  9.1 0.6 copy.40.refs_6_
  9.7 0.6 copy.41.refs_7_
  10.4 287.6 %shard_map.297 = (bf16[9,8,8,2048]{3,2,1,0:T(8,128)(2,1)}, f32[9,4,16,1024]{3,2,1,0:T(8,128)}, f32[2,3,512]{2,1,0:T(4,128)}, f32[2,3,512]{2,1,0:T(4,128)}, f32[2...) custom-call(s32[72]{0:T(128)} %refs_0_.1, ...), custom_call_target="tpu_custom_call" | custom-call | tf_op jit(solution)/shard_map/pallas_call | solution.py:1365
  298.0 4.6 %copy.43 = bf16[9,8,7,2048]{3,1,2,0:T(8,128)(2,1)} copy(bf16[9,8,7,2048]{3,2,1,0:T(8,128)(2,1)} %bitcast.24) | data formatting | bytes 4128768
  302.6 2.7 copy.44
  305.2 1.2 convert.2
  306.4 1.2 convert.3
  307.6 1.1 convert_element_type.27
  308.7 0.8 convert_element_type.26
  309.5 0.9 convert_element_type.28
  310.4 0.8 convert_element_type.29
  311.2 0.7 convert_element_type.25
  312.0 0.7 copy.47
  312.6 0.7 copy.48
  313.3 0.7 copy.51
  (52 shorter events, 3.2 us)
Async XLA Ops:
  3.0 1.2 copy-start.4
  4.7 1.2 copy-start.12
  4.7 1.8 copy-start.13
  4.7 2.5 copy-start.14
  4.8 3.2 copy-start.19
  4.8 3.8 %copy-start.20 = (f32[2,3,512]{2,0,1:T(2,128)S(1)}, f32[2,3,512]{2,0,1:T(2,128)}, u32[]{:S(2)}) copy-start(f32[2,3,512]{2,0,1:T(2,128)} %param.27) | copy-start | bytes 36868
  4.8 4.4 %copy-start.21 = (f32[2,3,512]{2,0,1:T(2,128)S(1)}, f32[2,3,512]{2,0,1:T(2,128)}, u32[]{:S(2)}) copy-start(f32[2,3,512]{2,0,1:T(2,128)} %param.30) | copy-start | bytes 36868
  4.8 5.0 %copy-start.22 = (f32[2,3,512]{2,0,1:T(2,128)S(1)}, f32[2,3,512]{2,0,1:T(2,128)}, u32[]{:S(2)}) copy-start(f32[2,3,512]{2,0,1:T(2,128)} %param.31) | copy-start | bytes 36868
  298.0 4.6 %copy-start = (f32[9,4,16,1024]{3,2,1,0:T(8,128)S(1)}, f32[9,4,16,1024]{3,2,1,0:T(8,128)}, u32[]{:S(2)}) copy-start(f32[9,4,16,1024]{3,2,1,0:T(8,128)} %get-tuple-element.33) | copy-start | bytes 7077892
  302.6 2.7 copy-start.2
  305.2 1.2 copy-start.1
  306.4 1.2 copy-start.3
  307.6 1.1 copy-start.7
  307.6 1.9 copy-start.6
  308.7 1.7 copy-start.5
  308.7 2.6 copy-start.8
  309.5 2.5 copy-start.11
  309.5 3.1 copy-start.10
  309.5 3.8 %copy-start.9 = (f32[2,3,2048]{2,1,0:T(4,128)S(1)}, f32[2,3,2048]{2,1,0:T(4,128)}, u32[]{:S(2)}) copy-start(f32[2,3,2048]{2,1,0:T(4,128)} %get-tuple-element.63) | copy-start | bytes 147460
  309.5 4.5 %copy-start.18 = (f32[2,3,512]{2,1,0:T(4,128)S(1)}, f32[2,3,512]{2,1,0:T(4,128)}, u32[]{:S(2)}) copy-start(f32[2,3,512]{2,1,0:T(4,128)} %get-tuple-element.57) | copy-start | bytes 36868
  309.5 5.1 %copy-start.17 = (f32[2,3,512]{2,1,0:T(4,128)S(1)}, f32[2,3,512]{2,1,0:T(4,128)}, u32[]{:S(2)}) copy-start(f32[2,3,512]{2,1,0:T(4,128)} %get-tuple-element.58) | copy-start | bytes 36868
  309.5 5.6 %copy-start.16 = (f32[2,3,512]{2,1,0:T(4,128)S(1)}, f32[2,3,512]{2,1,0:T(4,128)}, u32[]{:S(2)}) copy-start(f32[2,3,512]{2,1,0:T(4,128)} %get-tuple-element.61) | copy-start | bytes 36868
  309.5 6.2 %copy-start.15 = (f32[2,3,512]{2,1,0:T(4,128)S(1)}, f32[2,3,512]{2,1,0:T(4,128)}, u32[]{:S(2)}) copy-start(f32[2,3,512]{2,1,0:T(4,128)} %get-tuple-element.62) | copy-start | bytes 36868

commit v3 on v2

--- a/solution.py
+++ b/solution.py
@@ -39,6 +39,14 @@
         return carry
 
     lax.fori_loop(0, count, step, 0)
+
+
+def each(count, body):
+    if count > 16:
+        loop(count, body)
+        return
+    for i in range(count):
+        body(i)
 
 
 def silu_parts(u):
@@ -64,9 +72,14 @@
     x_row = lax.rem(r + 2, 4)
     diag = 3 - r
     half = lax.rem(b, 2)
-    y_b = b + 1 - 2 * half
 
     def flip(i, j):
+        if isinstance(j, int):
+            out = i
+            for bit in range((2 * NB - 1).bit_length()):
+                if j >> bit & 1:
+                    out = out + (1 << bit) * (1 - 2 * lax.rem(lax.div(i, 1 << bit), 2))
+            return out
         out = jnp.int32(0)
         bit = 1
         while bit < 2 * NB:
@@ -87,24 +100,38 @@
 
     units = cfg.units
     wsend, wrecv, wloc = R.wsend, R.wrecv, R.wloc
-
-    def wview(u, shard, part):
-        w, k0, kn = units[u]
-        start, size = k0, kn
-        if part is not None:
-            size = kn // 2
-            start = k0 + part * size
+    near = lax.rem(lax.div(b, 2), 2)
+    sides = ((half, (b + 1 - 2 * half, r)), (near, (b + 2 - 4 * near, r)))
+
+    def wview(u, shard, at, fourths):
+        w, k0, kn, _ = units[u]
         full = getattr(R, "f" + str(w))
-        return full.at[pl.ds(pl.multiple_of(shard * (full.shape[0] // 4) + start, 16), size)]
+        start = shard * (full.shape[0] // 4) + k0 + at * (kn // 4)
+        return full.at[pl.ds(pl.multiple_of(start, 16), fourths * kn // 4)]
 
     def w_copy(u, i):
-        if i < 2:
-            view = wview(u, r, None if i == 0 else half)
-            dev = (b, core_peer) if i == 0 else (b, x_row)
-        else:
-            view = wview(u, x_row, 1 - half if i == 4 else half)
-            dev = (y_b, r) if i == 3 else (b, core_peer)
+        mode = units[u][3]
+        first, second = sides if mode == 1 else sides[::-1]
+        quarter = x_row if i > 1 else r
+        at, fourths, dev = 0, 4, (b, core_peer)
+        if i == 1:
+            dev = (b, x_row)
+        if mode and i > 0:
+            fourths = 2 if i > 4 else 1
+            at = 2 * second[0] + first[0]
+            if i == 3:
+                dev = first[1]
+            elif i == 4:
+                at = at + 1 - 2 * first[0]
+            elif i == 5:
+                at, dev = 2 * second[0], second[1]
+            elif i == 6:
+                at = 2 - 2 * second[0]
+        view = wview(u, quarter, at, fourths)
         return remote(view, view, wsend.at[u, i], wrecv.at[u, i], dev)
+
+    def w_stages(u):
+        return range(7) if units[u][3] else range(3)
 
     def w_local(w):
         src, full = getattr(R, "w" + str(w)), getattr(R, "f" + str(w))
@@ -118,6 +145,15 @@
             for i in range(src.shape[1] // 512)
         ]
 
+    bar = pltpu.get_barrier_semaphore()
+    for dev in ((b, core_peer), (b, diag)):
+        pl.semaphore_signal(bar, inc=1, device_id=dev, device_id_type=MESH)
+
+    def greet(j):
+        pl.semaphore_signal(bar, inc=1, device_id=team(flip(me, j + 1)), device_id_type=MESH)
+
+    loop(2 * NB - 1, greet)
+
     loaded = [w_local(w) for w in range(7)]
     for w in range(7):
         for c in loaded[w]:
@@ -125,8 +161,13 @@
         if w == 0:
             x0_load = pltpu.make_async_copy(R.features, R.x0, R.ld.at[0])
             x0_load.start()
+    norm_load = pltpu.make_async_copy(R.norms, R.norm_values, R.ld.at[2])
+    norm_load.start()
     ct_load = pltpu.make_async_copy(R.cotangent, R.ct, R.ld.at[1])
     ct_load.start()
+    norm_reduce, norm_spatial, norm_squeeze, norm_mixing, norm_expand, norm_shortcut, norm_widen = [
+        R.norm_values.at[:, :, pl.ds(at, width)] for at, width in cfg.norm_columns
+    ]
     at_home = set()
 
     images = cfg.images
@@ -161,14 +202,6 @@
             for p in range(2):
                 R.pix_in[k, p * S + 8 * i : p * S + 8 * i + 8, :] = jnp.where(2.0 * column + p < inside, 1.0, 0.0)
 
-    bar = pltpu.get_barrier_semaphore()
-    for dev in ((b, core_peer), (b, diag)):
-        pl.semaphore_signal(bar, inc=1, device_id=dev, device_id_type=MESH)
-
-    def greet(j):
-        pl.semaphore_signal(bar, inc=1, device_id=team(flip(me, j + 1)), device_id_type=MESH)
-
-    loop(2 * NB - 1, greet)
     pl.semaphore_wait(bar, 2 * NB + 1)
 
     def w_start(u):
@@ -182,35 +215,39 @@
 
     def w_second(u):
         w_copy(u, 1).wait_recv()
-        w_copy(u, 3).start()
+        if units[u][3]:
+            w_copy(u, 3).start()
         w_copy(u, 2).start()
 
     def w_third(u):
-        w_copy(u, 3).wait_recv()
-        w_copy(u, 4).start()
+        if units[u][3]:
+            w_copy(u, 3).wait_recv()
+            w_copy(u, 5).start()
+            w_copy(u, 4).start()
+
+    def w_fourth(u):
+        if units[u][3]:
+            w_copy(u, 5).wait_recv()
+            w_copy(u, 6).start()
 
     def w_ready(u):
-        for i in (0, 2, 4):
+        for i in w_stages(u)[::2]:
             w_copy(u, i).wait_recv()
 
     pumped = [0]
+    lags = cfg.lags
 
     def pump(steps):
         for _ in range(steps):
             n = pumped[0]
-            if n >= len(units) + 2:
-                return
-            if n < len(units):
-                w_start(n)
-            if 0 <= n - 1 < len(units):
-                w_second(n - 1)
-            if 0 <= n - 2 < len(units):
-                w_third(n - 2)
+            for lag, stage in zip(lags, (w_start, w_second, w_third, w_fourth)):
+                if 0 <= n - lag < len(units):
+                    stage(n - lag)
             pumped[0] = n + 1
 
     def need(name):
         last = max(u for u in range(len(units)) if units[u][0] == name)
-        while pumped[0] < last + 3:
+        while pumped[0] < last + lags[3 if units[last][3] else 1] + 1:
             pump(1)
         for u in range(len(units)):
             if units[u][0] == name:
@@ -225,14 +262,14 @@
 
         def send(j):
             to = team(flip(me, j + 1))
-            remote(R.rq.at[p, me], R.rq.at[p, me], R.ms.at[1], R.mr.at[1, p], to).start()
-
-        loop(2 * NB - 1, send)
+            remote(R.rq.at[p, me, pl.ds(0, 6)], R.rq.at[p, me, pl.ds(0, 6)], R.ms.at[1], R.mr.at[1, p], to).start()
+
+        each(2 * NB - 1, send)
         swap.wait_send()
 
     def mid_finish(k, tot):
         p = k % 2
-        rest = R.rq.at[p, pl.ds(0, 2 * NB - 1)]
+        rest = R.rq.at[p, pl.ds(0, 2 * NB - 1), pl.ds(0, 6)]
         every = remote(rest, rest, R.ms.at[1], R.mr.at[1, p], (b, x_row))
         every.wait_recv()
         total = R.rq[p, 0]
@@ -258,7 +295,7 @@
             to = lax.rem(b + j + 1, NB)
             remote(wb.at[b], wb.at[b], R.ws.at[k, 1], R.wr.at[k, 1], (to, r)).start()
 
-        loop(NB - 1, send)
+        each(NB - 1, send)
         three.wait_send()
 
     def wide_finish(k, tot):
@@ -308,8 +345,8 @@
 
     def forward_terms(sums, params, cols, inv_n, row=0):
         means, invs = moments(sums, inv_n, row)
-        scales = [invs[g] * params[0, g : g + 1, cols] for g in range(3)]
-        shifts = [params[1, g : g + 1, cols] - means[g] * scales[g] for g in range(3)]
+        scales = [invs[g] * params[g, 0:1, cols] for g in range(3)]
+        shifts = [params[g, 1:2, cols] - means[g] * scales[g] for g in range(3)]
         return spread(scales), spread(shifts)
 
     def xhat_terms(sums, inv_n, row=0):
@@ -321,7 +358,7 @@
         fs, az, bz = [], [], []
         for g in range(3):
             n = 1.0 / inv_n[g]
-            f = invs[g] * params[0, g : g + 1, cols]
+            f = invs[g] * params[g, 0:1, cols]
             gain = grads[g0 + g : g0 + g + 1, :] * n * invs[g]
             bias = grads[g1 + g : g1 + g + 1, :] * n
             fs.append(f)
@@ -418,8 +455,8 @@
             down.wait_recv()
             up.wait_send()
 
-    pump(3)
     x0_load.wait()
+    norm_load.wait()
     need(REDUCE)
 
     def z1_rows(k):
@@ -452,14 +489,14 @@
 
     loop(MID // LANES, z1_stats)
     mid_start(0)
-    pump(1)
+    pump(cfg.pumps[0])
     mid_finish(0, R.t1)
 
     last = RD - 1
 
     def h1_body(j):
         cols = aligned(j, LANES)
-        sc, sh = forward_terms(mid_at(R.t1, j), R.norm_reduce, cols, IN)
+        sc, sh = forward_terms(mid_at(R.t1, j), norm_reduce, cols, IN)
         ch = keep(j, 1.0)
         for k in range(RD - 1, -1, -1):
             for p in range(2):
@@ -484,7 +521,7 @@
     def _():
         down.start()
 
-    pump(1)
+    pump(cfg.pumps[1])
 
     @pl.when(r > 0)
     def _():
@@ -519,7 +556,7 @@
     conv(R.win1, R.f1, R.z2)
     forward_stats(R.z2, lambda j: mid_at(R.loc, j))
     mid_start(1)
-    pump(1)
+    pump(cfg.pumps[2])
     mid_finish(1, R.t2)
 
     def activate(z, tot, params, dest):
@@ -536,7 +573,7 @@
     def to_h2(o, cols, v):
         R.h2[out_rows(o), cols] = v
 
-    activate(R.z2, R.t2, R.norm_spatial, to_h2)
+    activate(R.z2, R.t2, norm_spatial, to_h2)
     need(EXPAND)
 
     def piece(weight, shard, j):
@@ -565,14 +602,14 @@
     forward_stats(R.z3, lambda j: wide_at(R.locw2, j), 0)
     forward_stats(R.zs, lambda j: wide_at(R.locw2, j), 8)
     wide_start(0, R.locw2)
-    pump(2)
+    pump(cfg.pumps[3])
     wide_finish(0, R.t3)
 
     def u1_terms(j):
         cols = aligned(j, LANES)
         tot = wide_at(R.t3, j)
-        sc3, sh3 = forward_terms(tot, R.norm_expand, cols, OUT, 0)
-        scs, shs = forward_terms(tot, R.norm_shortcut, cols, OUT, 8)
+        sc3, sh3 = forward_terms(tot, norm_expand, cols, OUT, 0)
+        scs, shs = forward_terms(tot, norm_shortcut, cols, OUT, 8)
         shift = sh3 + shs
 
         def u1(o):
@@ -598,15 +635,15 @@
     loop(MID // 256, squeeze_body)
     forward_stats(R.z4, lambda j: mid_at(R.loc, j))
     mid_start(2)
-    pump(2)
+    pump(cfg.pumps[4])
     mid_finish(2, R.t4)
 
     def to_h4(o, cols, v):
         R.h4[o + 1, :, cols] = v
 
-    activate(R.z4, R.t4, R.norm_squeeze, to_h4)
+    activate(R.z4, R.t4, norm_squeeze, to_h4)
     pair = edge_exchange(R.h4, 0)
-    pump(1)
+    pump(cfg.pumps[5])
     unit_windows(R.h4, R.win4, range(1, OD + 1), False)
     edge_wait(pair)
     unit_windows(R.h4, R.win4, (0, OD + 1), False)
@@ -614,26 +651,26 @@
     conv(R.win4, R.f5, R.z5)
     forward_stats(R.z5, lambda j: mid_at(R.loc, j))
     mid_start(3)
-    pump(20)
+    pump(cfg.pumps[6])
     mid_finish(3, R.t5)
 
     def to_h5(o, cols, v):
         R.h5[out_rows(o), cols] = v
 
-    activate(R.z5, R.t5, R.norm_mixing, to_h5)
+    activate(R.z5, R.t5, norm_mixing, to_h5)
     need(WIDEN)
     expand_to(R.h5, R.f6, R.z6)
     forward_stats(R.z6, lambda j: wide_at(R.locw, j))
     wide_start(1, R.locw)
     wide_finish(1, R.t6)
     for u in range(len(units)):
-        for i in range(5):
+        for i in w_stages(u):
             w_copy(u, i).wait_send()
 
     def u2_body(j):
         cols = aligned(j, LANES)
         tot = wide_at(R.t6, j)
-        sc, sh = forward_terms(tot, R.norm_widen, cols, OUT)
+        sc, sh = forward_terms(tot, norm_widen, cols, OUT)
         xa, xs = xhat_terms(tot, OUT)
         ch = keep(j, float(WIDE // MID))
         g0 = jnp.zeros((S, LANES), F32)
@@ -665,13 +702,13 @@
         return remote(src, dst, R.xs.at[i, o], R.xr.at[i, o], (b, x_row if i == 1 else core_peer))
 
     for o in range(OD):
-        for i in (1, 0, 3):
+        for i in (0, 3):
             mixed_copy(i, o).start()
     wide_finish(2, R.g6)
 
     def widen_back(j):
         cols = aligned(j, LANES)
-        f, a, bz = backward_terms(wide_at(R.t6, j), wide_at(R.g6, j), R.norm_widen, cols, OUT)
+        f, a, bz = backward_terms(wide_at(R.t6, j), wide_at(R.g6, j), norm_widen, cols, OUT)
         for o in range(OD):
             d = f * R.du2[groups16(o), :, cols].reshape(S, LANES) - a - R.z6[out_rows(o), cols] * bz
             R.dz6[out_rows(o), cols] = (d * R.pix_out[out_rows(o), :]).astype(BF)
@@ -802,6 +839,8 @@
             return
         for w in kernels:
             stage, step = begun[w]
+            if step > 5:
+                continue
             if step == 5:
                 fin_copy(w, 1).wait_recv()
                 fin_copy(w, 2).start()
@@ -818,17 +857,17 @@
                         fin_copy(w, i).start()
             begun[w] = (stage, step + 1)
 
+    def rs_round():
+        if cfg.reduce:
+            rs_step(*[w for w in reversed(list(begun)) if begun[w][1] < 6])
+
     def rs_end():
         if not cfg.reduce:
             for copy in begun.values():
                 copy.wait()
             return
-        left = True
-        while left:
-            left = [w for w in cfg.rows if begun[w][1] < 6]
-            if left:
-                low = min(begun[w][1] for w in left)
-                rs_step(*[w for w in left if begun[w][1] == low])
+        while any(begun[w][1] < 6 for w in begun):
+            rs_round()
         for w in cfg.rows:
             fin_copy(w, 0).wait()
             fin_copy(w, 1).wait_send()
@@ -916,15 +955,16 @@
         )
 
     reduce_back(R.dz6, R.f6, R.dh)
-    mid_back_sums(R.dh, R.z5, R.t5, R.norm_mixing)
+    mid_back_sums(R.dh, R.z5, R.t5, norm_mixing)
     mid_start(4)
+    mixed_copy(1, 0).start()
     staged(WIDEN, fill_out(WIDEN, lambda: R.h5[...], R.dz6))
     mid_finish(4, R.g5)
 
     def to_d5(o, cols, v):
         R.d5[o + 1, :, cols] = v
 
-    mid_back_apply(R.dh, R.z5, R.t5, R.g5, R.norm_mixing, to_d5)
+    mid_back_apply(R.dh, R.z5, R.t5, R.g5, norm_mixing, to_d5)
     pair = edge_exchange(R.d5, 1)
     rs_step(WIDEN)
     unit_windows(R.d5, R.win5, range(1, OD + 1), True)
@@ -939,8 +979,10 @@
         R.dh[:, aligned(j, MID // 2)] = acc
 
     loop(2, conv_back)
-    mid_back_sums(R.dh, R.z4, R.t4, R.norm_squeeze)
+    mid_back_sums(R.dh, R.z4, R.t4, norm_squeeze)
     mid_start(5)
+    for o in range(1, OD):
+        mixed_copy(1, o).start()
     rs_step(WIDEN)
     staged(MIXING, fill_conv(MIXING, R.win4, lambda: R.d5[1 : OD + 1].reshape(M, MID)))
     mid_finish(5, R.g4)
@@ -948,7 +990,7 @@
     def to_d4(o, cols, v):
         R.dz4[out_rows(o), cols] = v
 
-    mid_back_apply(R.dh, R.z4, R.t4, R.g4, R.norm_squeeze, to_d4)
+    mid_back_apply(R.dh, R.z4, R.t4, R.g4, norm_squeeze, to_d4)
 
     def squeeze_back(j):
         n = WIDE // 4
@@ -1004,8 +1046,8 @@
     def u1_apply(j):
         cols = aligned(j, LANES)
         tot, grads = wide_at(R.t3, j), wide_at(R.g3, j)
-        f3, a3, b3 = backward_terms(tot, grads, R.norm_expand, cols, OUT, 0, 0, 3)
-        fs, as_, bs = backward_terms(tot, grads, R.norm_shortcut, cols, OUT, 8, 8, 3)
+        f3, a3, b3 = backward_terms(tot, grads, norm_expand, cols, OUT, 0, 0, 3)
+        fs, as_, bs = backward_terms(tot, grads, norm_shortcut, cols, OUT, 8, 8, 3)
         for o in range(OD):
             rows = out_rows(o)
             d = R.du1[groups16(o), :, cols].reshape(S, LANES)
@@ -1015,7 +1057,7 @@
 
     loop(WIDE // LANES, u1_apply)
     reduce_back(R.dz6, R.f2, R.dh)
-    mid_back_sums(R.dh, R.z2, R.t2, R.norm_spatial)
+    mid_back_sums(R.dh, R.z2, R.t2, norm_spatial)
     mid_start(6)
     rs_step(SQUEEZE, MIXING, WIDEN)
     staged(EXPAND, fill_out(EXPAND, lambda: R.h2[...], R.dz6))
@@ -1029,7 +1071,7 @@
     def to_d2(o, cols, v):
         R.d2[o, :, cols] = v
 
-    mid_back_apply(R.dh, R.z2, R.t2, R.g2, R.norm_spatial, to_d2)
+    mid_back_apply(R.dh, R.z2, R.t2, R.g2, norm_spatial, to_d2)
     up = remote(R.d2.at[0], R.d2.at[OD], R.hs.at[1], R.hr.at[1], (b, jnp.maximum(r - 1, 0)))
 
     @pl.when(r > 0)
@@ -1089,7 +1131,7 @@
     def h1_back(j):
         cols = aligned(j, LANES)
         sums = mid_at(R.t1, j)
-        sc, sh = forward_terms(sums, R.norm_reduce, cols, IN)
+        sc, sh = forward_terms(sums, norm_reduce, cols, IN)
         xa, xs = xhat_terms(sums, IN)
         ch = keep(j, 1.0)
         g0 = jnp.zeros((S, LANES), F32)
@@ -1111,6 +1153,21 @@
     mid_start(7)
     rs_step(SPATIAL, SQUEEZE, MIXING, EXPAND, SHORTCUT)
 
+    def norm_grads(i, src, gains, biases):
+        at, width = cfg.norm_columns[i]
+        parts, _, n = src.shape
+        for h in range(parts):
+            cols = slice(at + h * n, at + (h + 1) * n)
+            for g in range(3):
+                R.gn_values[g, 0:1, cols] = src[h, gains + g : gains + g + 1, :]
+                R.gn_values[g, 1:2, cols] = src[h, biases + g : biases + g + 1, :]
+
+    def gn_copy(first):
+        at = MID if first else 0
+        n = R.gn.shape[2] - MID if first else MID
+        cols = pl.ds(at, n)
+        return pltpu.make_async_copy(R.gn_values.at[:, :, cols], R.gn.at[:, :, cols], R.ld.at[3 + first])
+
     def short_back(j):
         acc = None
         for i in range(4):
@@ -1119,11 +1176,15 @@
         R.z6[:, aligned(j, CIN // 4)] = acc
 
     loop(4, short_back)
+    for i, (src, gains) in enumerate(((R.g2, 0), (R.g4, 0), (R.g5, 0), (R.g3, 0), (R.g3, 8), (R.g6, 0))):
+        norm_grads(i + 1, src, gains, 3)
+    gn_copies = [gn_copy(1)]
+    gn_copies[0].start()
     mid_finish(7, R.g1)
 
     def h1_apply(j):
         cols = aligned(j, LANES)
-        f, a, bz = backward_terms(mid_at(R.t1, j), mid_at(R.g1, j), R.norm_reduce, cols, IN)
+        f, a, bz = backward_terms(mid_at(R.t1, j), mid_at(R.g1, j), norm_reduce, cols, IN)
         for k in range(RD):
             for p in range(2):
                 rows = out_rows(p)
@@ -1147,9 +1208,8 @@
 
         loop(4, body)
 
-    rs_step(SPATIAL, SQUEEZE, MIXING, EXPAND, SHORTCUT)
     staged(REDUCE, fill_reduce)
-    rs_step(SPATIAL, SQUEEZE, MIXING, EXPAND, SHORTCUT)
+    rs_round()
 
     def input_grad(j):
         cols = aligned(j, CIN // 4)
@@ -1172,10 +1232,15 @@
                 woven = R.weave[base : base + 2 * S, :]
                 (R.du2, R.du1)[k // 2][:, :, at] = woven.reshape(M // 16, 16, LANES)
 
-    loop(4, input_grad)
+    for j in range(4):
+        input_grad(j)
+        if j < 3:
+            rs_round()
     gin_copies = [
         pltpu.make_async_copy(
-            (R.du2, R.du1)[k // 2].at[pl.ds(0, images), :, pl.ds(k % 2 * CIN, CIN)], R.gin.at[:, k], R.gn.at[k]
+            (R.du2, R.du1)[k // 2].at[pl.ds(0, images), :, pl.ds(k % 2 * CIN, CIN)],
+            R.gin.at[:, k],
+            R.gi.at[k],
         )
         for k in range(RD)
     ]
@@ -1183,21 +1248,16 @@
         c.start()
     rs_end()
 
-    for out, src in ((R.gn1, R.g1), (R.gn2, R.g2), (R.gn4, R.g4), (R.gn5, R.g5)):
-        for h in range(2):
-            for i in range(2):
-                out[i, :, h * (MID // 2) : (h + 1) * (MID // 2)] = src[h, 3 * i : 3 * i + 3, :]
-    for out, src, rows in ((R.gn3, R.g3, (0, 3)), (R.gns, R.g3, (8, 3)), (R.gn6, R.g6, (0, 3))):
-        for h in range(4):
-            for i in range(2):
-                out[i, :, h * (WIDE // 4) : (h + 1) * (WIDE // 4)] = src[h, rows[i] : rows[i] + 3, :]
+    norm_grads(0, R.g1, 0, 3)
+    gn_copies.append(gn_copy(0))
+    gn_copies[1].start()
 
     for o in range(OD):
         mixed_copy(0, o).wait()
         mixed_copy(1, o).wait_send()
         mixed_copy(2, o).wait()
         mixed_copy(3, o).wait()
-    for c in gin_copies:
+    for c in gin_copies + gn_copies:
         c.wait()
 
 
@@ -1219,14 +1279,20 @@
         WIDEN: mid * wide // 512,
     }
     pieces = {SPATIAL: 3, MIXING: 3, SHORTCUT: 2}
+    widths = (mid,) * 4 + (wide,) * 3
+    cfg.norm_columns = [(sum(widths[:i]), n) for i, n in enumerate(widths)]
     cfg.units = []
     for name, n in flat.items():
         k = pieces.get(name, 1)
-        cfg.units += [(name, i * n // 4 // k, n // 4 // k) for i in range(k)]
+        for i in range(k):
+            mode = 1 + len(cfg.units) % 2 if name else 0
+            cfg.units.append((name, i * n // 4 // k, n // 4 // k, mode))
+    cfg.lags = (0, 2, 4, 6)
+    cfg.pumps = (3, 2, 2, 3, 2, 1, 20)
     cfg.flat = flat
     cfg.rows = {name: n // 32 for name, n in flat.items()}
     cfg.reduce = batch == 8
-    orders = ((DX, DY, DN, DF), (DY, DX, DN, DF), (DN, DF, DX, DY))
+    orders = ((DX, DY, DN, DF), (DY, DN, DX, DF), (DN, DX, DY, DF))
     thirds = {WIDEN: 1, SQUEEZE: 0, EXPAND: 2}
     cfg.parts = {}
     for name, n in cfg.rows.items():
@@ -1250,24 +1316,17 @@
     return cfg
 
 
-def run_blocks(cfg, smem_args, vmem_args, hbm_args):
+def run_blocks(cfg, smem_args, hbm_args):
     S, RD, OD, NB = cfg.slots, cfg.in_rows, cfg.out_rows, cfg.batch
     MID, WIDE, CIN = cfg.mid, cfg.wide, cfg.cin
     M = OD * S
     U = len(cfg.units)
-    vmem = pl.BlockSpec(memory_space=pltpu.VMEM)
     hbm = pl.BlockSpec(memory_space=pl.ANY)
     sds = jax.ShapeDtypeStruct
     outs = dict(
         mixed=(sds((cfg.images, 4 * OD, 8, WIDE), BF), hbm),
         gin=(sds((cfg.images, RD, 16, CIN), F32), hbm),
-        gn1=(sds((2, 3, MID), F32), vmem),
-        gn2=(sds((2, 3, MID), F32), vmem),
-        gn3=(sds((2, 3, WIDE), F32), vmem),
-        gns=(sds((2, 3, WIDE), F32), vmem),
-        gn4=(sds((2, 3, MID), F32), vmem),
-        gn5=(sds((2, 3, MID), F32), vmem),
-        gn6=(sds((2, 3, WIDE), F32), vmem),
+        gn=(sds((3, 2, 4 * MID + 3 * WIDE), F32), hbm),
     )
     final = {}
     if cfg.reduce:
@@ -1327,8 +1386,8 @@
         rq=V((2, 2 * NB, 8, MID // 2), F32),
         rw=V((2, 4, 16, WIDE // 4), F32),
         wb=V((2, NB, 16, WIDE // 4), F32),
-        wsend=pltpu.SemaphoreType.DMA((U, 5)),
-        wrecv=pltpu.SemaphoreType.DMA((U, 5)),
+        wsend=pltpu.SemaphoreType.DMA((U, 7)),
+        wrecv=pltpu.SemaphoreType.DMA((U, 7)),
         wloc=pltpu.SemaphoreType.DMA((7, 4)),
         ms=pltpu.SemaphoreType.DMA((3,)),
         mr=pltpu.SemaphoreType.DMA((3, 2)),
@@ -1342,7 +1401,7 @@
         xr=pltpu.SemaphoreType.DMA((3, OD)),
         xl=pltpu.SemaphoreType.DMA((OD,)),
         gs=pltpu.SemaphoreType.DMA((2,)),
-        gn=pltpu.SemaphoreType.DMA((RD,)),
+        gi=pltpu.SemaphoreType.DMA((RD,)),
         rs=pltpu.SemaphoreType.DMA((7, 3, 5)),
         rr=pltpu.SemaphoreType.DMA((7, 3, 5)),
         fs=pltpu.SemaphoreType.DMA((7, 3)),
@@ -1355,23 +1414,25 @@
         active_slot=V((S, LANES), F32),
         pix_in=V((RD, 2 * S, LANES), F32),
         pix_out=V((M, LANES), F32),
-        ld=pltpu.SemaphoreType.DMA((2,)),
+        ld=pltpu.SemaphoreType.DMA((5,)),
+        norm_values=V((3, 2, 4 * MID + 3 * WIDE), F32),
+        gn_values=V((3, 2, 4 * MID + 3 * WIDE), F32),
     )
     scratch.update({"f" + str(name): V((n, 512), BF) for name, n in cfg.flat.items()})
     scratch.update({"l" + str(name): V((cfg.flat[name], 512), BF) for name in cfg.own_landing if cfg.reduce})
     scratch.update({"e" + str(w): V(shape, BF) for w, shape in final.items()})
-    names = list(smem_args) + list(vmem_args) + list(hbm_args) + list(outs) + list(scratch)
+    names = list(smem_args) + list(hbm_args) + list(outs) + list(scratch)
     smem = pl.BlockSpec(memory_space=pltpu.SMEM)
     res = pl.pallas_call(
         functools.partial(block_kernel, names, cfg),
         out_shape=[o[0] for o in outs.values()],
-        in_specs=[smem] * len(smem_args) + [vmem] * len(vmem_args) + [hbm] * len(hbm_args),
+        in_specs=[smem] * len(smem_args) + [hbm] * len(hbm_args),
         out_specs=[o[1] for o in outs.values()],
         scratch_shapes=list(scratch.values()),
         compiler_params=pltpu.CompilerParams(
             collective_id=0, has_side_effects=True, vmem_limit_bytes=63 * 2**20
         ),
-    )(*smem_args.values(), *vmem_args.values(), *hbm_args.values())
+    )(*smem_args.values(), *hbm_args.values())
     return SimpleNamespace(**dict(zip(outs, res)))
 
 
@@ -1397,20 +1458,19 @@
     x = jnp.pad(x, ((0, 0), (0, 0), (0, S - images * 8), (0, 0))).reshape(rd, 2 * S, cin)
     out_cols = cotangent.shape[2]
     ct = slot_layout(jnp.pad(cotangent, ((0, 0), (0, 0), (0, 8 - out_cols), (0, 0))), S)
+    norms = jnp.concatenate(
+        [
+            jnp.transpose(n, (1, 0, 2))
+            for n in (norm_reduce, norm_spatial, norm_squeeze, norm_mixing, norm_expand, norm_shortcut, norm_widen)
+        ],
+        axis=2,
+    )
     res = run_blocks(
         cfg,
         dict(resolution=resolution, active=active),
         dict(
-            norm_reduce=norm_reduce,
-            norm_spatial=norm_spatial,
-            norm_expand=norm_expand,
-            norm_shortcut=norm_shortcut,
-            norm_squeeze=norm_squeeze,
-            norm_mixing=norm_mixing,
-            norm_widen=norm_widen,
-        ),
-        dict(
             features=x,
+            norms=norms,
             cotangent=ct.reshape(od * S, wide),
             w0=w_reduce,
             w1=w_spatial.reshape(-1, mid),
@@ -1422,7 +1482,6 @@
         ),
     )
     mixed = res.mixed[:, :, :out_cols]
-    gin = res.gin[:, :, :cols_in]
 
     def unpack(g, name):
         b8, _, n, _ = g.shape
@@ -1446,7 +1505,8 @@
         part = lax.psum_scatter(part, "batch", scatter_dimension=dim, tiled=True)
         totals.append(lax.psum(part, "rows").astype(F32))
 
-    return (mixed, gin, *totals, res.gn1, res.gn2, res.gn3, res.gns, res.gn4, res.gn5, res.gn6)
+    gn = [jnp.transpose(res.gn[:, :, at : at + n], (1, 0, 2)) for at, n in cfg.norm_columns]
+    return (mixed, res.gin[:, :, :cols_in], *totals, gn[0], gn[1], gn[4], gn[5], gn[2], gn[3], gn[6])
 
 
 def solution(mesh):

time: 317 us -> 280 us (0.88)
  Pallas kernels: 288 us -> 256 us
  local copies, waits for them, and re-layouts: 21.3 us -> 16.1 us
    pallas_call x1, Pallas kernels: 288 us -> 256 us  [run_blocks(): pl.pallas_call(functools.partial(block_kernel, names, cfg), out_shape=[o[...]
    unnamed x62 -> x42, local copies, waits for them, and re-layouts: 16.2 us -> 8.05 us
where the time goes in v3:
time: 280 us
  Pallas kernels  256 us (91%)
  local copies, waits for them, and re-layouts  16.1 us (6%)
  other arithmetic  6.64 us (2%)
    pallas_call x1, Pallas kernels, run_blocks(): pl.pallas_call(functools.partial(block_kernel, names, cfg), out_shape=[o[...  256 us
    unnamed x42, local copies, waits for them, and re-layouts  8.05 us

profile of v3, /device:TPU:0, one launch (start us, length us, event | category | flops | bytes accessed | tf_op | source)
XLA Modules:
  0.0 279.5 jit_solution(13170216495174905199)
XLA Ops:
  0.6 1.7 pad.16
  2.4 0.7 copy.39
  3.0 0.0 copy-start.4
  3.0 1.2 pad.17
  4.2 0.5 pad.18
  4.7 0.0 copy-start.13
  4.7 0.0 copy-start.14
  4.8 0.0 copy-start.16
  4.8 0.0 copy-start.10
  4.8 0.2 copy.35
  5.0 0.9 pad.19
  6.1 0.7 copy-done.8
  6.7 256.0 %shard_map.297 = (bf16[9,8,8,2048]{3,2,1,0:T(8,128)(2,1)}, f32[9,4,16,1024]{3,2,1,0:T(8,128)}, f32[3,2,8192]{2,1,0:T(2,128)}, bf16[128,512]{1,0:T(8,128)(2,1)}, ...) custom-call(s32[72]{0:T(128)} %refs_0_.1, ...), custom_call_target="tpu_custom_call" | custom-call | tf_op jit(solution)/shard_map/pallas_call | solution.py:1426
  262.7 1.4 slice_bitcast_fusion.3
  264.1 1.5 slice_bitcast_fusion
  265.6 4.6 %copy.36 = bf16[9,8,7,2048]{3,1,2,0:T(8,128)(2,1)} copy(bf16[9,8,7,2048]{3,2,1,0:T(8,128)(2,1)} %bitcast.52) | data formatting | bytes 4128768
  270.2 2.7 copy.37
  272.9 1.2 convert.2
  274.0 1.2 convert.3
  275.2 1.1 convert_element_type.27
  276.3 0.8 convert_element_type.26
  277.1 0.9 convert_element_type.28
  278.0 0.8 convert_element_type.29
  278.8 0.7 convert_element_type.25
  (35 shorter events, 0.1 us)
Async XLA Ops:
  3.0 1.2 copy-start.4
  4.7 1.2 copy-start.13
  4.7 1.2 copy-start.14
  4.7 1.2 copy-start.15
  4.8 1.2 copy-start.16
  4.8 1.2 copy-start.10
  4.8 1.2 copy-start.11
  4.8 1.2 copy-start.12
  6.0 0.7 copy-start.8
  265.6 4.6 %copy-start = (f32[9,4,16,1024]{3,2,1,0:T(8,128)S(1)}, f32[9,4,16,1024]{3,2,1,0:T(8,128)}, u32[]{:S(2)}) copy-start(f32[9,4,16,1024]{3,2,1,0:T(8,128)} %get-tuple-element.27) | copy-start | bytes 7077892
  270.2 2.7 copy-start.2
  272.9 1.2 copy-start.1
  274.0 1.2 copy-start.3
  275.2 1.1 copy-start.7
  275.2 1.9 copy-start.6
  276.3 1.7 copy-start.5
  276.3 2.5 copy-start.9

commit v4 on v3

--- a/solution.py
+++ b/solution.py
@@ -555,8 +555,25 @@
 
     conv(R.win1, R.f1, R.z2)
     forward_stats(R.z2, lambda j: mid_at(R.loc, j))
+    def piece(weight, shard, j):
+        n = weight.shape[0] // 16
+        return weight[pl.ds(pl.multiple_of((shard * 4 + j) * n, n), n), :]
+
+    def block(weight, j):
+        return jnp.concatenate([piece(weight, q, j) for q in range(4)], axis=0)
+
     mid_start(1)
     pump(cfg.pumps[2])
+    need(SHORTCUT)
+
+    def zs_body(j):
+        cols = aligned(j, 512)
+        w = block(R.f3, j)
+        for o in range(OD):
+            R.zs[out_rows(o), cols] = dot(R.x0[2 * o, 0:S, :], w)
+
+    loop(WIDE // 512, zs_body)
+    forward_stats(R.zs, lambda j: wide_at(R.locw2, j), 8)
     mid_finish(1, R.t2)
 
     def activate(z, tot, params, dest):
@@ -576,13 +593,6 @@
     activate(R.z2, R.t2, norm_spatial, to_h2)
     need(EXPAND)
 
-    def piece(weight, shard, j):
-        n = weight.shape[0] // 16
-        return weight[pl.ds(pl.multiple_of((shard * 4 + j) * n, n), n), :]
-
-    def block(weight, j):
-        return jnp.concatenate([piece(weight, q, j) for q in range(4)], axis=0)
-
     def expand_to(h, weight, z):
         def body(j):
             z[:, aligned(j, 512)] = dot(h[...], block(weight, j))
@@ -590,17 +600,7 @@
         loop(WIDE // 512, body)
 
     expand_to(R.h2, R.f2, R.z3)
-    need(SHORTCUT)
-
-    def zs_body(j):
-        cols = aligned(j, 512)
-        w = block(R.f3, j)
-        for o in range(OD):
-            R.zs[out_rows(o), cols] = dot(R.x0[2 * o, 0:S, :], w)
-
-    loop(WIDE // 512, zs_body)
     forward_stats(R.z3, lambda j: wide_at(R.locw2, j), 0)
-    forward_stats(R.zs, lambda j: wide_at(R.locw2, j), 8)
     wide_start(0, R.locw2)
     pump(cfg.pumps[3])
     wide_finish(0, R.t3)
@@ -749,7 +749,7 @@
         assert 32 * n <= stage.shape[0], w
         if cfg.reduce:
             fill(stage)
-            begun[w] = (stage, 0)
+            begun[w] = (stage, [0] * len(cfg.parts[w]), [0])
             for p in range(len(cfg.parts[w])):
                 rs_core(w, p).start()
             return
@@ -834,39 +834,41 @@
             return pltpu.make_async_copy(src, dst, R.fl.at[w])
         return remote(src, dst, R.fs.at[w, i], R.fr.at[w, i], (b, x_row if i == 1 else core_peer))
 
-    def rs_step(*kernels):
+    def rs_step(*kernels, parts=(0, 1, 2)):
         if not cfg.reduce:
             return
         for w in kernels:
-            stage, step = begun[w]
-            if step > 5:
-                continue
-            if step == 5:
+            stage, steps, ends = begun[w]
+            if ends[0] == 1:
                 fin_copy(w, 1).wait_recv()
                 fin_copy(w, 2).start()
-            else:
-                for p in range(len(cfg.parts[w])):
-                    c = rs_core(w, p) if step == 0 else rs_link(w, p, step)
-                    c.wait_recv()
-                    rs_add(w, p, step)
-                    if step < 4:
-                        rs_link(w, p, step + 1).start()
-                    c.wait_send()
-                if step == 4:
-                    for i in (1, 0, 3):
-                        fin_copy(w, i).start()
-            begun[w] = (stage, step + 1)
+                ends[0] = 2
+            for p in parts:
+                if p >= len(steps) or steps[p] > 4:
+                    continue
+                step = steps[p]
+                c = rs_core(w, p) if step == 0 else rs_link(w, p, step)
+                c.wait_recv()
+                rs_add(w, p, step)
+                if step < 4:
+                    rs_link(w, p, step + 1).start()
+                c.wait_send()
+                steps[p] = step + 1
+            if ends[0] == 0 and min(steps) == 5:
+                for i in (1, 0, 3):
+                    fin_copy(w, i).start()
+                ends[0] = 1
 
     def rs_round():
         if cfg.reduce:
-            rs_step(*[w for w in reversed(list(begun)) if begun[w][1] < 6])
+            rs_step(*[w for w in reversed(list(begun)) if begun[w][2][0] < 2])
 
     def rs_end():
         if not cfg.reduce:
             for copy in begun.values():
                 copy.wait()
             return
-        while any(begun[w][1] < 6 for w in begun):
+        while any(begun[w][2][0] < 2 for w in begun):
             rs_round()
         for w in cfg.rows:
             fin_copy(w, 0).wait()
@@ -1082,7 +1084,7 @@
     def _():
         R.d2[OD] = jnp.zeros(R.d2.shape[1:], BF)
 
-    rs_step(EXPAND, SHORTCUT, WIDEN)
+    rs_step(EXPAND, SHORTCUT, MIXING, SQUEEZE, WIDEN)
     staged(SPATIAL, fill_conv(SPATIAL, R.win1, lambda: R.d2[0:OD].reshape(M, MID)))
 
     @pl.when(r < 3)
@@ -1282,13 +1284,13 @@
     widths = (mid,) * 4 + (wide,) * 3
     cfg.norm_columns = [(sum(widths[:i]), n) for i, n in enumerate(widths)]
     cfg.units = []
-    for name, n in flat.items():
-        k = pieces.get(name, 1)
+    for name in (REDUCE, SPATIAL, SHORTCUT, EXPAND, SQUEEZE, MIXING, WIDEN):
+        n, k = flat[name], pieces.get(name, 1)
         for i in range(k):
             mode = 1 + len(cfg.units) % 2 if name else 0
             cfg.units.append((name, i * n // 4 // k, n // 4 // k, mode))
     cfg.lags = (0, 2, 4, 6)
-    cfg.pumps = (3, 2, 2, 3, 2, 1, 20)
+    cfg.pumps = (3, 1, 2, 2, 2, 2, 3)
     cfg.flat = flat
     cfg.rows = {name: n // 32 for name, n in flat.items()}
     cfg.reduce = batch == 8

time: 280 us -> 274 us (0.979)
  Pallas kernels: 256 us -> 250 us
    pallas_call x1, Pallas kernels: 256 us -> 250 us  [run_blocks(): pl.pallas_call(functools.partial(block_kernel, names, cfg), out_shape=[o[...]
where the time goes in v4:
time: 274 us
  Pallas kernels  250 us (91%)
  local copies, waits for them, and re-layouts  16.1 us (6%)
  other arithmetic  6.64 us (2%)
    pallas_call x1, Pallas kernels, run_blocks(): pl.pallas_call(functools.partial(block_kernel, names, cfg), out_shape=[o[...  250 us
    unnamed x42, local copies, waits for them, and re-layouts  8.05 us

profile of v4, /device:TPU:0, one launch (start us, length us, event | category | flops | bytes accessed | tf_op | source)
XLA Modules:
  0.0 274.0 jit_solution(6231232310792566592)
XLA Ops:
  0.6 1.7 pad.16
  2.4 0.7 copy.39
  3.0 0.0 copy-start.4
  3.0 1.2 pad.17
  4.2 0.5 pad.18
  4.7 0.0 copy-start.13
  4.7 0.0 copy-start.14
  4.8 0.0 copy-start.10
  4.8 0.0 copy-start.11
  4.8 0.2 copy.35
  5.0 0.9 pad.19
  6.1 0.7 copy-done.8
  6.7 250.4 %shard_map.297 = (bf16[9,8,8,2048]{3,2,1,0:T(8,128)(2,1)}, f32[9,4,16,1024]{3,2,1,0:T(8,128)}, f32[3,2,8192]{2,1,0:T(2,128)}, bf16[128,512]{1,0:T(8,128)(2,1)}, ...) custom-call(s32[72]{0:T(128)} %refs_0_.1, ...), custom_call_target="tpu_custom_call" | custom-call | tf_op jit(solution)/shard_map/pallas_call | solution.py:1428
  257.2 1.4 slice_bitcast_fusion.3
  258.5 1.5 slice_bitcast_fusion
  260.0 4.6 %copy.36 = bf16[9,8,7,2048]{3,1,2,0:T(8,128)(2,1)} copy(bf16[9,8,7,2048]{3,2,1,0:T(8,128)(2,1)} %bitcast.52) | data formatting | bytes 4128768
  264.6 2.7 copy.37
  267.3 1.2 convert.2
  268.5 1.2 convert.3
  269.6 1.1 convert_element_type.27
  270.7 0.8 convert_element_type.26
  271.6 0.9 convert_element_type.28
  272.4 0.8 convert_element_type.29
  273.2 0.7 convert_element_type.25
  (35 shorter events, 0.1 us)
Async XLA Ops:
  3.0 1.2 copy-start.4
  4.7 1.2 copy-start.13
  4.7 1.2 copy-start.14
  4.7 1.2 copy-start.15
  4.8 1.2 copy-start.16
  4.8 1.2 copy-start.10
  4.8 1.2 copy-start.11
  4.8 1.2 copy-start.12
  6.0 0.7 copy-start.8
  260.0 4.6 %copy-start = (f32[9,4,16,1024]{3,2,1,0:T(8,128)S(1)}, f32[9,4,16,1024]{3,2,1,0:T(8,128)}, u32[]{:S(2)}) copy-start(f32[9,4,16,1024]{3,2,1,0:T(8,128)} %get-tuple-element.27) | copy-start | bytes 7077892
  264.6 2.7 copy-start.2
  267.3 1.2 copy-start.1
  268.5 1.2 copy-start.3
  269.6 1.1 copy-start.7
  269.6 1.9 copy-start.6
  270.7 1.7 copy-start.5
  270.7 2.5 copy-start.9

commit v5 on v4

--- a/solution.py
+++ b/solution.py
@@ -281,19 +281,24 @@
         every.wait_send()
         back.wait()
 
+    six = pl.ds(0, 6)
+
     def wide_start(k, loc):
         n = loc.shape[1]
-        rw, wb = R.rw.at[k % 2, :, pl.ds(0, n)], R.wb.at[k % 2, :, pl.ds(0, n)]
+        norms = pl.ds(0, n)
+        rw, wb = R.rw.at[k % 2, :, norms], R.wb.at[k % 2, :, norms]
         rw[r] = loc[r]
         for to in (core_peer, x_row, diag):
-            remote(loc.at[to], rw.at[r], R.ws.at[k, 0], R.wr.at[k, 0], (b, to)).start()
-        three = remote(loc.at[pl.ds(0, 3)], rw.at[pl.ds(0, 3)], R.ws.at[k, 0], R.wr.at[k, 0], (b, core_peer))
+            remote(loc.at[to, :, six], rw.at[r, :, six], R.ws.at[k, 0], R.wr.at[k, 0], (b, to)).start()
+        three = remote(
+            loc.at[pl.ds(0, 3), :, six], rw.at[pl.ds(0, 3), :, six], R.ws.at[k, 0], R.wr.at[k, 0], (b, core_peer)
+        )
         three.wait_recv()
         wb[b] = rw[0] + rw[1] + (rw[2] + rw[3])
 
         def send(j):
             to = lax.rem(b + j + 1, NB)
-            remote(wb.at[b], wb.at[b], R.ws.at[k, 1], R.wr.at[k, 1], (to, r)).start()
+            remote(wb.at[b, :, six], wb.at[b, :, six], R.ws.at[k, 1], R.wr.at[k, 1], (to, r)).start()
 
         each(NB - 1, send)
         three.wait_send()
@@ -301,7 +306,7 @@
     def wide_finish(k, tot):
         n = tot.shape[1]
         wb = R.wb.at[k % 2, :, pl.ds(0, n)]
-        rest = wb.at[pl.ds(0, NB - 1)]
+        rest = wb.at[pl.ds(0, NB - 1), :, six]
         every = remote(rest, rest, R.ws.at[k, 1], R.wr.at[k, 1], (b, x_row))
         every.wait_recv()
         total = wb[0]
@@ -309,16 +314,17 @@
             total = total + wb[j]
         tot[r] = total
         for to in (core_peer, x_row, diag):
-            remote(tot.at[r], tot.at[r], R.ws.at[k, 2], R.wr.at[k, 2], (b, to)).start()
-        three = remote(tot.at[pl.ds(0, 3)], tot.at[pl.ds(0, 3)], R.ws.at[k, 2], R.wr.at[k, 2], (b, core_peer))
+            remote(tot.at[r, :, six], tot.at[r, :, six], R.ws.at[k, 2], R.wr.at[k, 2], (b, to)).start()
+        rest = tot.at[pl.ds(0, 3), :, six]
+        three = remote(rest, rest, R.ws.at[k, 2], R.wr.at[k, 2], (b, core_peer))
         every.wait_send()
         three.wait()
 
     def mid_at(ref, j):
         return ref.at[lax.div(j, 2), :, aligned(lax.rem(j, 2), LANES)]
 
-    def wide_at(ref, j):
-        return ref.at[lax.div(j, 4), :, aligned(lax.rem(j, 4), LANES)]
+    def wide_at(ref, j, norm=0):
+        return ref.at[lax.div(j, 4), norm, :, aligned(lax.rem(j, 4), LANES)]
 
     def group_rows(ref, row, values):
         for g in range(3):
@@ -573,7 +579,7 @@
             R.zs[out_rows(o), cols] = dot(R.x0[2 * o, 0:S, :], w)
 
     loop(WIDE // 512, zs_body)
-    forward_stats(R.zs, lambda j: wide_at(R.locw2, j), 8)
+    forward_stats(R.zs, lambda j: wide_at(R.locw2, j, 1), 0)
     mid_finish(1, R.t2)
 
     def activate(z, tot, params, dest):
@@ -609,7 +615,7 @@
         cols = aligned(j, LANES)
         tot = wide_at(R.t3, j)
         sc3, sh3 = forward_terms(tot, norm_expand, cols, OUT, 0)
-        scs, shs = forward_terms(tot, norm_shortcut, cols, OUT, 8)
+        scs, shs = forward_terms(wide_at(R.t3, j, 1), norm_shortcut, cols, OUT, 0)
         shift = sh3 + shs
 
         def u1(o):
@@ -1005,7 +1011,7 @@
         u1 = u1_terms(j)
         tot = wide_at(R.t3, j)
         xa3, xs3 = xhat_terms(tot, OUT, 0)
-        xas, xss = xhat_terms(tot, OUT, 8)
+        xas, xss = xhat_terms(wide_at(R.t3, j, 1), OUT, 0)
         ch = keep(j, float(WIDE // MID))
         g0 = jnp.zeros((S, LANES), F32)
         g1 = jnp.zeros((S, LANES), F32)
@@ -1021,8 +1027,10 @@
         group_rows(st, 0, g0)
         group_rows(st, 3, g1)
         blank(st, 6, 2)
-        group_rows(st, 8, g2)
-        blank(st, 11, 5)
+        st = wide_at(R.locw2, j, 1)
+        group_rows(st, 0, g2)
+        group_rows(st, 3, g1)
+        blank(st, 6, 2)
 
     loop(WIDE // LANES, u1_back)
     wide_start(3, R.locw2)
@@ -1049,7 +1057,7 @@
         cols = aligned(j, LANES)
         tot, grads = wide_at(R.t3, j), wide_at(R.g3, j)
         f3, a3, b3 = backward_terms(tot, grads, norm_expand, cols, OUT, 0, 0, 3)
-        fs, as_, bs = backward_terms(tot, grads, norm_shortcut, cols, OUT, 8, 8, 3)
+        fs, as_, bs = backward_terms(wide_at(R.t3, j, 1), wide_at(R.g3, j, 1), norm_shortcut, cols, OUT)
         for o in range(OD):
             rows = out_rows(o)
             d = R.du1[groups16(o), :, cols].reshape(S, LANES)
@@ -1178,7 +1186,7 @@
         R.z6[:, aligned(j, CIN // 4)] = acc
 
     loop(4, short_back)
-    for i, (src, gains) in enumerate(((R.g2, 0), (R.g4, 0), (R.g5, 0), (R.g3, 0), (R.g3, 8), (R.g6, 0))):
+    for i, (src, gains) in enumerate(((R.g2, 0), (R.g4, 0), (R.g5, 0), (R.g3.at[:, 0], 0), (R.g3.at[:, 1], 0), (R.g6.at[:, 0], 0))):
         norm_grads(i + 1, src, gains, 3)
     gn_copies = [gn_copy(1)]
     gn_copies[0].start()
@@ -1370,24 +1378,24 @@
         stage0=V((32 * cfg.rows[MIXING], 512), BF),
         stage1=V((32 * cfg.rows[SHORTCUT], 512), BF),
         loc=mid_tot,
-        locw=V((4, 8, WIDE // 4), F32),
-        locw2=V((4, 16, WIDE // 4), F32),
+        locw=V((4, 1, 8, WIDE // 4), F32),
+        locw2=V((4, 2, 8, WIDE // 4), F32),
         t1=mid_tot,
         t2=mid_tot,
-        t3=V((4, 16, WIDE // 4), F32),
+        t3=V((4, 2, 8, WIDE // 4), F32),
         t4=mid_tot,
         t5=mid_tot,
-        t6=V((4, 8, WIDE // 4), F32),
+        t6=V((4, 1, 8, WIDE // 4), F32),
         g1=mid_tot,
         g2=mid_tot,
-        g3=V((4, 16, WIDE // 4), F32),
+        g3=V((4, 2, 8, WIDE // 4), F32),
         g4=mid_tot,
         g5=mid_tot,
-        g6=V((4, 8, WIDE // 4), F32),
+        g6=V((4, 1, 8, WIDE // 4), F32),
         rc=V((2, 8, MID // 2), F32),
         rq=V((2, 2 * NB, 8, MID // 2), F32),
-        rw=V((2, 4, 16, WIDE // 4), F32),
-        wb=V((2, NB, 16, WIDE // 4), F32),
+        rw=V((2, 4, 2, 8, WIDE // 4), F32),
+        wb=V((2, NB, 2, 8, WIDE // 4), F32),
         wsend=pltpu.SemaphoreType.DMA((U, 7)),
         wrecv=pltpu.SemaphoreType.DMA((U, 7)),
         wloc=pltpu.SemaphoreType.DMA((7, 4)),

time: 274 us -> 271 us (0.989)
  Pallas kernels: 250 us -> 247 us
    pallas_call x1, Pallas kernels: 250 us -> 247 us  [run_blocks(): pl.pallas_call(functools.partial(block_kernel, names, cfg), out_shape=[o[...]
where the time goes in v5:
time: 271 us
  Pallas kernels  247 us (91%)
  local copies, waits for them, and re-layouts  16.1 us (6%)
  other arithmetic  6.64 us (2%)
    pallas_call x1, Pallas kernels, run_blocks(): pl.pallas_call(functools.partial(block_kernel, names, cfg), out_shape=[o[...  247 us
    unnamed x42, local copies, waits for them, and re-layouts  8.05 us

profile of v5, /device:TPU:0, one launch (start us, length us, event | category | flops | bytes accessed | tf_op | source)
XLA Modules:
  0.0 270.9 jit_solution(41892280606185255)
XLA Ops:
  0.6 1.7 pad.16
  2.4 0.7 copy.39
  3.0 1.2 pad.17
  4.2 0.5 pad.18
  4.7 0.0 copy-start.15
  4.8 0.0 copy-start.16
  4.8 0.0 copy-start.11
  4.8 0.0 copy-start.12
  4.8 0.2 copy.35
  5.0 0.9 pad.19
  6.0 0.0 copy-start.8
  6.1 0.7 copy-done.8
  6.7 247.4 %shard_map.297 = (bf16[9,8,8,2048]{3,2,1,0:T(8,128)(2,1)}, f32[9,4,16,1024]{3,2,1,0:T(8,128)}, f32[3,2,8192]{2,1,0:T(2,128)}, bf16[128,512]{1,0:T(8,128)(2,1)}, ...) custom-call(s32[72]{0:T(128)} %refs_0_.1, ...), custom_call_target="tpu_custom_call" | custom-call | tf_op jit(solution)/shard_map/pallas_call | solution.py:1436
  254.1 1.4 slice_bitcast_fusion.3
  255.5 1.5 slice_bitcast_fusion
  257.0 4.6 %copy.36 = bf16[9,8,7,2048]{3,1,2,0:T(8,128)(2,1)} copy(bf16[9,8,7,2048]{3,2,1,0:T(8,128)(2,1)} %bitcast.52) | data formatting | bytes 4128768
  261.6 2.7 copy.37
  264.2 1.2 convert.2
  265.4 1.2 convert.3
  266.6 1.1 convert_element_type.27
  267.6 0.8 convert_element_type.26
  268.5 0.9 convert_element_type.28
  269.3 0.8 convert_element_type.29
  270.2 0.7 convert_element_type.25
  (35 shorter events, 0.1 us)
Async XLA Ops:
  3.0 1.2 copy-start.4
  4.7 1.2 copy-start.13
  4.7 1.2 copy-start.14
  4.7 1.2 copy-start.15
  4.8 1.2 copy-start.16
  4.8 1.2 copy-start.10
  4.8 1.2 copy-start.11
  4.8 1.2 copy-start.12
  6.0 0.7 copy-start.8
  257.0 4.6 %copy-start = (f32[9,4,16,1024]{3,2,1,0:T(8,128)S(1)}, f32[9,4,16,1024]{3,2,1,0:T(8,128)}, u32[]{:S(2)}) copy-start(f32[9,4,16,1024]{3,2,1,0:T(8,128)} %get-tuple-element.27) | copy-start | bytes 7077892
  261.6 2.7 copy-start.2
  264.2 1.2 copy-start.1
  265.4 1.2 copy-start.3
  266.5 1.1 copy-start.7
  266.6 1.9 copy-start.6
  267.6 1.7 copy-start.5
  267.6 2.5 copy-start.9

commit v6 on v5

--- a/solution.py
+++ b/solution.py
@@ -261,7 +261,7 @@
         R.rq[p, me] = R.loc[core] + R.rc[p]
 
         def send(j):
-            to = team(flip(me, j + 1))
+            to = team(flip(me, 2 * NB - 1 - j))
             remote(R.rq.at[p, me, pl.ds(0, 6)], R.rq.at[p, me, pl.ds(0, 6)], R.ms.at[1], R.mr.at[1, p], to).start()
 
         each(2 * NB - 1, send)
@@ -297,7 +297,7 @@
         wb[b] = rw[0] + rw[1] + (rw[2] + rw[3])
 
         def send(j):
-            to = lax.rem(b + j + 1, NB)
+            to = flip(b, NB - 1 - j)
             remote(wb.at[b, :, six], wb.at[b, :, six], R.ws.at[k, 1], R.wr.at[k, 1], (to, r)).start()
 
         each(NB - 1, send)

time: 271 us -> 270 us (level)
  no operation moved by 1% of the time
where the time goes in v6:
time: 270 us
  Pallas kernels  246 us (91%)
  local copies, waits for them, and re-layouts  16.1 us (6%)
  other arithmetic  6.64 us (2%)
    pallas_call x1, Pallas kernels, run_blocks(): pl.pallas_call(functools.partial(block_kernel, names, cfg), out_shape=[o[...  246 us
    unnamed x42, local copies, waits for them, and re-layouts  8.05 us

profile of v6, /device:TPU:0, one launch (start us, length us, event | category | flops | bytes accessed | tf_op | source)
XLA Modules:
  0.0 269.9 jit_solution(4406772573895456454)
XLA Ops:
  0.6 1.7 pad.16
  2.4 0.7 copy.39
  3.0 0.0 copy-start.4
  3.0 1.2 pad.17
  4.2 0.5 pad.18
  4.7 0.0 copy-start.13
  4.7 0.0 copy-start.14
  4.8 0.0 copy-start.16
  4.8 0.0 copy-start.10
  4.8 0.2 copy.35
  5.0 0.9 pad.19
  6.1 0.7 copy-done.8
  6.7 246.3 %shard_map.297 = (bf16[9,8,8,2048]{3,2,1,0:T(8,128)(2,1)}, f32[9,4,16,1024]{3,2,1,0:T(8,128)}, f32[3,2,8192]{2,1,0:T(2,128)}, bf16[128,512]{1,0:T(8,128)(2,1)}, ...) custom-call(s32[72]{0:T(128)} %refs_0_.1, ...), custom_call_target="tpu_custom_call" | custom-call | tf_op jit(solution)/shard_map/pallas_call | solution.py:1436
  253.1 1.4 slice_bitcast_fusion.3
  254.4 1.5 slice_bitcast_fusion
  256.0 4.6 %copy.36 = bf16[9,8,7,2048]{3,1,2,0:T(8,128)(2,1)} copy(bf16[9,8,7,2048]{3,2,1,0:T(8,128)(2,1)} %bitcast.52) | data formatting | bytes 4128768
  260.5 2.7 copy.37
  263.2 1.2 convert.2
  264.4 1.2 convert.3
  265.5 1.1 convert_element_type.27
  266.6 0.8 convert_element_type.26
  267.5 0.9 convert_element_type.28
  268.3 0.8 convert_element_type.29
  269.1 0.7 convert_element_type.25
  (35 shorter events, 0.1 us)
Async XLA Ops:
  3.0 1.2 copy-start.4
  4.7 1.2 copy-start.13
  4.7 1.2 copy-start.14
  4.7 1.2 copy-start.15
  4.8 1.2 copy-start.16
  4.8 1.2 copy-start.10
  4.8 1.2 copy-start.11
  4.8 1.2 copy-start.12
  6.0 0.7 copy-start.8
  256.0 4.6 %copy-start = (f32[9,4,16,1024]{3,2,1,0:T(8,128)S(1)}, f32[9,4,16,1024]{3,2,1,0:T(8,128)}, u32[]{:S(2)}) copy-start(f32[9,4,16,1024]{3,2,1,0:T(8,128)} %get-tuple-element.27) | copy-start | bytes 7077892
  260.5 2.7 copy-start.2
  263.2 1.2 copy-start.1
  264.4 1.2 copy-start.3
  265.5 1.1 copy-start.7
  265.5 1.9 copy-start.6
  266.6 1.7 copy-start.5
  266.6 2.5 copy-start.9
